TPU v7x, 256 devices: a whole 4x4x8 slice. The times are simulated.
256 devices in a mesh: lat: 16 (over y_lo, x, core), lon: 16 (over z, y_hi).
Axes of the slice: x: 4, y: 4 (y_hi: 2, y_lo: 2; y = y_hi * 2 + y_lo), z: 8, core: 2. Of those that a mesh axis runs over, the one named last changes fastest.
Arguments:
- field: bfloat16 [1, 64, 512, 2048], P(None, None, 'lat', 'lon'), may hold values from -6 to 6
- kernel: bfloat16 [3, 3, 64, 64], replicated, may hold values from -0.25 to 0.25
- cotangent: bfloat16 [1, 64, 512, 2048], P(None, None, 'lat', 'lon'), may hold values from -6 to 6
Outputs:
- output: bfloat16 [1, 64, 512, 2048], P(None, None, 'lat', 'lon')
- grad_input: bfloat16 [1, 64, 512, 2048], P(None, None, 'lat', 'lon')
- grad_kernel: float32 [3, 3, 64, 64], replicated
All inputs are finite; a program needn't handle non-finite values.
Results may differ from a plain program's by a relative error of at most 0.0039.
Values may be sent and summed in bfloat16 or wider, within the bound.
No kernel may reach another device: no remote copies, remote signals or barrier semaphores. Data moves between devices by JAX's collectives and lax.ppermute only.
A program may use at most 64 MiB of HBM per device.

v0:
```python
import math

import jax
import jax.numpy as jnp
from jax import lax
from jax.sharding import PartitionSpec as P

gelu_scale = math.sqrt(2.0 / math.pi)


def with_halo(cells, sides, width, closed):
    for axis, dim in sides:
        count = lax.axis_size(axis)
        ends = count if closed else count - 1
        head = lax.slice_in_dim(cells, 0, width, axis=dim)
        tail = lax.slice_in_dim(cells, cells.shape[dim] - width, cells.shape[dim], axis=dim)
        cells = jnp.concatenate(
            [
                lax.ppermute(tail, axis, [(i, (i + 1) % count) for i in range(ends)]),
                cells,
                lax.ppermute(head, axis, [((i + 1) % count, i) for i in range(ends)]),
            ],
            axis=dim,
        )
    return cells


def from_behind(value, axis, steps):
    count = lax.axis_size(axis)
    pairs = [(source, (source + steps) % count) for source in range(count)]
    return lax.ppermute(value, axis, pairs)


def gelu_parts(hidden):
    cubic = hidden * hidden * hidden
    tangent = jnp.tanh(gelu_scale * (hidden + 0.044715 * cubic))
    value = 0.5 * hidden * (1.0 + tangent)
    slope = 0.5 * (1.0 + tangent) + 0.5 * hidden * (1.0 - tangent * tangent) * gelu_scale * (
        1.0 + 3.0 * 0.044715 * hidden * hidden
    )
    return (value, slope)


def polar_gradient(kernel, upper_rows, lower_rows, width):
    upper_sum = None
    lower_sum = None
    for tap_col in range(3):
        start = 2 - tap_col
        upper_term = jnp.einsum(
            "oc,bow->bcw",
            kernel[0, tap_col],
            upper_rows[:, :, start : start + width],
            preferred_element_type=jnp.float32,
        )
        lower_term = jnp.einsum(
            "oc,bow->bcw",
            kernel[2, tap_col],
            lower_rows[:, :, start : start + width],
            preferred_element_type=jnp.float32,
        )
        upper_sum = upper_term if upper_sum is None else upper_sum + upper_term
        lower_sum = lower_term if lower_sum is None else lower_sum + lower_term
    return jnp.stack([upper_sum, lower_sum], 2)


def on_device(field, kernel, cotangent):
    lat_count = lax.axis_size("lat")
    lon_count = lax.axis_size("lon")
    row_index = lax.axis_index("lat")
    samples, channels, rows, cols = field.shape
    wide = with_halo(field, (("lon", 3),), 1, True)
    banded = with_halo(wide, (("lat", 2),), 1, False)
    edges = jnp.concatenate([wide[:, :, :1], wide[:, :, -1:]], 2)
    opposite = from_behind(edges, "lon", lon_count // 2)
    upper = jnp.where(row_index == 0, opposite[:, :, :1], banded[:, :, :1])
    lower = jnp.where(row_index == lat_count - 1, opposite[:, :, 1:], banded[:, :, -1:])
    padded = jnp.concatenate([upper, banded[:, :, 1:-1], lower], 2)
    hidden = jnp.zeros((samples, channels, rows, cols), jnp.float32)
    for tap_row in range(3):
        for tap_col in range(3):
            window = padded[:, :, tap_row : tap_row + rows, tap_col : tap_col + cols]
            hidden = hidden + jnp.einsum(
                "oc,bchw->bohw",
                kernel[tap_row, tap_col],
                window,
                preferred_element_type=jnp.float32,
            )
    value, slope = gelu_parts(hidden)
    output = (field.astype(jnp.float32) + value).astype(jnp.bfloat16)
    delta = (cotangent.astype(jnp.float32) * slope).astype(jnp.bfloat16)
    delta_wide = with_halo(delta, (("lon", 3),), 1, True)
    delta_pad = with_halo(delta_wide, (("lat", 2),), 1, False)
    back = jnp.zeros((samples, channels, rows, cols), jnp.float32)
    for tap_row in range(3):
        for tap_col in range(3):
            window = delta_pad[
                :, :, 2 - tap_row : 2 - tap_row + rows, 2 - tap_col : 2 - tap_col + cols
            ]
            back = back + jnp.einsum(
                "oc,bohw->bchw",
                kernel[tap_row, tap_col],
                window,
                preferred_element_type=jnp.float32,
            )
    local_terms = polar_gradient(kernel, delta_pad[:, :, 1], delta_pad[:, :, rows], cols)
    arrived_terms = from_behind(local_terms.astype(jnp.bfloat16), "lon", lon_count // 2).astype(
        local_terms.dtype
    )
    top_extra = jnp.where(row_index == 0, arrived_terms[:, :, :1], 0.0)
    bottom_extra = jnp.where(row_index == lat_count - 1, arrived_terms[:, :, 1:], 0.0)
    back = back.at[:, :, :1].add(top_extra)
    back = back.at[:, :, rows - 1 :].add(bottom_extra)
    grad_input = (cotangent.astype(jnp.float32) + back).astype(jnp.bfloat16)
    tap_terms = []
    for tap_row in range(3):
        row_terms = []
        for tap_col in range(3):
            window = padded[:, :, tap_row : tap_row + rows, tap_col : tap_col + cols]
            row_terms.append(
                jnp.einsum("bohw,bchw->oc", delta, window, preferred_element_type=jnp.float32)
            )
        tap_terms.append(jnp.stack(row_terms, 0))
    local_grad = jnp.stack(tap_terms, 0)
    summed = lax.psum(local_grad, ("lat", "lon"))
    scale = float(samples * rows * lat_count * cols * lon_count) ** (-0.5)
    return (output, grad_input, summed * scale)


def solution(mesh):
    return jax.shard_map(
        on_device,
        mesh=mesh,
        in_specs=(P(None, None, "lat", "lon"), P(), P(None, None, "lat", "lon")),
        out_specs=(P(None, None, "lat", "lon"), P(None, None, "lat", "lon"), P()),
        check_vma=False,
    )
```

profile of v0, /device:TPU:1, one launch (start us, length us, event | category | flops | bytes accessed | tf_op | source)
XLA Modules:
  0.0 325.6 jit_solution(2687897451942304069)
XLA Ops:
  7.2 1.2 copy.6
  8.5 0.2 fusion.110
  8.7 3.8 %collective-permute-start = (bf16[1,64,32,1]{3,1,2,0:T(8,128)(2,1)S(1)}, bf16[1,64,32,1]{3,1,2,0:T(8,128)(2,1)S(1)}, u32[]{:S(2)}, u32[]{:S(2)}) collective-permute-start(bf16[1,64,32,1]{3,1,2,0:T(8,128)(2,1)S(1)} %get-tuple-element.42), channel_id=1, source_target_pairs={{0,1},{1,2},{2,3},{3,4},{4,5},{5,6},{6,7},{7,8},{8,9},{9,10},{10,1... | collective-permute-start | bytes 12296 | tf_op jit(solution)/shard_map/ppermute | solution.py:19
  12.6 5.4 %collective-permute-start.1 = (bf16[1,64,32,1]{3,1,2,0:T(8,128)(2,1)S(1)}, bf16[1,64,32,1]{3,1,2,0:T(8,128)(2,1)S(1)}, u32[]{:S(2)}, u32[]{:S(2)}) collective-permute-start(bf16[1,64,32,1]{3,1,2,0:T(8,128)(2,1)S(1)} %get-tuple-element.43), channel_id=1, source_target_pairs={{1,0},{2,1},{3,2},{4,3},{5,4},{6,5},{7,6},{8,7},{9,8},{10,9},{11,1... | collective-permute-start | bytes 12296 | tf_op jit(solution)/shard_map/ppermute | solution.py:21
  17.9 16.4 %collective-permute-done = bf16[1,64,32,1]{3,1,2,0:T(8,128)(2,1)S(1)} collective-permute-done((bf16[1,64,32,1]{3,1,2,0:T(8,128)(2,1)S(1)}, bf16[1,64,32,1]{3,1,2,0:T(8,128)(2,1)S(1)}, u32[]{:S(2)}, u32[]{:S(2)}) %collective-permute-start) | collective-permute-done | bytes 4128 | tf_op jit(solution)/shard_map/ppermute | solution.py:19
  34.4 3.4 %collective-permute-done.1 = bf16[1,64,32,1]{3,1,2,0:T(8,128)(2,1)S(1)} collective-permute-done((bf16[1,64,32,1]{3,1,2,0:T(8,128)(2,1)S(1)}, bf16[1,64,32,1]{3,1,2,0:T(8,128)(2,1)S(1)}, u32[]{:S(2)}, u32[]{:S(2)}) %collective-permute-start.1) | collective-permute-done | bytes 4128 | tf_op jit(solution)/shard_map/ppermute | solution.py:21
  37.8 0.1 pad_maximum_fusion.11
  37.9 4.9 %collective-permute-start.3 = (bf16[1,64,1,130]{3,1,2,0:T(8,128)(2,1)S(1)}, bf16[1,64,1,130]{3,1,2,0:T(8,128)(2,1)S(1)}, u32[]{:S(2)}, u32[]{:S(2)}) collective-permute-start(bf16[1,64,1,130]{3,1,2,0:T(8,128)(2,1)S(1)} %get-tuple-element.36), channel_id=1, source_target_pairs={{0,16},{16,32},{32,48},{48,64},{64,80},{80,96},{96,112},{112,128},... | collective-permute-start | bytes 49928 | tf_op jit(solution)/shard_map/ppermute | solution.py:19
  42.8 1.9 collective-permute-start.4
  44.7 6.2 %collective-permute-start.2 = (bf16[1,64,2,130]{3,1,2,0:T(8,128)(2,1)S(1)}, bf16[1,64,2,130]{3,1,2,0:T(8,128)(2,1)S(1)}, u32[]{:S(2)}, u32[]{:S(2)}) collective-permute-start(bf16[1,64,2,130]{3,1,2,0:T(8,128)(2,1)S(1)} %pad_maximum_fusion.7), channel_id=1, source_target_pairs={{0,8},{1,9},{2,10},{3,11},{4,12},{5,13},{6,14},{7,15},{8,0},{9,1},... | collective-permute-start | bytes 99848 | tf_op jit(solution)/shard_map/ppermute | solution.py:31
  50.9 0.3 fusion.43
  51.2 1.3 collective-permute-done.2
  52.6 1.0 maximum_maximum_fusion
  53.6 0.3 fusion.40
  53.8 0.4 convolution_add_fusion.5
  54.2 0.4 convolution_add_fusion.4
  54.6 0.3 fusion.41
  54.9 0.4 fusion.2
  55.3 0.5 fusion.1
  55.9 0.4 convolution_add_fusion.1
  56.2 0.7 copy-done.2
  56.9 0.2 copy-done.5
  57.0 2.0 fusion.10
  59.0 0.4 convolution_bitcast_fusion.6
  59.4 0.4 convolution_bitcast_fusion.7
  59.8 0.3 convolution_bitcast_fusion.8
  60.1 0.3 convolution_bitcast_fusion.4
  60.4 0.4 convolution_bitcast_fusion
  60.8 0.4 convolution_bitcast_fusion.1
  61.2 0.3 convolution_bitcast_fusion.2
  61.5 1.2 fusion.109
  62.7 1.4 fusion.38
  64.0 0.9 collective-permute-start.5
  64.9 4.2 %collective-permute-start.6 = (bf16[1,64,32,1]{3,1,2,0:T(8,128)(2,1)}, bf16[1,64,32,1]{3,1,2,0:T(8,128)(2,1)S(1)}, u32[]{:S(2)}, u32[]{:S(2)}) collective-permute-start(bf16[1,64,32,1]{3,1,2,0:T(8,128)(2,1)} %get-tuple-element.41), channel_id=1, source_target_pairs={{1,0},{2,1},{3,2},{4,3},{5,4},{6,5},{7,6},{8,7},{9,8},{10,9},{11,1... | collective-permute-start | bytes 12296 | tf_op jit(solution)/shard_map/ppermute | solution.py:21
  69.1 0.5 convolution_bitcast_fusion.3
  69.7 0.4 convolution_bitcast_fusion.5
  70.1 0.7 pad_maximum_fusion.6
  70.9 1.1 copy.24
  72.0 15.3 %collective-permute-done.5 = bf16[1,64,32,1]{3,1,2,0:T(8,128)(2,1)S(1)} collective-permute-done((bf16[1,64,32,1]{3,1,2,0:T(8,128)(2,1)}, bf16[1,64,32,1]{3,1,2,0:T(8,128)(2,1)S(1)}, u32[]{:S(2)}, u32[]{:S(2)}) %collective-permute-start.5) | collective-permute-done | bytes 4128 | tf_op jit(solution)/shard_map/ppermute | solution.py:19
  87.3 3.6 %collective-permute-done.6 = bf16[1,64,32,1]{3,1,2,0:T(8,128)(2,1)S(1)} collective-permute-done((bf16[1,64,32,1]{3,1,2,0:T(8,128)(2,1)}, bf16[1,64,32,1]{3,1,2,0:T(8,128)(2,1)S(1)}, u32[]{:S(2)}, u32[]{:S(2)}) %collective-permute-start.6) | collective-permute-done | bytes 4128 | tf_op jit(solution)/shard_map/ppermute | solution.py:21
  91.0 1.9 collective-permute-start.7
  93.0 0.2 fusion.54
  93.2 0.2 convolution_add_fusion.15
  93.4 0.2 fusion.9
  93.6 4.4 %collective-permute-start.8 = (bf16[1,64,1,130]{3,1,2,0:T(8,128)(2,1)S(1)}, bf16[1,64,1,130]{3,1,2,0:T(8,128)(2,1)S(1)}, u32[]{:S(2)}, u32[]{:S(2)}) collective-permute-start(bf16[1,64,1,130]{3,1,2,0:T(8,128)(2,1)S(1)} %get-tuple-element.33), channel_id=1, source_target_pairs={{0,16},{16,32},{32,48},{48,64},{64,80},{80,96},{96,112},{112,128},... | collective-permute-start | bytes 49928 | tf_op jit(solution)/shard_map/ppermute | solution.py:19
  98.1 0.2 fusion.53
  98.3 0.2 convolution_add_fusion.13
  98.5 0.2 fusion.8
  98.7 5.4 %collective-permute-start.9 = (bf16[1,64,2,128]{3,1,2,0:T(8,128)(2,1)S(1)}, bf16[1,64,2,128]{3,1,2,0:T(8,128)(2,1)S(1)}, u32[]{:S(2)}, u32[]{:S(2)}) collective-permute-start(bf16[1,64,2,128]{3,1,2,0:T(8,128)(2,1)S(1)} %pad_maximum_fusion.14), channel_id=1, source_target_pairs={{0,8},{1,9},{2,10},{3,11},{4,12},{5,13},{6,14},{7,15},{8,0},{9,1},... | collective-permute-start | bytes 98312 | tf_op jit(solution)/shard_map/ppermute | solution.py:31
  104.2 0.9 pad_maximum_fusion.1
  105.1 0.4 fusion.26
  105.5 0.4 convolution_add_fusion.11
  105.9 0.3 convolution_add_fusion.10
  106.3 0.4 fusion.19
  106.7 0.8 copy-done
  107.5 0.6 fusion.5
  108.0 0.4 fusion.4
  108.5 0.4 convolution_add_fusion.7
  108.9 0.3 fusion.3
  109.3 0.6 copy-done.6
  109.9 0.2 fusion.11
  110.2 1.1 copy.25
  111.3 205.8 %all-reduce.2.cloned.1.call-done = f32[3,3,64,64]{3,2,1,0:T(8,128)} async-done(((f32[3,3,64,64]{3,2,1,0:T(8,128)}), f32[3,3,64,64]{3,2,1,0:T(8,128)}) %all-reduce.2.cloned.1.call-update) | async-done | bytes 147472 | tf_op jit(solution)/shard_map/psum | solution.py:124
  317.1 1.7 broadcast_multiply_fusion
  (26 shorter events, 0.3 us)
Async XLA Ops:
  7.2 309.9 %all-reduce.2.cloned.1.call-start = ((), (), s32[]{:S(2)}) async-start(), calls=%async_computation | async-start | bytes 589824 | tf_op jit(solution)/shard_map/psum | solution.py:124
  8.7 42.2 %copy-start.1 = (bf16[1,64,32,128]{3,2,1,0:T(8,128)(2,1)S(1)}, bf16[1,64,32,128]{3,2,1,0:T(8,128)(2,1)}, u32[]{:S(2)}) copy-start(bf16[1,64,32,128]{3,2,1,0:T(8,128)(2,1)} %param.7) | copy-start | bytes 1572868
  8.7 42.2 %copy-start.3 = (bf16[3,3,64,64]{3,2,1,0:T(8,128)(2,1)S(1)}, bf16[3,3,64,64]{3,2,1,0:T(8,128)(2,1)}, u32[]{:S(2)}) copy-start(bf16[3,3,64,64]{3,2,1,0:T(8,128)(2,1)} %param.8) | copy-start | bytes 221188
  8.7 25.6 %collective-permute-start = (bf16[1,64,32,1]{3,1,2,0:T(8,128)(2,1)S(1)}, bf16[1,64,32,1]{3,1,2,0:T(8,128)(2,1)S(1)}, u32[]{:S(2)}, u32[]{:S(2)}) collective-permute-start(bf16[1,64,32,1]{3,1,2,0:T(8,128)(2,1)S(1)} %get-tuple-element.42), channel_id=1, source_target_pairs={{0,1},{1,2},{2,3},{3,4},{4,5},{5,6},{6,7},{7,8},{8,9},{9,10},{10,1... | collective-permute-start | bytes 12296 | tf_op jit(solution)/shard_map/ppermute | solution.py:19
  12.6 25.2 %collective-permute-start.1 = (bf16[1,64,32,1]{3,1,2,0:T(8,128)(2,1)S(1)}, bf16[1,64,32,1]{3,1,2,0:T(8,128)(2,1)S(1)}, u32[]{:S(2)}, u32[]{:S(2)}) collective-permute-start(bf16[1,64,32,1]{3,1,2,0:T(8,128)(2,1)S(1)} %get-tuple-element.43), channel_id=1, source_target_pairs={{1,0},{2,1},{3,2},{4,3},{5,4},{6,5},{7,6},{8,7},{9,8},{10,9},{11,1... | collective-permute-start | bytes 12296 | tf_op jit(solution)/shard_map/ppermute | solution.py:21
  37.9 13.3 %collective-permute-start.3 = (bf16[1,64,1,130]{3,1,2,0:T(8,128)(2,1)S(1)}, bf16[1,64,1,130]{3,1,2,0:T(8,128)(2,1)S(1)}, u32[]{:S(2)}, u32[]{:S(2)}) collective-permute-start(bf16[1,64,1,130]{3,1,2,0:T(8,128)(2,1)S(1)} %get-tuple-element.36), channel_id=1, source_target_pairs={{0,16},{16,32},{32,48},{48,64},{64,80},{80,96},{96,112},{112,128},... | collective-permute-start | bytes 49928 | tf_op jit(solution)/shard_map/ppermute | solution.py:19
  42.8 8.5 %collective-permute-start.4 = (bf16[1,64,1,130]{3,1,2,0:T(8,128)(2,1)S(1)}, bf16[1,64,1,130]{3,1,2,0:T(8,128)(2,1)S(1)}, u32[]{:S(2)}, u32[]{:S(2)}) collective-permute-start(bf16[1,64,1,130]{3,1,2,0:T(8,128)(2,1)S(1)} %get-tuple-element.37), channel_id=1, source_target_pairs={{16,0},{32,16},{48,32},{64,48},{80,64},{96,80},{112,96},{128,112},... | collective-permute-start | bytes 49928 | tf_op jit(solution)/shard_map/ppermute | solution.py:21
  44.7 7.8 %collective-permute-start.2 = (bf16[1,64,2,130]{3,1,2,0:T(8,128)(2,1)S(1)}, bf16[1,64,2,130]{3,1,2,0:T(8,128)(2,1)S(1)}, u32[]{:S(2)}, u32[]{:S(2)}) collective-permute-start(bf16[1,64,2,130]{3,1,2,0:T(8,128)(2,1)S(1)} %pad_maximum_fusion.7), channel_id=1, source_target_pairs={{0,8},{1,9},{2,10},{3,11},{4,12},{5,13},{6,14},{7,15},{8,0},{9,1},... | collective-permute-start | bytes 99848 | tf_op jit(solution)/shard_map/ppermute | solution.py:31
  55.8 1.0 copy-start.2
  55.8 1.2 copy-start.5
  64.0 23.3 %collective-permute-start.5 = (bf16[1,64,32,1]{3,1,2,0:T(8,128)(2,1)}, bf16[1,64,32,1]{3,1,2,0:T(8,128)(2,1)S(1)}, u32[]{:S(2)}, u32[]{:S(2)}) collective-permute-start(bf16[1,64,32,1]{3,1,2,0:T(8,128)(2,1)} %get-tuple-element.40), channel_id=1, source_target_pairs={{0,1},{1,2},{2,3},{3,4},{4,5},{5,6},{6,7},{7,8},{8,9},{9,10},{10,1... | collective-permute-start | bytes 12296 | tf_op jit(solution)/shard_map/ppermute | solution.py:19
  64.9 26.0 %collective-permute-start.6 = (bf16[1,64,32,1]{3,1,2,0:T(8,128)(2,1)}, bf16[1,64,32,1]{3,1,2,0:T(8,128)(2,1)S(1)}, u32[]{:S(2)}, u32[]{:S(2)}) collective-permute-start(bf16[1,64,32,1]{3,1,2,0:T(8,128)(2,1)} %get-tuple-element.41), channel_id=1, source_target_pairs={{1,0},{2,1},{3,2},{4,3},{5,4},{6,5},{7,6},{8,7},{9,8},{10,9},{11,1... | collective-permute-start | bytes 12296 | tf_op jit(solution)/shard_map/ppermute | solution.py:21
  69.6 1.2 copy-start.4
  91.0 13.1 %collective-permute-start.7 = (bf16[1,64,1,130]{3,1,2,0:T(8,128)(2,1)S(1)}, bf16[1,64,1,130]{3,1,2,0:T(8,128)(2,1)S(1)}, u32[]{:S(2)}, u32[]{:S(2)}) collective-permute-start(bf16[1,64,1,130]{3,1,2,0:T(8,128)(2,1)S(1)} %get-tuple-element.32), channel_id=1, source_target_pairs={{16,0},{32,16},{48,32},{64,48},{80,64},{96,80},{112,96},{128,112},... | collective-permute-start | bytes 49928 | tf_op jit(solution)/shard_map/ppermute | solution.py:21
  93.6 10.6 %collective-permute-start.8 = (bf16[1,64,1,130]{3,1,2,0:T(8,128)(2,1)S(1)}, bf16[1,64,1,130]{3,1,2,0:T(8,128)(2,1)S(1)}, u32[]{:S(2)}, u32[]{:S(2)}) collective-permute-start(bf16[1,64,1,130]{3,1,2,0:T(8,128)(2,1)S(1)} %get-tuple-element.33), channel_id=1, source_target_pairs={{0,16},{16,32},{32,48},{48,64},{64,80},{80,96},{96,112},{112,128},... | collective-permute-start | bytes 49928 | tf_op jit(solution)/shard_map/ppermute | solution.py:19
  98.7 10.5 %collective-permute-start.9 = (bf16[1,64,2,128]{3,1,2,0:T(8,128)(2,1)S(1)}, bf16[1,64,2,128]{3,1,2,0:T(8,128)(2,1)S(1)}, u32[]{:S(2)}, u32[]{:S(2)}) collective-permute-start(bf16[1,64,2,128]{3,1,2,0:T(8,128)(2,1)S(1)} %pad_maximum_fusion.14), channel_id=1, source_target_pairs={{0,8},{1,9},{2,10},{3,11},{4,12},{5,13},{6,14},{7,15},{8,0},{9,1},... | collective-permute-start | bytes 98312 | tf_op jit(solution)/shard_map/ppermute | solution.py:31
  106.3 1.2 copy-start
  108.9 1.0 copy-start.6
Sparse Core Ops, SparseCore 0:
  71.0 246.0 all-reduce.1
where the time goes:
time: 326 us
  waiting for transfers between devices  246 us (75%)
  starting transfers between devices  39.1 us (12%)
  between operations  14.4 us (4%)
  matrix products  14.1 us (4%)
  local copies, waits for them, and re-layouts  7.26 us (2%)
  other arithmetic  4.87 us (1%)
    psum x1, waiting for transfers between devices, on_device(): summed = lax.psum(local_grad, ('lat', 'lon'))  206 us
    ppermute x4, waiting for transfers between devices, with_halo(): lax.ppermute(tail, axis, [(i, (i + 1) % count) for i in range(ends)])  31.8 us
    ppermute x4, starting transfers between devices, with_halo(): lax.ppermute(tail, axis, [(i, (i + 1) % count) for i in range(ends)])  14 us
    ppermute x4, starting transfers between devices, with_halo(): lax.ppermute(head, axis, [((i + 1) % count, i) for i in range(ends)])  13.4 us
    ppermute x2, starting transfers between devices, from_behind(): return lax.ppermute(value, axis, pairs)  11.6 us
    ppermute x4, waiting for transfers between devices, with_halo(): lax.ppermute(head, axis, [((i + 1) % count, i) for i in range(ends)])  6.99 us
  transfers between devices with their start and end apart: 11, of which 6 were waited for; matrix products, arithmetic and copies ran while one was open for 3% of the time, Pallas kernels for 0%

commit v1 on v0

v1 whole, which is shorter than its diff:
```python
import math

import jax
import jax.numpy as jnp
from jax import lax
from jax.experimental import pallas as pl
from jax.experimental.pallas import tpu as pltpu
from jax.sharding import Mesh
from jax.sharding import PartitionSpec as P

gelu_scale = math.sqrt(2.0 / math.pi)
ROWS, COLS, CH = 32, 128, 64
TAPS = 3 * CH
PIECES = 4
ROW_SLOTS = ({0: (0,), 1: (1,), ROWS - 1: (3,), ROWS - 2: (4,)}, {0: (2,), ROWS - 1: (5,)})
f32, bf16 = jnp.float32, jnp.bfloat16
LON = ("z", "side")
PLANE = ("lat", "side")
EVERY = ("lat", "z", "side")


def gelu_parts(hidden):
    square = hidden * hidden
    half = 0.5 + 0.5 * jnp.tanh(gelu_scale * hidden * (1.0 + 0.044715 * square))
    steep = gelu_scale * (1.0 + 3.0 * 0.044715 * square)
    return (hidden * half, half + 2.0 * hidden * half * (1.0 - half) * steep)


def roll(x, shift):
    return pltpu.roll(x, shift % x.shape[1], 1)


def lanes(width=COLS):
    return lax.broadcasted_iota(jnp.int32, (CH, width), 1)


def call(body, out_shape, args, scratch=(), flops=0, space=pltpu.VMEM, limit=24):
    outs = [jax.ShapeDtypeStruct(s, d) for s, d in out_shape]
    size = sum(a.size * a.dtype.itemsize for a in list(args) + outs)
    return pl.pallas_call(
        body,
        out_shape=outs,
        in_specs=[pl.BlockSpec(memory_space=space)] * len(args),
        out_specs=[pl.BlockSpec(memory_space=pltpu.VMEM)] * len(outs),
        scratch_shapes=list(scratch),
        cost_estimate=pl.CostEstimate(flops=flops, bytes_accessed=size, transcendentals=0),
        compiler_params=pltpu.CompilerParams(vmem_limit_bytes=limit * 2**20),
    )(*args)


def pack_body(f_hbm, g_hbm, edge_ref, rows_ref, wide, f_ref, g_ref, sems):
    lane = lanes()
    part = CH * ROWS // PIECES
    copies = [
        [
            pltpu.make_async_copy(src.at[pl.ds(i * part, part)], dst.at[pl.ds(i * part, part)], sems.at[at, i])
            for i in range(PIECES)
        ]
        for at, (src, dst) in enumerate(((f_hbm, f_ref), (g_hbm, g_ref)))
    ]
    for copy in copies[0] + copies[1]:
        copy.start()
    for at, src in enumerate((f_ref, g_ref)):
        for i, copy in enumerate(copies[at]):
            copy.wait()
            wide[pl.ds(i * part, part), :] = src[pl.ds(i * part, part), :].astype(f32)
        edge = jnp.zeros((CH, COLS), f32)
        for r in range(ROWS):
            row = wide[pl.ds(r, CH, stride=ROWS), :]
            edge = jnp.where((lane >= 4 * r) & (lane < 4 * r + 4), roll(row, 4 * r + 2), edge)
            for slot in ROW_SLOTS[at].get(r, ()):
                rows_ref[pl.ds(slot * CH, CH), :] = row.astype(bf16)
        edge_ref[pl.ds(at * CH, CH), :] = edge.astype(bf16)


def turn_body(f_ref, g_ref, fr_ref, gr_ref, wide):
    for src, dst in ((f_ref, fr_ref), (g_ref, gr_ref)):
        wide[...] = src[...].astype(f32)
        for r in range(ROWS):
            dst[r] = wide[pl.ds(r, CH, stride=ROWS), :].astype(bf16)


def strip(west_ref, east_ref, part):
    at = pl.ds(part * CH, CH)
    return jnp.where(lanes() % 4 < 2, west_ref[at, :].astype(f32), east_ref[at, :].astype(f32))


def ring_body(rows_ref, west_ref, east_ref, ahead_ref, behind_ref):
    rising = lax.axis_index("z") < lax.axis_size("z") // 2
    lane = lanes()
    s = strip(west_ref, east_ref, 0)
    gs = strip(west_ref, east_ref, 1)
    top = jnp.where(lane < 8, s, roll(gs, 8))
    bottom = jnp.where(lane < 4, roll(s, 4), jnp.where(lane < 8, roll(s, 12), roll(gs, 12)))
    half = pl.ds(0, TAPS)
    first = rows_ref[pl.ds(0, TAPS), :]
    last = rows_ref[pl.ds(TAPS, TAPS), :]
    ahead_ref[half, :] = jnp.where(rising, last, first)
    behind_ref[half, :] = jnp.where(rising, first, last)
    corner = pl.ds(TAPS, CH)
    ahead_ref[corner, :] = jnp.where(rising, bottom, top).astype(bf16)
    behind_ref[corner, :] = jnp.where(rising, top, bottom).astype(bf16)


def stack_taps(out_ref, at, own, halo, lane):
    out_ref[at, pl.ds(0, CH), :] = roll(jnp.where(lane == COLS - 1, halo, own), 1).astype(bf16)
    out_ref[at, pl.ds(CH, CH), :] = own.astype(bf16)
    out_ref[at, pl.ds(2 * CH, CH), :] = roll(jnp.where(lane == 0, halo, own), -1).astype(bf16)


def dot(a, b):
    return jnp.dot(a, b, preferred_element_type=f32)


def forward_body(
    fr_ref, gr_ref, edge_ref, west_ref, east_ref, ahead_ref, behind_ref, w_ref, w3_ref, wa_ref,
    out_ref, delta_ref, dstrip_ref, grad_ref, xs, wide,
):
    lat = lax.axis_index("lat")
    at_top = lat == 0
    at_bottom = lat == lax.axis_size("lat") - 1
    rising = lax.axis_index("z") < lax.axis_size("z") // 2
    lane = lanes()
    north = jnp.where(rising, ahead_ref[...], behind_ref[...]).astype(f32)
    south = jnp.where(rising, behind_ref[...], ahead_ref[...]).astype(f32)
    n_near, n_far, n_cot, n_corner = [north[i * CH : (i + 1) * CH] for i in range(4)]
    s_near, s_far, s_cot, s_corner = [south[i * CH : (i + 1) * CH] for i in range(4)]

    s = strip(west_ref, east_ref, 0)
    beyond = jnp.where(
        lane < 64, s_corner, jnp.where(lane >= 124, roll(n_corner, 124), roll(n_corner, 116))
    )
    gs = strip(west_ref, east_ref, 1)
    gbeyond = jnp.where(lane < 64, roll(s_corner, 120), roll(n_corner, 116))

    stack_taps(xs, 0, n_far, roll(beyond, -122), lane)
    stack_taps(xs, 1, n_near, roll(beyond, -126), lane)
    for r in range(ROWS):
        stack_taps(xs, r + 2, fr_ref[r].astype(f32), roll(s, -(4 * r + 2)), lane)
    stack_taps(xs, ROWS + 2, s_near, roll(beyond, -2), lane)
    stack_taps(xs, ROWS + 3, s_far, roll(beyond, -6), lane)

    weights = w_ref[...]
    for r in range(0, ROWS, 2):
        window = jnp.concatenate(
            [xs[r + 1 : r + 4].reshape(3 * TAPS, COLS), xs[r + 2 : r + 5].reshape(3 * TAPS, COLS)], 1
        )
        value, slope = gelu_parts(dot(weights, window))
        for k in range(2):
            cut = slice(k * COLS, (k + 1) * COLS)
            wide[pl.ds(r + k, CH, stride=ROWS), :] = fr_ref[r + k].astype(f32) + value[:, cut]
            delta_ref[r + k + 1] = (gr_ref[r + k].astype(f32) * slope[:, cut]).astype(bf16)
    out_ref[...] = wide[...].astype(bf16)

    def outer(inside, near, far, flip, cot, up):
        ends = (far, inside) if up else (inside, far)
        first = jnp.where(flip, xs[ends[1]], xs[ends[0]])
        last = jnp.where(flip, xs[ends[0]], xs[ends[1]])
        total = dot(w3_ref[0], first) + dot(w3_ref[1], xs[near]) + dot(w3_ref[2], last)
        return (cot * gelu_parts(total)[1]).astype(bf16)

    delta_ref[0] = outer(2, 1, 0, at_top, n_cot, True)
    delta_ref[ROWS + 1] = outer(ROWS + 1, ROWS + 2, ROWS + 3, at_bottom, s_cot, False)

    own_beyond = jnp.where(
        lane < 64,
        jnp.where(lane < 4, roll(s_near, 2), roll(s_far, 6)),
        jnp.where(lane >= 124, roll(n_near, 126), roll(n_far, 122)),
    )
    halo = jnp.concatenate([s, beyond], 1)
    own = jnp.concatenate([edge_ref[pl.ds(0, CH), :].astype(f32), own_beyond], 1)
    wide_lane = lanes(2 * COLS)
    kind = wide_lane % 4
    columns = jnp.concatenate(
        [roll(jnp.where(kind == 0, halo, own), 1), halo, roll(jnp.where(kind == 3, halo, own), -1)], 0
    ).astype(bf16)
    y = dot(wa_ref[...], columns)
    y0, y1, y2 = [y[i * CH : (i + 1) * CH] for i in range(3)]
    straight = roll(y0, 4) + y1 + roll(y2, -4)
    turned = roll(y2, 4) + y1 + roll(y0, -4)
    flip = ((wide_lane >= 252) & at_top) | ((wide_lane >= 128) & (wide_lane < 132) & at_bottom)
    slope = gelu_parts(jnp.where(flip, turned, straight))[1]
    dstrip_ref[...] = (jnp.concatenate([gs, gbeyond], 1) * slope).astype(bf16)

    total = None
    group = 8
    for r in range(0, ROWS, group):
        left = jnp.concatenate([delta_ref[r + k + 1] for k in range(group)], 1)
        right = jnp.concatenate([xs[r + k + 1 : r + k + 4].reshape(3 * TAPS, COLS) for k in range(group)], 1)
        term = lax.dot_general(left, right, (((1,), (1,)), ((), ())), preferred_element_type=f32)
        total = term if total is None else total + term
    total = total * grad_scale()
    pieces = [total[:, p * COLS : (p + 1) * COLS] for p in range(4)] + [total[:, 4 * COLS :]]
    count = grad_ref.shape[0]
    for at, piece in enumerate(pieces):
        for j in range(CH // count):
            width = piece.shape[1]
            start = at * COLS * CH // count + j * width
            grad_ref[:, 0, pl.ds(start, width)] = piece[j * count : (j + 1) * count]


def grad_scale():
    return float(ROWS * COLS * lax.axis_size(EVERY)) ** (-0.5)


def backward_body(delta_ref, dstrip_ref, gr_ref, wb_ref, wb3_ref, out_ref, xs, wide):
    lat = lax.axis_index("lat")
    at_top = lat == 0
    at_bottom = lat == lax.axis_size("lat") - 1
    lane = lanes()
    s = dstrip_ref[:, :COLS].astype(f32)
    beyond = dstrip_ref[:, COLS:].astype(f32)
    stack_taps(xs, 0, delta_ref[0].astype(f32), roll(beyond, -126), lane)
    for r in range(ROWS):
        stack_taps(xs, r + 1, delta_ref[r + 1].astype(f32), roll(s, -(4 * r + 2)), lane)
    stack_taps(xs, ROWS + 1, delta_ref[ROWS + 1].astype(f32), roll(beyond, -2), lane)
    weights = wb_ref[...]

    def put(r, back):
        wide[pl.ds(r, CH, stride=ROWS), :] = gr_ref[r].astype(f32) + back

    upper = jnp.where(at_top, wb3_ref[2], wb3_ref[0])
    lower = jnp.where(at_bottom, wb3_ref[0], wb3_ref[2])
    put(0, dot(upper, xs[0]) + dot(wb3_ref[1], xs[1]) + dot(wb3_ref[2], xs[2]))
    end = ROWS - 1
    put(end, dot(wb3_ref[0], xs[end]) + dot(wb3_ref[1], xs[end + 1]) + dot(lower, xs[end + 2]))
    for r in range(1, ROWS - 1, 2):
        window = jnp.concatenate(
            [xs[r : r + 3].reshape(3 * TAPS, COLS), xs[r + 1 : r + 4].reshape(3 * TAPS, COLS)], 1
        )
        back = dot(weights, window)
        put(r, back[:, :COLS])
        put(r + 1, back[:, COLS:])
    out_ref[...] = wide[...].astype(bf16)


def fold_body(parts_ref, out_ref):
    total = jnp.sum(parts_ref[...], 0)
    for i in range(out_ref.shape[0]):
        out_ref[i] = total


def unpack_body(parts_ref, out_ref):
    count = parts_ref.shape[0]
    for tap in range(9):
        at = tap // 2
        width = min(COLS, 9 * CH - at * COLS)
        for j in range(CH // count):
            start = at * COLS * CH // count + j * width + (tap % 2) * CH
            out_ref[tap, pl.ds(j * count, count), :] = parts_ref[:, 0, pl.ds(start, CH)]


def ring_pairs(lat_count, lon_count):
    half = lon_count // 2
    pairs = []
    for l in range(lat_count):
        for m in range(lon_count):
            if m < half:
                to = (l + 1, m) if l + 1 < lat_count else (l, m + half)
            else:
                to = (l - 1, m) if l > 0 else (l, m - half)
            pairs.append((l * lon_count + m, to[0] * lon_count + to[1]))
    return pairs


def on_device(field, kernel, cotangent):
    lat_count = lax.axis_size("lat")
    lon_count = lax.axis_size(LON)
    plane = lax.axis_size(PLANE)
    flat = (CH * ROWS, COLS)
    rows_shape = (ROWS, CH, COLS)

    flat_field, flat_cotangent = field.reshape(flat), cotangent.reshape(flat)
    edge, rows = call(
        pack_body,
        [((2 * CH, COLS), bf16), ((2 * TAPS, COLS), bf16)],
        (flat_field, flat_cotangent),
        [
            pltpu.VMEM(flat, f32),
            pltpu.VMEM(flat, bf16),
            pltpu.VMEM(flat, bf16),
            pltpu.SemaphoreType.DMA((2, PIECES)),
        ],
        space=pl.ANY,
        limit=56,
    )
    fr, gr = call(
        turn_body, [(rows_shape, bf16)] * 2, (flat_field, flat_cotangent), [pltpu.VMEM(flat, f32)]
    )
    right = [(i, (i + 1) % lon_count) for i in range(lon_count)]
    left = [(b, a) for a, b in right]
    west = lax.ppermute(edge, LON, right)
    east = lax.ppermute(edge, LON, left)

    ahead, behind = call(
        ring_body, [((4 * CH, COLS), bf16), ((4 * CH, COLS), bf16)], (rows, west, east)
    )
    ring = ring_pairs(lat_count, lon_count)
    ahead = lax.ppermute(ahead, EVERY, ring)
    behind = lax.ppermute(behind, EVERY, [(b, a) for a, b in ring])

    w3 = jnp.transpose(kernel, (0, 2, 1, 3)).reshape(3, CH, TAPS)
    w = jnp.transpose(kernel, (2, 0, 1, 3)).reshape(CH, 3 * TAPS)
    turned = kernel[::-1, ::-1]
    wb3 = jnp.transpose(turned, (0, 3, 1, 2)).reshape(3, CH, TAPS)
    wb = jnp.transpose(turned, (3, 0, 1, 2)).reshape(CH, 3 * TAPS)

    conv_flops = 2 * 9 * CH * CH * ROWS * COLS
    output, delta, dstrip, grad = call(
        forward_body,
        [
            (flat, bf16),
            ((ROWS + 2, CH, COLS), bf16),
            ((CH, 2 * COLS), bf16),
            ((plane, 1, 9 * CH * CH // plane), f32),
        ],
        (fr, gr, edge, west, east, ahead, behind, w, w3, w3.reshape(TAPS, TAPS)),
        [pltpu.VMEM((ROWS + 4, TAPS, COLS), bf16), pltpu.VMEM(flat, f32)],
        2 * conv_flops,
    )

    def spread(parts, count):
        return call(fold_body, [((count,) + parts.shape[1:], f32)], (parts,))[0]

    parts = lax.all_to_all(grad, PLANE, 0, 0)
    parts = lax.all_to_all(spread(parts, lax.axis_size("z")), "z", 0, 0)
    (grad_input,) = call(
        backward_body,
        [(flat, bf16)],
        (delta, dstrip, gr, wb, wb3),
        [pltpu.VMEM((ROWS + 2, TAPS, COLS), bf16), pltpu.VMEM(flat, f32)],
        conv_flops,
    )
    parts = lax.all_to_all(spread(parts, plane), PLANE, 0, 0)
    (grad_kernel,) = call(unpack_body, [((9, CH, CH), f32)], (parts,))
    shape = field.shape
    return (output.reshape(shape), grad_input.reshape(shape), grad_kernel.reshape(kernel.shape))


def solution(mesh):
    lat_count, lon_count = mesh.devices.shape
    split = Mesh(mesh.devices.reshape(lat_count, lon_count // 2, 2), EVERY)
    block = P(None, None, "lat", LON)
    return jax.shard_map(
        on_device,
        mesh=split,
        in_specs=(block, P(), block),
        out_specs=(block, block, P()),
        check_vma=False,
    )
```

time: 326 us -> 71.9 us (0.22)
  waiting for transfers between devices: 246 us -> 7.46 us
  blocking collectives: 0 us -> 30.5 us
  starting transfers between devices: 39.1 us -> 17.6 us
  matrix products: 14.1 us -> 0 us
  between operations: 14.4 us -> 0.75 us
  Pallas kernels: 0 us -> 13.2 us
  local copies, waits for them, and re-layouts: 7.26 us -> 2.05 us
  other arithmetic: 4.87 us -> 0 us
    psum x1 -> x0, waiting for transfers between devices: 206 us -> none  [on_device(): summed = lax.psum(local_grad, ('lat', 'lon'))]
    ppermute x10 -> x4, waiting for transfers between devices: 40.1 us -> 2.92 us  [the longest x1 1.49 us: on_device(): behind = lax.ppermute(behind, EVERY, [(b, a) for a, b in ring])]
    all_to_all x0 -> x2, blocking collectives: none -> 30.5 us  [the longest x1 18.9 us: on_device(): parts = lax.all_to_all(grad, PLANE, 0, 0)]
    ppermute x10 -> x4, starting transfers between devices: 39.1 us -> 11.9 us  [the longest x1 5.38 us: on_device(): east = lax.ppermute(edge, LON, left)]
    dot_general x33 -> x0, matrix products: 14.1 us -> none  [the longest x9 4.9 us: on_device(): jnp.einsum('oc,bchw->bohw', kernel[tap_row, tap_col], window, preferred_e...]
    pallas_call x0 -> x8, Pallas kernels: none -> 13.2 us  [call(): pl.pallas_call(body, out_shape=outs, in_specs=[pl.BlockSpec(memory_space=...]
    all_to_all x0 -> x1, starting transfers between devices: none -> 5.67 us  [on_device(): parts = lax.all_to_all(spread(parts, plane), PLANE, 0, 0)]
    unnamed x17 -> x10, local copies, waits for them, and re-layouts: 5.81 us -> 0.91 us
  transfers between devices with their start and end apart: 11 -> 5, of which waited for: 6 -> 3; matrix products, arithmetic and copies ran while one was open for 3% -> 2% of each run, Pallas kernels for 0% -> 6%
where the time goes in v1:
time: 71.9 us; the launch traced here: 71.6 us
  blocking collectives  30.5 us (42%)
  starting transfers between devices  17.6 us (24%)
  Pallas kernels  13.2 us (18%)
  waiting for transfers between devices  7.46 us (10%)
  local copies, waits for them, and re-layouts  2.05 us (3%)
  between operations  0.75 us (1%)
    all_to_all x1, blocking collectives, on_device(): parts = lax.all_to_all(grad, PLANE, 0, 0)  18.9 us
    pallas_call x8, Pallas kernels, call(): pl.pallas_call(body, out_shape=outs, in_specs=[pl.BlockSpec(memory_space=...  13.2 us
    all_to_all x1, blocking collectives, on_device(): parts = lax.all_to_all(spread(parts, lax.axis_size('z')), 'z', 0, 0)  11.6 us
    all_to_all x1, starting transfers between devices, on_device(): parts = lax.all_to_all(spread(parts, plane), PLANE, 0, 0)  5.67 us
    ppermute x1, starting transfers between devices, on_device(): east = lax.ppermute(edge, LON, left)  5.38 us
    all_to_all x1, waiting for transfers between devices, on_device(): parts = lax.all_to_all(spread(parts, plane), PLANE, 0, 0)  4.54 us
    ppermute x1, starting transfers between devices, on_device(): west = lax.ppermute(edge, LON, right)  3.82 us
    ppermute x1, starting transfers between devices, on_device(): ahead = lax.ppermute(ahead, EVERY, ring)  2.72 us
  transfers between devices with their start and end apart: 5, of which 3 were waited for; matrix products, arithmetic and copies ran while one was open for 2% of the time, Pallas kernels for 6%

profile of v1, /device:TPU:1, one launch (start us, length us, event | category | flops | bytes accessed | tf_op | source)
XLA Modules:
  0.0 71.6 jit_solution(4663930871652209893)
XLA Ops:
  0.6 0.0 copy-start
  0.6 0.0 copy-start.1
  0.6 3.4 %shard_map.59 = (bf16[128,128]{1,0:T(8,128)(2,1)}, bf16[384,128]{1,0:T(8,128)(2,1)}) custom-call(bf16[2048,128]{1,0:T(8,128)(2,1)} %bitcast.15, bf16[2048,128]{1,0:T(8,128)(2,1)} %bitcast.17), custom_call_target="tpu_custom_call" | custom-call | bytes 1179648 | tf_op jit(solution)/shard_map/pallas_call | solution.py:40
  4.1 3.8 %collective-permute-start = (bf16[128,128]{1,0:T(8,128)(2,1)}, bf16[128,128]{1,0:T(8,128)(2,1)S(1)}, u32[]{:S(2)}, u32[]{:S(2)}) collective-permute-start(bf16[128,128]{1,0:T(8,128)(2,1)} %get-tuple-element.15.edge_ref), channel_id=1, source_target_pairs={{0,1},{1,2},{2,3},{3,4},{4,5},{5,6},{6,7},{7,8},{8,9},{9,10},{10,1... | collective-permute-start | bytes 98312 | tf_op jit(solution)/shard_map/ppermute | solution.py:292
  7.9 5.4 %collective-permute-start.1 = (bf16[128,128]{1,0:T(8,128)(2,1)}, bf16[128,128]{1,0:T(8,128)(2,1)S(1)}, u32[]{:S(2)}, u32[]{:S(2)}) collective-permute-start(bf16[128,128]{1,0:T(8,128)(2,1)} %get-tuple-element.15.edge_ref), channel_id=1, source_target_pairs={{1,0},{2,1},{3,2},{4,3},{5,4},{6,5},{7,6},{8,7},{9,8},{10,9},{11,1... | collective-permute-start | bytes 98312 | tf_op jit(solution)/shard_map/ppermute | solution.py:293
  13.3 1.4 %collective-permute-done.west_ref = bf16[128,128]{1,0:T(8,128)(2,1)S(1)} collective-permute-done((bf16[128,128]{1,0:T(8,128)(2,1)}, bf16[128,128]{1,0:T(8,128)(2,1)S(1)}, u32[]{:S(2)}, u32[]{:S(2)}) %collective-permute-start) | collective-permute-done | bytes 32800 | tf_op jit(solution)/shard_map/ppermute | solution.py:292
  14.7 0.0 collective-permute-done.1.east_ref
  14.7 0.0 copy-start.2
  14.7 0.9 %copy-done.2 = bf16[384,128]{1,0:T(8,128)(2,1)S(1)} copy-done((bf16[384,128]{1,0:T(8,128)(2,1)S(1)}, bf16[384,128]{1,0:T(8,128)(2,1)}, u32[]{:S(2)}) %copy-start.2) | copy-done | bytes 98328
  15.6 0.1 shard_map.60
  15.7 2.7 %collective-permute-start.2 = (bf16[256,128]{1,0:T(8,128)(2,1)S(1)}, bf16[256,128]{1,0:T(8,128)(2,1)S(1)}, u32[]{:S(2)}, u32[]{:S(2)}) collective-permute-start(bf16[256,128]{1,0:T(8,128)(2,1)S(1)} %get-tuple-element.17), channel_id=1, source_target_pairs={{0,16},{1,17},{2,18},{3,19},{4,20},{5,21},{6,22},{7,23},{8,0},{9,1... | collective-permute-start | bytes 196616 | tf_op jit(solution)/shard_map/ppermute | solution.py:299
  18.4 0.0 copy-start.4
  18.4 0.0 collective-permute-start.3
  18.4 0.0 copy-done
  18.4 0.0 copy-done.1
  18.4 1.3 %shard_map.58 = (bf16[32,64,128]{2,1,0:T(8,128)(2,1)S(1)}, bf16[32,64,128]{2,1,0:T(8,128)(2,1)S(1)}) custom-call(bf16[2048,128]{1,0:T(8,128)(2,1)S(1)} %bitcast.16, bf16[2048,128]{1,0:T(8,128)(2,1)S(1)} %bitcast.18), custom_call_target="tpu_custom_call" | custom-call | bytes 2097152 | tf_op jit(solution)/shard_map/pallas_call | solution.py:40
  19.7 0.0 copy-done.4
  19.7 0.1 copy.13
  19.9 0.1 copy.12
  20.0 0.2 reshape_reshape.3.wa_ref
  20.2 0.1 copy.15.w3_ref
  20.3 0.1 copy.11
  20.5 0.0 copy-start.3
  20.5 0.1 copy.14.w_ref
  20.6 0.0 collective-permute-done.2.ahead_ref
  20.6 1.5 %collective-permute-done.3.behind_ref = bf16[256,128]{1,0:T(8,128)(2,1)S(1)} collective-permute-done((bf16[256,128]{1,0:T(8,128)(2,1)S(1)}, bf16[256,128]{1,0:T(8,128)(2,1)S(1)}, u32[]{:S(2)}, u32[]{:S(2)}) %collective-permute-start.3) | collective-permute-done | bytes 65568 | tf_op jit(solution)/shard_map/ppermute | solution.py:300
  22.1 0.0 copy-done.3
  22.1 3.9 %shard_map.61 = (bf16[2048,128]{1,0:T(8,128)(2,1)}, bf16[34,64,128]{2,1,0:T(8,128)(2,1)S(1)}, bf16[64,256]{1,0:T(8,128)(2,1)S(1)}, f32[32,1,1152]{2,1,0:T(1,128)S(1)}) custom-call(bf16[32,64,128]{2,1,0:T(8,128)(2,1)S(1)} %get-tuple-element.13.fr_ref, bf16[32,64,128]{2,1,0:T(8,128)(2,1)S(1)} %get-tuple-element.14.gr_ref, bf16[128,128]{1,0:T(8,128)(2,1)S(1)} %copy-done.3, ...), custom_call_target="tpu_custom_call" | custom-call | flops 603979776 | bytes 2760704 | tf_op jit(solution)/shard_map/pallas_call | solution.py:40
  26.0 18.9 %all_to_all.15.parts_ref = f32[32,1,1152]{2,1,0:T(1,128)S(1)} all-to-all(f32[32,1,1152]{2,1,0:T(1,128)S(1)} %get-tuple-element.22), channel_id=1, replica_groups=mesh['lat'=16,'z'=8,'side'=2] {'lat','side'}, dimensions={0} | all-to-all | bytes 294912 | tf_op jit(solution)/shard_map/all_to_all | solution.py:325
  44.9 0.1 shard_map.63
  45.0 11.6 %all_to_all.16.parts_ref = f32[8,1,1152]{2,1,0:T(1,128)S(1)} all-to-all(f32[8,1,1152]{2,1,0:T(1,128)S(1)} %shard_map.63), channel_id=1, replica_groups=mesh['lat'=16,'z'=8,'side'=2] {'z'}, dimensions={0} | all-to-all | bytes 73728 | tf_op jit(solution)/shard_map/all_to_all | solution.py:326
  56.6 0.7 shard_map.64
  57.4 5.7 %all-to-all-start.2 = ((f32[32,1,1152]{2,1,0:T(1,128)}), f32[32,1,1152]{2,1,0:T(1,128)S(1)}, u32[]{:S(2)}, u32[]{:S(2)}) async-start(f32[32,1,1152]{2,1,0:T(1,128)} %shard_map.64), calls=%async_computation.2 | async-start | bytes 294912 | tf_op jit(solution)/shard_map/all_to_all | solution.py:334
  63.1 0.1 copy.17.wb3_ref
  63.2 0.1 copy.16.wb_ref
  63.3 2.8 %shard_map.62 = bf16[2048,128]{1,0:T(8,128)(2,1)} custom-call(bf16[34,64,128]{2,1,0:T(8,128)(2,1)S(1)} %get-tuple-element.20.delta_ref, bf16[64,256]{1,0:T(8,128)(2,1)S(1)} %get-tuple-element.21.dstrip_ref, bf16[32,64,128]{2,1,0:T(8,128)(2,1)S(1)} %get-tuple-element.14.gr_ref, bf16[64,576]{1,0:T(8,128)(2,1)S(1)} %copy.16.wb_ref, ...), custom_call_target="tpu_custom_call" | custom-call | flops 301989888 | bytes 1785856 | tf_op jit(solution)/shard_map/pallas_call | solution.py:40
  66.2 4.5 %all-to-all-done.2.parts_ref = f32[32,1,1152]{2,1,0:T(1,128)S(1)} async-done(((f32[32,1,1152]{2,1,0:T(1,128)}), f32[32,1,1152]{2,1,0:T(1,128)S(1)}, u32[]{:S(2)}, u32[]{:S(2)}) %all-to-all-start.2) | async-done | bytes 147488 | tf_op jit(solution)/shard_map/all_to_all | solution.py:334
  70.7 0.9 %shard_map.65 = f32[9,64,64]{2,1,0:T(8,128)} custom-call(f32[32,1,1152]{2,1,0:T(1,128)S(1)} %all-to-all-done.2.parts_ref), custom_call_target="tpu_custom_call" | custom-call | bytes 294912 | tf_op jit(solution)/shard_map/pallas_call | solution.py:40
  (1 shorter events, 0.0 us)
Async XLA Ops:
  0.6 17.8 %copy-start = (bf16[1,64,32,128]{3,2,1,0:T(8,128)(2,1)S(1)}, bf16[1,64,32,128]{3,2,1,0:T(8,128)(2,1)}, u32[]{:S(2)}) copy-start(bf16[1,64,32,128]{3,2,1,0:T(8,128)(2,1)} %param.3) | copy-start | bytes 1572868
  0.6 17.8 %copy-start.1 = (bf16[1,64,32,128]{3,2,1,0:T(8,128)(2,1)S(1)}, bf16[1,64,32,128]{3,2,1,0:T(8,128)(2,1)}, u32[]{:S(2)}) copy-start(bf16[1,64,32,128]{3,2,1,0:T(8,128)(2,1)} %param.5) | copy-start | bytes 1572868
  4.1 10.6 %collective-permute-start = (bf16[128,128]{1,0:T(8,128)(2,1)}, bf16[128,128]{1,0:T(8,128)(2,1)S(1)}, u32[]{:S(2)}, u32[]{:S(2)}) collective-permute-start(bf16[128,128]{1,0:T(8,128)(2,1)} %get-tuple-element.15.edge_ref), channel_id=1, source_target_pairs={{0,1},{1,2},{2,3},{3,4},{4,5},{5,6},{6,7},{7,8},{8,9},{9,10},{10,1... | collective-permute-start | bytes 98312 | tf_op jit(solution)/shard_map/ppermute | solution.py:292
  7.9 6.8 %collective-permute-start.1 = (bf16[128,128]{1,0:T(8,128)(2,1)}, bf16[128,128]{1,0:T(8,128)(2,1)S(1)}, u32[]{:S(2)}, u32[]{:S(2)}) collective-permute-start(bf16[128,128]{1,0:T(8,128)(2,1)} %get-tuple-element.15.edge_ref), channel_id=1, source_target_pairs={{1,0},{2,1},{3,2},{4,3},{5,4},{6,5},{7,6},{8,7},{9,8},{10,9},{11,1... | collective-permute-start | bytes 98312 | tf_op jit(solution)/shard_map/ppermute | solution.py:293
  14.7 0.9 %copy-start.2 = (bf16[384,128]{1,0:T(8,128)(2,1)S(1)}, bf16[384,128]{1,0:T(8,128)(2,1)}, u32[]{:S(2)}) copy-start(bf16[384,128]{1,0:T(8,128)(2,1)} %get-tuple-element.16.rows_ref) | copy-start | bytes 294916
  15.7 4.9 %collective-permute-start.2 = (bf16[256,128]{1,0:T(8,128)(2,1)S(1)}, bf16[256,128]{1,0:T(8,128)(2,1)S(1)}, u32[]{:S(2)}, u32[]{:S(2)}) collective-permute-start(bf16[256,128]{1,0:T(8,128)(2,1)S(1)} %get-tuple-element.17), channel_id=1, source_target_pairs={{0,16},{1,17},{2,18},{3,19},{4,20},{5,21},{6,22},{7,23},{8,0},{9,1... | collective-permute-start | bytes 196616 | tf_op jit(solution)/shard_map/ppermute | solution.py:299
  18.4 1.3 %copy-start.4 = (bf16[3,3,64,64]{3,2,1,0:T(8,128)(2,1)S(1)}, bf16[3,3,64,64]{3,2,1,0:T(8,128)(2,1)}, u32[]{:S(2)}) copy-start(bf16[3,3,64,64]{3,2,1,0:T(8,128)(2,1)} %param.4) | copy-start | bytes 221188
  18.4 3.7 %collective-permute-start.3 = (bf16[256,128]{1,0:T(8,128)(2,1)S(1)}, bf16[256,128]{1,0:T(8,128)(2,1)S(1)}, u32[]{:S(2)}, u32[]{:S(2)}) collective-permute-start(bf16[256,128]{1,0:T(8,128)(2,1)S(1)} %get-tuple-element.18), channel_id=1, source_target_pairs={{16,0},{17,1},{18,2},{19,3},{20,4},{21,5},{22,6},{23,7},{0,8},{1,9... | collective-permute-start | bytes 196616 | tf_op jit(solution)/shard_map/ppermute | solution.py:300
  20.5 1.7 %copy-start.3 = (bf16[128,128]{1,0:T(8,128)(2,1)S(1)}, bf16[128,128]{1,0:T(8,128)(2,1)}, u32[]{:S(2)}) copy-start(bf16[128,128]{1,0:T(8,128)(2,1)} %get-tuple-element.15.edge_ref) | copy-start | bytes 98308
  57.4 13.4 %all-to-all-start.2 = ((f32[32,1,1152]{2,1,0:T(1,128)}), f32[32,1,1152]{2,1,0:T(1,128)S(1)}, u32[]{:S(2)}, u32[]{:S(2)}) async-start(f32[32,1,1152]{2,1,0:T(1,128)} %shard_map.64), calls=%async_computation.2 | async-start | bytes 294912 | tf_op jit(solution)/shard_map/all_to_all | solution.py:334

commit v2 on v1

--- a/solution.py
+++ b/solution.py
@@ -12,11 +12,11 @@
 ROWS, COLS, CH = 32, 128, 64
 TAPS = 3 * CH
 PIECES = 4
-ROW_SLOTS = ({0: (0,), 1: (1,), ROWS - 1: (3,), ROWS - 2: (4,)}, {0: (2,), ROWS - 1: (5,)})
 f32, bf16 = jnp.float32, jnp.bfloat16
 LON = ("z", "side")
-PLANE = ("lat", "side")
-EVERY = ("lat", "z", "side")
+LAT = ("low", "x", "core")
+EVERY = LAT + LON
+STAGES = (("x", "core"), ("low", "side"), ("z",))
 
 
 def gelu_parts(hidden):
@@ -44,11 +44,11 @@
         out_specs=[pl.BlockSpec(memory_space=pltpu.VMEM)] * len(outs),
         scratch_shapes=list(scratch),
         cost_estimate=pl.CostEstimate(flops=flops, bytes_accessed=size, transcendentals=0),
-        compiler_params=pltpu.CompilerParams(vmem_limit_bytes=limit * 2**20),
+        compiler_params=pltpu.CompilerParams(vmem_limit_bytes=int(limit * 2**20)),
     )(*args)
 
 
-def pack_body(f_hbm, g_hbm, edge_ref, rows_ref, wide, f_ref, g_ref, sems):
+def pack_body(f_hbm, g_hbm, edge_ref, f_ref, g_ref, wide, sems):
     lane = lanes()
     part = CH * ROWS // PIECES
     copies = [
@@ -68,8 +68,6 @@
         for r in range(ROWS):
             row = wide[pl.ds(r, CH, stride=ROWS), :]
             edge = jnp.where((lane >= 4 * r) & (lane < 4 * r + 4), roll(row, 4 * r + 2), edge)
-            for slot in ROW_SLOTS[at].get(r, ()):
-                rows_ref[pl.ds(slot * CH, CH), :] = row.astype(bf16)
         edge_ref[pl.ds(at * CH, CH), :] = edge.astype(bf16)
 
 
@@ -85,18 +83,19 @@
     return jnp.where(lanes() % 4 < 2, west_ref[at, :].astype(f32), east_ref[at, :].astype(f32))
 
 
-def ring_body(rows_ref, west_ref, east_ref, ahead_ref, behind_ref):
+def ring_body(fr_ref, gr_ref, west_ref, east_ref, ahead_ref, behind_ref):
     rising = lax.axis_index("z") < lax.axis_size("z") // 2
     lane = lanes()
     s = strip(west_ref, east_ref, 0)
     gs = strip(west_ref, east_ref, 1)
     top = jnp.where(lane < 8, s, roll(gs, 8))
     bottom = jnp.where(lane < 4, roll(s, 4), jnp.where(lane < 8, roll(s, 12), roll(gs, 12)))
-    half = pl.ds(0, TAPS)
-    first = rows_ref[pl.ds(0, TAPS), :]
-    last = rows_ref[pl.ds(TAPS, TAPS), :]
-    ahead_ref[half, :] = jnp.where(rising, last, first)
-    behind_ref[half, :] = jnp.where(rising, first, last)
+    end = ROWS - 1
+    pairs = ((fr_ref, 0, end), (fr_ref, 1, end - 1), (gr_ref, 0, end))
+    for at, (src, low, high) in enumerate(pairs):
+        part = pl.ds(at * CH, CH)
+        ahead_ref[part, :] = jnp.where(rising, src[high], src[low])
+        behind_ref[part, :] = jnp.where(rising, src[low], src[high])
     corner = pl.ds(TAPS, CH)
     ahead_ref[corner, :] = jnp.where(rising, bottom, top).astype(bf16)
     behind_ref[corner, :] = jnp.where(rising, top, bottom).astype(bf16)
@@ -114,11 +113,11 @@
 
 def forward_body(
     fr_ref, gr_ref, edge_ref, west_ref, east_ref, ahead_ref, behind_ref, w_ref, w3_ref, wa_ref,
-    out_ref, delta_ref, dstrip_ref, grad_ref, xs, wide,
+    out_ref, delta_ref, dstrip_ref, grad_ref, xs,
 ):
-    lat = lax.axis_index("lat")
+    lat = lax.axis_index(LAT)
     at_top = lat == 0
-    at_bottom = lat == lax.axis_size("lat") - 1
+    at_bottom = lat == lax.axis_size(LAT) - 1
     rising = lax.axis_index("z") < lax.axis_size("z") // 2
     lane = lanes()
     north = jnp.where(rising, ahead_ref[...], behind_ref[...]).astype(f32)
@@ -148,9 +147,8 @@
         value, slope = gelu_parts(dot(weights, window))
         for k in range(2):
             cut = slice(k * COLS, (k + 1) * COLS)
-            wide[pl.ds(r + k, CH, stride=ROWS), :] = fr_ref[r + k].astype(f32) + value[:, cut]
+            out_ref[r + k] = (fr_ref[r + k].astype(f32) + value[:, cut]).astype(bf16)
             delta_ref[r + k + 1] = (gr_ref[r + k].astype(f32) * slope[:, cut]).astype(bf16)
-    out_ref[...] = wide[...].astype(bf16)
 
     def outer(inside, near, far, flip, cot, up):
         ends = (far, inside) if up else (inside, far)
@@ -190,13 +188,16 @@
         term = lax.dot_general(left, right, (((1,), (1,)), ((), ())), preferred_element_type=f32)
         total = term if total is None else total + term
     total = total * grad_scale()
-    pieces = [total[:, p * COLS : (p + 1) * COLS] for p in range(4)] + [total[:, 4 * COLS :]]
-    count = grad_ref.shape[0]
-    for at, piece in enumerate(pieces):
-        for j in range(CH // count):
-            width = piece.shape[1]
-            start = at * COLS * CH // count + j * width
-            grad_ref[:, 0, pl.ds(start, width)] = piece[j * count : (j + 1) * count]
+    for p in range(4):
+        grad_ref[pl.ds(p * CH, CH), :] = total[:, p * COLS : (p + 1) * COLS]
+    tail = total[:, 4 * COLS :]
+    grad_ref[pl.ds(4 * CH, CH // 2), :] = jnp.concatenate([tail[: CH // 2], tail[CH // 2 :]], 1)
+
+
+def restore_body(rows_ref, out_ref, wide):
+    for r in range(ROWS):
+        wide[pl.ds(r, CH, stride=ROWS), :] = rows_ref[r].astype(f32)
+    out_ref[...] = wide[...].astype(bf16)
 
 
 def grad_scale():
@@ -204,9 +205,9 @@
 
 
 def backward_body(delta_ref, dstrip_ref, gr_ref, wb_ref, wb3_ref, out_ref, xs, wide):
-    lat = lax.axis_index("lat")
+    lat = lax.axis_index(LAT)
     at_top = lat == 0
-    at_bottom = lat == lax.axis_size("lat") - 1
+    at_bottom = lat == lax.axis_size(LAT) - 1
     lane = lanes()
     s = dstrip_ref[:, :COLS].astype(f32)
     beyond = dstrip_ref[:, COLS:].astype(f32)
@@ -234,20 +235,14 @@
     out_ref[...] = wide[...].astype(bf16)
 
 
-def fold_body(parts_ref, out_ref):
-    total = jnp.sum(parts_ref[...], 0)
-    for i in range(out_ref.shape[0]):
-        out_ref[i] = total
-
-
 def unpack_body(parts_ref, out_ref):
-    count = parts_ref.shape[0]
-    for tap in range(9):
-        at = tap // 2
-        width = min(COLS, 9 * CH - at * COLS)
-        for j in range(CH // count):
-            start = at * COLS * CH // count + j * width + (tap % 2) * CH
-            out_ref[tap, pl.ds(j * count, count), :] = parts_ref[:, 0, pl.ds(start, CH)]
+    for p in range(4):
+        block = parts_ref[pl.ds(p * CH, CH), :]
+        out_ref[2 * p] = block[:, :CH]
+        out_ref[2 * p + 1] = block[:, CH:]
+    tail = parts_ref[pl.ds(4 * CH, CH // 2), :]
+    out_ref[8, pl.ds(0, CH // 2), :] = tail[:, :CH]
+    out_ref[8, pl.ds(CH // 2, CH // 2), :] = tail[:, CH:]
 
 
 def ring_pairs(lat_count, lon_count):
@@ -264,28 +259,25 @@
 
 
 def on_device(field, kernel, cotangent):
-    lat_count = lax.axis_size("lat")
+    lat_count = lax.axis_size(LAT)
     lon_count = lax.axis_size(LON)
-    plane = lax.axis_size(PLANE)
     flat = (CH * ROWS, COLS)
     rows_shape = (ROWS, CH, COLS)
 
     flat_field, flat_cotangent = field.reshape(flat), cotangent.reshape(flat)
-    edge, rows = call(
+    edge, f_near, g_near = call(
         pack_body,
-        [((2 * CH, COLS), bf16), ((2 * TAPS, COLS), bf16)],
+        [((2 * CH, COLS), bf16), (flat, bf16), (flat, bf16)],
         (flat_field, flat_cotangent),
         [
             pltpu.VMEM(flat, f32),
-            pltpu.VMEM(flat, bf16),
-            pltpu.VMEM(flat, bf16),
             pltpu.SemaphoreType.DMA((2, PIECES)),
         ],
         space=pl.ANY,
-        limit=56,
+        limit=52.5,
     )
     fr, gr = call(
-        turn_body, [(rows_shape, bf16)] * 2, (flat_field, flat_cotangent), [pltpu.VMEM(flat, f32)]
+        turn_body, [(rows_shape, bf16)] * 2, (f_near, g_near), [pltpu.VMEM(flat, f32)]
     )
     right = [(i, (i + 1) % lon_count) for i in range(lon_count)]
     left = [(b, a) for a, b in right]
@@ -293,7 +285,7 @@
     east = lax.ppermute(edge, LON, left)
 
     ahead, behind = call(
-        ring_body, [((4 * CH, COLS), bf16), ((4 * CH, COLS), bf16)], (rows, west, east)
+        ring_body, [((4 * CH, COLS), bf16), ((4 * CH, COLS), bf16)], (fr, gr, west, east)
     )
     ring = ring_pairs(lat_count, lon_count)
     ahead = lax.ppermute(ahead, EVERY, ring)
@@ -306,24 +298,20 @@
     wb = jnp.transpose(turned, (3, 0, 1, 2)).reshape(CH, 3 * TAPS)
 
     conv_flops = 2 * 9 * CH * CH * ROWS * COLS
-    output, delta, dstrip, grad = call(
+    out_rows, delta, dstrip, grad = call(
         forward_body,
         [
-            (flat, bf16),
+            (rows_shape, bf16),
             ((ROWS + 2, CH, COLS), bf16),
             ((CH, 2 * COLS), bf16),
-            ((plane, 1, 9 * CH * CH // plane), f32),
+            ((9 * CH * CH // COLS, COLS), f32),
         ],
         (fr, gr, edge, west, east, ahead, behind, w, w3, w3.reshape(TAPS, TAPS)),
-        [pltpu.VMEM((ROWS + 4, TAPS, COLS), bf16), pltpu.VMEM(flat, f32)],
+        [pltpu.VMEM((ROWS + 4, TAPS, COLS), bf16)],
         2 * conv_flops,
     )
 
-    def spread(parts, count):
-        return call(fold_body, [((count,) + parts.shape[1:], f32)], (parts,))[0]
-
-    parts = lax.all_to_all(grad, PLANE, 0, 0)
-    parts = lax.all_to_all(spread(parts, lax.axis_size("z")), "z", 0, 0)
+    (output,) = call(restore_body, [(flat, bf16)], (out_rows,), [pltpu.VMEM(flat, f32)])
     (grad_input,) = call(
         backward_body,
         [(flat, bf16)],
@@ -331,16 +319,18 @@
         [pltpu.VMEM((ROWS + 2, TAPS, COLS), bf16), pltpu.VMEM(flat, f32)],
         conv_flops,
     )
-    parts = lax.all_to_all(spread(parts, plane), PLANE, 0, 0)
-    (grad_kernel,) = call(unpack_body, [((9, CH, CH), f32)], (parts,))
+    for stage in STAGES:
+        grad = lax.optimization_barrier(lax.psum(grad, stage))
+    (grad_kernel,) = call(unpack_body, [((9, CH, CH), f32)], (grad,))
     shape = field.shape
     return (output.reshape(shape), grad_input.reshape(shape), grad_kernel.reshape(kernel.shape))
 
 
 def solution(mesh):
     lat_count, lon_count = mesh.devices.shape
-    split = Mesh(mesh.devices.reshape(lat_count, lon_count // 2, 2), EVERY)
-    block = P(None, None, "lat", LON)
+    x = min(4, lat_count // 2)
+    split = Mesh(mesh.devices.reshape(lat_count // (2 * x), x, 2, lon_count // 2, 2), EVERY)
+    block = P(None, None, LAT, LON)
     return jax.shard_map(
         on_device,
         mesh=split,

time: 71.9 us -> 227 us (3.16); the launches traced: 71.6 us -> 223 us
  waiting for transfers between devices: 7.46 us -> 182 us
  blocking collectives: 30.5 us -> 0 us
  between operations: 0.75 us -> 13.8 us
  starting transfers between devices: 17.6 us -> 12.1 us
    psum x0 -> x3, waiting for transfers between devices: none -> 179 us  [on_device(): grad = lax.optimization_barrier(lax.psum(grad, stage))]
    all_to_all x2 -> x0, blocking collectives: 30.5 us -> none  [the longest x1 18.9 us: on_device(): parts = lax.all_to_all(grad, PLANE, 0, 0)]
    all_to_all x1 -> x0, starting transfers between devices: 5.67 us -> none  [on_device(): parts = lax.all_to_all(spread(parts, plane), PLANE, 0, 0)]
    all_to_all x1 -> x0, waiting for transfers between devices: 4.54 us -> none  [on_device(): parts = lax.all_to_all(spread(parts, plane), PLANE, 0, 0)]
    pallas_call x8 -> x7, Pallas kernels: 13.2 us -> 13.7 us  [call(): pl.pallas_call(body, out_shape=outs, in_specs=[pl.BlockSpec(memory_space=...]
  transfers between devices with their start and end apart: 5 -> 7, of which waited for: 3 -> 5; matrix products, arithmetic and copies ran while one was open for 2% -> 1% of each run, Pallas kernels for 6% -> 3%
where the time goes in v2:
time: 227 us; the launch traced here: 223 us
  waiting for transfers between devices  182 us (80%)
  between operations  13.8 us (6%)
  Pallas kernels  13.7 us (6%)
  starting transfers between devices  12.1 us (5%)
    psum x3, waiting for transfers between devices, on_device(): grad = lax.optimization_barrier(lax.psum(grad, stage))  179 us
    pallas_call x7, Pallas kernels, call(): pl.pallas_call(body, out_shape=outs, in_specs=[pl.BlockSpec(memory_space=...  13.7 us
    ppermute x1, starting transfers between devices, on_device(): east = lax.ppermute(edge, LON, left)  5.38 us
  transfers between devices with their start and end apart: 7, of which 5 were waited for; matrix products, arithmetic and copies ran while one was open for 1% of the time, Pallas kernels for 3%

profile of v2, /device:TPU:1, one launch (start us, length us, event | category | flops | bytes accessed | tf_op | source)
XLA Modules:
  0.0 223.3 jit_solution(16277774892971835296)
XLA Ops:
  7.2 0.0 all-reduce.4.cloned.1.call-start
  7.2 2.7 %shard_map.58 = (bf16[128,128]{1,0:T(8,128)(2,1)S(1)}, bf16[2048,128]{1,0:T(8,128)(2,1)S(1)}, bf16[2048,128]{1,0:T(8,128)(2,1)S(1)}) custom-call(bf16[2048,128]{1,0:T(8,128)(2,1)} %bitcast.23, bf16[2048,128]{1,0:T(8,128)(2,1)} %bitcast.24), custom_call_target="tpu_custom_call" | custom-call | bytes 2129920 | tf_op jit(solution)/shard_map/pallas_call | solution.py:40
  9.9 3.8 %collective-permute-start = (bf16[128,128]{1,0:T(8,128)(2,1)S(1)}, bf16[128,128]{1,0:T(8,128)(2,1)S(1)}, u32[]{:S(2)}, u32[]{:S(2)}) collective-permute-start(bf16[128,128]{1,0:T(8,128)(2,1)S(1)} %get-tuple-element.18.edge_ref), channel_id=1, source_target_pairs={{0,1},{1,2},{2,3},{3,4},{4,5},{5,6},{6,7},{7,8},{8,9},{9,10},{10,1... | collective-permute-start | bytes 98312 | tf_op jit(solution)/shard_map/ppermute | solution.py:284
  13.8 5.4 %collective-permute-start.1 = (bf16[128,128]{1,0:T(8,128)(2,1)S(1)}, bf16[128,128]{1,0:T(8,128)(2,1)S(1)}, u32[]{:S(2)}, u32[]{:S(2)}) collective-permute-start(bf16[128,128]{1,0:T(8,128)(2,1)S(1)} %get-tuple-element.18.edge_ref), channel_id=1, source_target_pairs={{1,0},{2,1},{3,2},{4,3},{5,4},{6,5},{7,6},{8,7},{9,8},{10,9},{11,1... | collective-permute-start | bytes 98312 | tf_op jit(solution)/shard_map/ppermute | solution.py:285
  19.1 1.3 shard_map.59
  20.4 0.0 collective-permute-done.west_ref
  20.4 0.0 collective-permute-done.1.east_ref
  20.4 0.0 copy-start.1
  20.4 0.1 shard_map.60
  20.5 2.6 %collective-permute-start.2 = (bf16[256,128]{1,0:T(8,128)(2,1)S(1)}, bf16[256,128]{1,0:T(8,128)(2,1)S(1)}, u32[]{:S(2)}, u32[]{:S(2)}) collective-permute-start(bf16[256,128]{1,0:T(8,128)(2,1)S(1)} %get-tuple-element.19), channel_id=1, source_target_pairs={{0,16},{1,17},{2,18},{3,19},{4,20},{5,21},{6,22},{7,23},{8,0},{9,1... | collective-permute-start | bytes 196616 | tf_op jit(solution)/shard_map/ppermute | solution.py:291
  23.2 0.0 collective-permute-start.3
  23.2 0.0 copy-done.1
  23.2 0.1 copy.13
  23.3 0.1 copy.12
  23.5 0.2 reshape_reshape.3.wa_ref
  23.6 0.1 copy.15.w3_ref
  23.8 0.1 copy.11
  23.9 0.1 copy.14.w_ref
  24.1 0.4 collective-permute-done.2.ahead_ref
  24.5 2.4 %collective-permute-done.3.behind_ref = bf16[256,128]{1,0:T(8,128)(2,1)S(1)} collective-permute-done((bf16[256,128]{1,0:T(8,128)(2,1)S(1)}, bf16[256,128]{1,0:T(8,128)(2,1)S(1)}, u32[]{:S(2)}, u32[]{:S(2)}) %collective-permute-start.3) | collective-permute-done | bytes 65568 | tf_op jit(solution)/shard_map/ppermute | solution.py:292
  26.9 4.0 %shard_map.61 = (bf16[32,64,128]{2,1,0:T(8,128)(2,1)S(1)}, bf16[34,64,128]{2,1,0:T(8,128)(2,1)S(1)}, bf16[64,256]{1,0:T(8,128)(2,1)S(1)}, f32[288,128]{1,0:T(8,128)}) custom-call(bf16[32,64,128]{2,1,0:T(8,128)(2,1)S(1)} %get-tuple-element.16.fr_ref, bf16[32,64,128]{2,1,0:T(8,128)(2,1)S(1)} %get-tuple-element.17.gr_ref, ...), custom_call_target="tpu_custom_call" | custom-call | flops 603979776 | bytes 2760704 | tf_op jit(solution)/shard_map/pallas_call | solution.py:40
  30.9 0.0 all-reduce.4.cloned.1.call-update
  30.9 0.0 all-reduce.6.cloned.1.call-start
  31.0 64.5 %all-reduce.4.cloned.1.call-done = f32[288,128]{1,0:T(8,128)} async-done(((f32[288,128]{1,0:T(8,128)}), f32[288,128]{1,0:T(8,128)}) %all-reduce.4.cloned.1.call-update) | async-done | bytes 147472 | tf_op jit(solution)/shard_map/psum | solution.py:323
  95.5 0.0 all-reduce.6.cloned.1.call-update
  95.5 0.2 all-reduce.8.cloned.1.call-start
  95.8 47.4 %all-reduce.6.cloned.1.call-done = f32[288,128]{1,0:T(8,128)} async-done(((f32[288,128]{1,0:T(8,128)}), f32[288,128]{1,0:T(8,128)}) %all-reduce.6.cloned.1.call-update) | async-done | bytes 147472 | tf_op jit(solution)/shard_map/psum | solution.py:323
  143.2 0.0 all-reduce.8.cloned.1.call-update
  143.2 0.1 copy.17.wb3_ref
  143.4 0.1 copy.16.wb_ref
  143.5 1.9 shard_map.62
  145.4 2.8 %shard_map.63 = bf16[2048,128]{1,0:T(8,128)(2,1)} custom-call(bf16[34,64,128]{2,1,0:T(8,128)(2,1)S(1)} %get-tuple-element.22.delta_ref, bf16[64,256]{1,0:T(8,128)(2,1)S(1)} %get-tuple-element.23.dstrip_ref, bf16[32,64,128]{2,1,0:T(8,128)(2,1)S(1)} %get-tuple-element.17.gr_ref, bf16[64,576]{1,0:T(8,128)(2,1)S(1)} %copy.16.wb_ref, ...), custom_call_target="tpu_custom_call" | custom-call | flops 301989888 | bytes 1785856 | tf_op jit(solution)/shard_map/pallas_call | solution.py:40
  148.3 66.8 %all-reduce.8.cloned.1.call-done.parts_ref = f32[288,128]{1,0:T(8,128)} async-done(((f32[288,128]{1,0:T(8,128)}), f32[288,128]{1,0:T(8,128)}) %all-reduce.8.cloned.1.call-update) | async-done | bytes 147472 | tf_op jit(solution)/shard_map/psum | solution.py:323
  215.0 0.0 copy-start
  215.0 0.9 copy-done
  215.9 0.8 shard_map.64
  (1 shorter events, 0.0 us)
Async XLA Ops:
  7.2 88.4 %all-reduce.4.cloned.1.call-start = ((), (), s32[]{:S(2)}) async-start(), calls=%async_computation | async-start | bytes 294912 | tf_op jit(solution)/shard_map/psum | solution.py:323
  9.9 10.5 %collective-permute-start = (bf16[128,128]{1,0:T(8,128)(2,1)S(1)}, bf16[128,128]{1,0:T(8,128)(2,1)S(1)}, u32[]{:S(2)}, u32[]{:S(2)}) collective-permute-start(bf16[128,128]{1,0:T(8,128)(2,1)S(1)} %get-tuple-element.18.edge_ref), channel_id=1, source_target_pairs={{0,1},{1,2},{2,3},{3,4},{4,5},{5,6},{6,7},{7,8},{8,9},{9,10},{10,1... | collective-permute-start | bytes 98312 | tf_op jit(solution)/shard_map/ppermute | solution.py:284
  13.8 6.7 %collective-permute-start.1 = (bf16[128,128]{1,0:T(8,128)(2,1)S(1)}, bf16[128,128]{1,0:T(8,128)(2,1)S(1)}, u32[]{:S(2)}, u32[]{:S(2)}) collective-permute-start(bf16[128,128]{1,0:T(8,128)(2,1)S(1)} %get-tuple-element.18.edge_ref), channel_id=1, source_target_pairs={{1,0},{2,1},{3,2},{4,3},{5,4},{6,5},{7,6},{8,7},{9,8},{10,9},{11,1... | collective-permute-start | bytes 98312 | tf_op jit(solution)/shard_map/ppermute | solution.py:285
  20.4 2.7 %copy-start.1 = (bf16[3,3,64,64]{3,2,1,0:T(8,128)(2,1)S(1)}, bf16[3,3,64,64]{3,2,1,0:T(8,128)(2,1)}, u32[]{:S(2)}) copy-start(bf16[3,3,64,64]{3,2,1,0:T(8,128)(2,1)} %param.4) | copy-start | bytes 221188
  20.5 4.0 %collective-permute-start.2 = (bf16[256,128]{1,0:T(8,128)(2,1)S(1)}, bf16[256,128]{1,0:T(8,128)(2,1)S(1)}, u32[]{:S(2)}, u32[]{:S(2)}) collective-permute-start(bf16[256,128]{1,0:T(8,128)(2,1)S(1)} %get-tuple-element.19), channel_id=1, source_target_pairs={{0,16},{1,17},{2,18},{3,19},{4,20},{5,21},{6,22},{7,23},{8,0},{9,1... | collective-permute-start | bytes 196616 | tf_op jit(solution)/shard_map/ppermute | solution.py:291
  23.2 3.7 %collective-permute-start.3 = (bf16[256,128]{1,0:T(8,128)(2,1)S(1)}, bf16[256,128]{1,0:T(8,128)(2,1)S(1)}, u32[]{:S(2)}, u32[]{:S(2)}) collective-permute-start(bf16[256,128]{1,0:T(8,128)(2,1)S(1)} %get-tuple-element.20), channel_id=1, source_target_pairs={{16,0},{17,1},{18,2},{19,3},{20,4},{21,5},{22,6},{23,7},{0,8},{1,9... | collective-permute-start | bytes 196616 | tf_op jit(solution)/shard_map/ppermute | solution.py:292
  30.9 112.3 %all-reduce.6.cloned.1.call-start = ((), (), s32[]{:S(2)}) async-start(), calls=%async_computation.1 | async-start | bytes 294912 | tf_op jit(solution)/shard_map/psum | solution.py:323
  95.5 119.5 %all-reduce.8.cloned.1.call-start = ((), (), s32[]{:S(2)}) async-start(), calls=%async_computation.2 | async-start | bytes 294912 | tf_op jit(solution)/shard_map/psum | solution.py:323
  215.0 0.9 copy-start
Sparse Core Ops, SparseCore 0:
  31.0 64.4 all-reduce.3
  98.0 45.2 all-reduce.5
  145.5 69.4 all-reduce.7

commit v3 on v1

--- a/solution.py
+++ b/solution.py
@@ -12,7 +12,6 @@
 ROWS, COLS, CH = 32, 128, 64
 TAPS = 3 * CH
 PIECES = 4
-ROW_SLOTS = ({0: (0,), 1: (1,), ROWS - 1: (3,), ROWS - 2: (4,)}, {0: (2,), ROWS - 1: (5,)})
 f32, bf16 = jnp.float32, jnp.bfloat16
 LON = ("z", "side")
 PLANE = ("lat", "side")
@@ -44,12 +43,11 @@
         out_specs=[pl.BlockSpec(memory_space=pltpu.VMEM)] * len(outs),
         scratch_shapes=list(scratch),
         cost_estimate=pl.CostEstimate(flops=flops, bytes_accessed=size, transcendentals=0),
-        compiler_params=pltpu.CompilerParams(vmem_limit_bytes=limit * 2**20),
+        compiler_params=pltpu.CompilerParams(vmem_limit_bytes=int(limit * 2**20)),
     )(*args)
 
 
-def pack_body(f_hbm, g_hbm, edge_ref, rows_ref, wide, f_ref, g_ref, sems):
-    lane = lanes()
+def pack_body(f_hbm, g_hbm, ahead_ref, behind_ref, f_ref, g_ref, wide, sems):
     part = CH * ROWS // PIECES
     copies = [
         [
@@ -60,46 +58,53 @@
     ]
     for copy in copies[0] + copies[1]:
         copy.start()
+    rising = lax.axis_index("z") < lax.axis_size("z") // 2
+    end = ROWS - 1
+    slots = (((0, 0, end), (1, 1, end - 1)), ((2, 0, end),))
     for at, src in enumerate((f_ref, g_ref)):
         for i, copy in enumerate(copies[at]):
             copy.wait()
             wide[pl.ds(i * part, part), :] = src[pl.ds(i * part, part), :].astype(f32)
+        for slot, low, high in slots[at]:
+            first = wide[pl.ds(low, CH, stride=ROWS), :]
+            last = wide[pl.ds(high, CH, stride=ROWS), :]
+            ahead_ref[pl.ds(slot * CH, CH), :] = jnp.where(rising, last, first).astype(bf16)
+            behind_ref[pl.ds(slot * CH, CH), :] = jnp.where(rising, first, last).astype(bf16)
+
+
+def turn_body(f_ref, g_ref, fr_ref, gr_ref, edge_ref, wide):
+    lane = lanes()
+    for at, (src, dst) in enumerate(((f_ref, fr_ref), (g_ref, gr_ref))):
+        wide[...] = src[...].astype(f32)
         edge = jnp.zeros((CH, COLS), f32)
         for r in range(ROWS):
             row = wide[pl.ds(r, CH, stride=ROWS), :]
             edge = jnp.where((lane >= 4 * r) & (lane < 4 * r + 4), roll(row, 4 * r + 2), edge)
-            for slot in ROW_SLOTS[at].get(r, ()):
-                rows_ref[pl.ds(slot * CH, CH), :] = row.astype(bf16)
+            dst[r] = row.astype(bf16)
         edge_ref[pl.ds(at * CH, CH), :] = edge.astype(bf16)
 
 
-def turn_body(f_ref, g_ref, fr_ref, gr_ref, wide):
-    for src, dst in ((f_ref, fr_ref), (g_ref, gr_ref)):
-        wide[...] = src[...].astype(f32)
-        for r in range(ROWS):
-            dst[r] = wide[pl.ds(r, CH, stride=ROWS), :].astype(bf16)
+def row_halos(ahead_ref, behind_ref):
+    rising = lax.axis_index("z") < lax.axis_size("z") // 2
+    north = jnp.where(rising, ahead_ref[...], behind_ref[...]).astype(f32)
+    south = jnp.where(rising, behind_ref[...], ahead_ref[...]).astype(f32)
+    return [half[i * CH : (i + 1) * CH] for half in (north, south) for i in range(3)]
+
+
+def edge_body(edge_ref, ahead_ref, behind_ref, out_ref):
+    n_near, n_far, n_cot, s_near, s_far, s_cot = row_halos(ahead_ref, behind_ref)
+    lane = lanes()
+    low = jnp.where(lane < 4, roll(s_near, 2), jnp.where(lane < 8, roll(s_far, 6), roll(s_cot, 10)))
+    high = jnp.where(
+        lane >= 124, roll(n_near, 126), jnp.where(lane >= 120, roll(n_far, 122), roll(n_cot, 118))
+    )
+    out_ref[pl.ds(0, 2 * CH), :] = edge_ref[...]
+    out_ref[pl.ds(2 * CH, CH), :] = jnp.where(lane < 64, low, high).astype(bf16)
 
 
 def strip(west_ref, east_ref, part):
     at = pl.ds(part * CH, CH)
     return jnp.where(lanes() % 4 < 2, west_ref[at, :].astype(f32), east_ref[at, :].astype(f32))
-
-
-def ring_body(rows_ref, west_ref, east_ref, ahead_ref, behind_ref):
-    rising = lax.axis_index("z") < lax.axis_size("z") // 2
-    lane = lanes()
-    s = strip(west_ref, east_ref, 0)
-    gs = strip(west_ref, east_ref, 1)
-    top = jnp.where(lane < 8, s, roll(gs, 8))
-    bottom = jnp.where(lane < 4, roll(s, 4), jnp.where(lane < 8, roll(s, 12), roll(gs, 12)))
-    half = pl.ds(0, TAPS)
-    first = rows_ref[pl.ds(0, TAPS), :]
-    last = rows_ref[pl.ds(TAPS, TAPS), :]
-    ahead_ref[half, :] = jnp.where(rising, last, first)
-    behind_ref[half, :] = jnp.where(rising, first, last)
-    corner = pl.ds(TAPS, CH)
-    ahead_ref[corner, :] = jnp.where(rising, bottom, top).astype(bf16)
-    behind_ref[corner, :] = jnp.where(rising, top, bottom).astype(bf16)
 
 
 def stack_taps(out_ref, at, own, halo, lane):
@@ -114,24 +119,18 @@
 
 def forward_body(
     fr_ref, gr_ref, edge_ref, west_ref, east_ref, ahead_ref, behind_ref, w_ref, w3_ref, wa_ref,
-    out_ref, delta_ref, dstrip_ref, grad_ref, xs, wide,
+    out_ref, delta_ref, dstrip_ref, grad_ref, xs,
 ):
     lat = lax.axis_index("lat")
     at_top = lat == 0
     at_bottom = lat == lax.axis_size("lat") - 1
-    rising = lax.axis_index("z") < lax.axis_size("z") // 2
     lane = lanes()
-    north = jnp.where(rising, ahead_ref[...], behind_ref[...]).astype(f32)
-    south = jnp.where(rising, behind_ref[...], ahead_ref[...]).astype(f32)
-    n_near, n_far, n_cot, n_corner = [north[i * CH : (i + 1) * CH] for i in range(4)]
-    s_near, s_far, s_cot, s_corner = [south[i * CH : (i + 1) * CH] for i in range(4)]
+    n_near, n_far, n_cot, s_near, s_far, s_cot = row_halos(ahead_ref, behind_ref)
 
     s = strip(west_ref, east_ref, 0)
-    beyond = jnp.where(
-        lane < 64, s_corner, jnp.where(lane >= 124, roll(n_corner, 124), roll(n_corner, 116))
-    )
     gs = strip(west_ref, east_ref, 1)
-    gbeyond = jnp.where(lane < 64, roll(s_corner, 120), roll(n_corner, 116))
+    beyond = strip(west_ref, east_ref, 2)
+    gbeyond = jnp.where(lane < 64, roll(beyond, 120), roll(beyond, 8))
 
     stack_taps(xs, 0, n_far, roll(beyond, -122), lane)
     stack_taps(xs, 1, n_near, roll(beyond, -126), lane)
@@ -148,9 +147,8 @@
         value, slope = gelu_parts(dot(weights, window))
         for k in range(2):
             cut = slice(k * COLS, (k + 1) * COLS)
-            wide[pl.ds(r + k, CH, stride=ROWS), :] = fr_ref[r + k].astype(f32) + value[:, cut]
+            out_ref[r + k] = (fr_ref[r + k].astype(f32) + value[:, cut]).astype(bf16)
             delta_ref[r + k + 1] = (gr_ref[r + k].astype(f32) * slope[:, cut]).astype(bf16)
-    out_ref[...] = wide[...].astype(bf16)
 
     def outer(inside, near, far, flip, cot, up):
         ends = (far, inside) if up else (inside, far)
@@ -162,13 +160,10 @@
     delta_ref[0] = outer(2, 1, 0, at_top, n_cot, True)
     delta_ref[ROWS + 1] = outer(ROWS + 1, ROWS + 2, ROWS + 3, at_bottom, s_cot, False)
 
-    own_beyond = jnp.where(
-        lane < 64,
-        jnp.where(lane < 4, roll(s_near, 2), roll(s_far, 6)),
-        jnp.where(lane >= 124, roll(n_near, 126), roll(n_far, 122)),
-    )
     halo = jnp.concatenate([s, beyond], 1)
-    own = jnp.concatenate([edge_ref[pl.ds(0, CH), :].astype(f32), own_beyond], 1)
+    own = jnp.concatenate(
+        [edge_ref[pl.ds(0, CH), :].astype(f32), edge_ref[pl.ds(2 * CH, CH), :].astype(f32)], 1
+    )
     wide_lane = lanes(2 * COLS)
     kind = wide_lane % 4
     columns = jnp.concatenate(
@@ -199,11 +194,17 @@
             grad_ref[:, 0, pl.ds(start, width)] = piece[j * count : (j + 1) * count]
 
 
+def restore_body(rows_ref, out_ref, wide):
+    for r in range(ROWS):
+        wide[pl.ds(r, CH, stride=ROWS), :] = rows_ref[r].astype(f32)
+    out_ref[...] = wide[...].astype(bf16)
+
+
 def grad_scale():
     return float(ROWS * COLS * lax.axis_size(EVERY)) ** (-0.5)
 
 
-def backward_body(delta_ref, dstrip_ref, gr_ref, wb_ref, wb3_ref, out_ref, xs, wide):
+def backward_body(after_ref, delta_ref, dstrip_ref, gr_ref, wb_ref, wb3_ref, out_ref, xs, wide):
     lat = lax.axis_index("lat")
     at_top = lat == 0
     at_bottom = lat == lax.axis_size("lat") - 1
@@ -271,33 +272,28 @@
     rows_shape = (ROWS, CH, COLS)
 
     flat_field, flat_cotangent = field.reshape(flat), cotangent.reshape(flat)
-    edge, rows = call(
+    ahead, behind, f_near, g_near = call(
         pack_body,
-        [((2 * CH, COLS), bf16), ((2 * TAPS, COLS), bf16)],
+        [((TAPS, COLS), bf16), ((TAPS, COLS), bf16), (flat, bf16), (flat, bf16)],
         (flat_field, flat_cotangent),
-        [
-            pltpu.VMEM(flat, f32),
-            pltpu.VMEM(flat, bf16),
-            pltpu.VMEM(flat, bf16),
-            pltpu.SemaphoreType.DMA((2, PIECES)),
-        ],
+        [pltpu.VMEM(flat, f32), pltpu.SemaphoreType.DMA((2, PIECES))],
         space=pl.ANY,
-        limit=56,
-    )
-    fr, gr = call(
-        turn_body, [(rows_shape, bf16)] * 2, (flat_field, flat_cotangent), [pltpu.VMEM(flat, f32)]
-    )
-    right = [(i, (i + 1) % lon_count) for i in range(lon_count)]
-    left = [(b, a) for a, b in right]
-    west = lax.ppermute(edge, LON, right)
-    east = lax.ppermute(edge, LON, left)
-
-    ahead, behind = call(
-        ring_body, [((4 * CH, COLS), bf16), ((4 * CH, COLS), bf16)], (rows, west, east)
+        limit=52.5,
     )
     ring = ring_pairs(lat_count, lon_count)
     ahead = lax.ppermute(ahead, EVERY, ring)
     behind = lax.ppermute(behind, EVERY, [(b, a) for a, b in ring])
+    fr, gr, edge = call(
+        turn_body,
+        [(rows_shape, bf16), (rows_shape, bf16), ((2 * CH, COLS), bf16)],
+        (f_near, g_near),
+        [pltpu.VMEM(flat, f32)],
+    )
+
+    (edge,) = call(edge_body, [((TAPS, COLS), bf16)], (edge, ahead, behind))
+    right = [(i, (i + 1) % lon_count) for i in range(lon_count)]
+    west = lax.ppermute(edge, LON, right)
+    east = lax.ppermute(edge, LON, [(b, a) for a, b in right])
 
     w3 = jnp.transpose(kernel, (0, 2, 1, 3)).reshape(3, CH, TAPS)
     w = jnp.transpose(kernel, (2, 0, 1, 3)).reshape(CH, 3 * TAPS)
@@ -306,16 +302,16 @@
     wb = jnp.transpose(turned, (3, 0, 1, 2)).reshape(CH, 3 * TAPS)
 
     conv_flops = 2 * 9 * CH * CH * ROWS * COLS
-    output, delta, dstrip, grad = call(
+    out_rows, delta, dstrip, grad = call(
         forward_body,
         [
-            (flat, bf16),
+            (rows_shape, bf16),
             ((ROWS + 2, CH, COLS), bf16),
             ((CH, 2 * COLS), bf16),
             ((plane, 1, 9 * CH * CH // plane), f32),
         ],
         (fr, gr, edge, west, east, ahead, behind, w, w3, w3.reshape(TAPS, TAPS)),
-        [pltpu.VMEM((ROWS + 4, TAPS, COLS), bf16), pltpu.VMEM(flat, f32)],
+        [pltpu.VMEM((ROWS + 4, TAPS, COLS), bf16)],
         2 * conv_flops,
     )
 
@@ -323,11 +319,12 @@
         return call(fold_body, [((count,) + parts.shape[1:], f32)], (parts,))[0]
 
     parts = lax.all_to_all(grad, PLANE, 0, 0)
+    (output,) = call(restore_body, [(flat, bf16)], (out_rows,), [pltpu.VMEM(flat, f32)])
     parts = lax.all_to_all(spread(parts, lax.axis_size("z")), "z", 0, 0)
     (grad_input,) = call(
         backward_body,
         [(flat, bf16)],
-        (delta, dstrip, gr, wb, wb3),
+        (parts, delta, dstrip, gr, wb, wb3),
         [pltpu.VMEM((ROWS + 2, TAPS, COLS), bf16), pltpu.VMEM(flat, f32)],
         conv_flops,
     )

time: 71.9 us -> 67.6 us (0.940)
  waiting for transfers between devices: 7.46 us -> 4.26 us
  blocking collectives: 30.5 us -> 32.6 us
  starting transfers between devices: 17.6 us -> 15.7 us
  local copies, waits for them, and re-layouts: 2.05 us -> 1.15 us
    all_to_all x1, blocking collectives: 18.9 us -> 21.5 us  [on_device(): parts = lax.all_to_all(grad, PLANE, 0, 0)]
    all_to_all x1, waiting for transfers between devices: 4.54 us -> 2.64 us  [on_device(): parts = lax.all_to_all(spread(parts, plane), PLANE, 0, 0)]
    ppermute x1, starting transfers between devices: 5.38 us -> 3.65 us  [on_device(): east = lax.ppermute(edge, LON, [(b, a) for a, b in right])]
    ppermute x1, waiting for transfers between devices: 1.43 us -> 0.51 us  [on_device(): west = lax.ppermute(edge, LON, right)]
    unnamed x10 -> x2, local copies, waits for them, and re-layouts: 0.91 us -> 0.01 us
    ppermute x1, starting transfers between devices: 3.82 us -> 2.99 us  [on_device(): west = lax.ppermute(edge, LON, right)]
    ppermute x1, starting transfers between devices: 0.01 us -> 0.73 us  [on_device(): behind = lax.ppermute(behind, EVERY, [(b, a) for a, b in ring])]
    pallas_call x8 -> x9, Pallas kernels: 13.2 us -> 12.9 us  [call(): pl.pallas_call(body, out_shape=outs, in_specs=[pl.BlockSpec(memory_space=...]
  transfers between devices with their start and end apart: 5 -> 5, of which waited for: 3 -> 3; matrix products, arithmetic and copies ran while one was open for 2% -> 2% of each run, Pallas kernels for 6% -> 9%
where the time goes in v3:
time: 67.6 us; the launch traced here: 67.4 us
  blocking collectives  32.6 us (48%)
  starting transfers between devices  15.7 us (23%)
  Pallas kernels  12.9 us (19%)
  waiting for transfers between devices  4.26 us (6%)
  local copies, waits for them, and re-layouts  1.15 us (2%)
  between operations  0.71 us (1%)
    all_to_all x1, blocking collectives, on_device(): parts = lax.all_to_all(grad, PLANE, 0, 0)  21.5 us
    pallas_call x9, Pallas kernels, call(): pl.pallas_call(body, out_shape=outs, in_specs=[pl.BlockSpec(memory_space=...  12.9 us
    all_to_all x1, blocking collectives, on_device(): parts = lax.all_to_all(spread(parts, lax.axis_size('z')), 'z', 0, 0)  11.1 us
    all_to_all x1, starting transfers between devices, on_device(): parts = lax.all_to_all(spread(parts, plane), PLANE, 0, 0)  5.68 us
    ppermute x1, starting transfers between devices, on_device(): east = lax.ppermute(edge, LON, [(b, a) for a, b in right])  3.65 us
    ppermute x1, starting transfers between devices, on_device(): west = lax.ppermute(edge, LON, right)  2.99 us
    ppermute x1, starting transfers between devices, on_device(): ahead = lax.ppermute(ahead, EVERY, ring)  2.68 us
    all_to_all x1, waiting for transfers between devices, on_device(): parts = lax.all_to_all(spread(parts, plane), PLANE, 0, 0)  2.64 us
  transfers between devices with their start and end apart: 5, of which 3 were waited for; matrix products, arithmetic and copies ran while one was open for 2% of the time, Pallas kernels for 9%

profile of v3, /device:TPU:1, one launch (start us, length us, event | category | flops | bytes accessed | tf_op | source)
XLA Modules:
  0.0 67.4 jit_solution(14173585196501082770)
XLA Ops:
  0.6 1.4 %shard_map.58 = (bf16[192,128]{1,0:T(8,128)(2,1)S(1)}, bf16[192,128]{1,0:T(8,128)(2,1)S(1)}, bf16[2048,128]{1,0:T(8,128)(2,1)S(1)}, bf16[2048,128]{1,0:T(8,128)(2,1)S(1)}) custom-call(bf16[2048,128]{1,0:T(8,128)(2,1)} %bitcast.23, bf16[2048,128]{1,0:T(8,128)(2,1)} %bitcast.24), custom_call_target="tpu_custom_call" | custom-call | bytes 2195456 | tf_op jit(solution)/shard_map/pallas_call | solution.py:39
  2.0 2.7 %collective-permute-start = (bf16[192,128]{1,0:T(8,128)(2,1)S(1)}, bf16[192,128]{1,0:T(8,128)(2,1)S(1)}, u32[]{:S(2)}, u32[]{:S(2)}) collective-permute-start(bf16[192,128]{1,0:T(8,128)(2,1)S(1)} %get-tuple-element.19), channel_id=1, source_target_pairs={{0,16},{1,17},{2,18},{3,19},{4,20},{5,21},{6,22},{7,23},{8,0},{9,1... | collective-permute-start | bytes 147464 | tf_op jit(solution)/shard_map/ppermute | solution.py:284
  4.7 0.7 %collective-permute-start.1 = (bf16[192,128]{1,0:T(8,128)(2,1)S(1)}, bf16[192,128]{1,0:T(8,128)(2,1)S(1)}, u32[]{:S(2)}, u32[]{:S(2)}) collective-permute-start(bf16[192,128]{1,0:T(8,128)(2,1)S(1)} %get-tuple-element.20), channel_id=1, source_target_pairs={{16,0},{17,1},{18,2},{19,3},{20,4},{21,5},{22,6},{23,7},{0,8},{1,9... | collective-permute-start | bytes 147464 | tf_op jit(solution)/shard_map/ppermute | solution.py:285
  5.5 1.6 %shard_map.59 = (bf16[32,64,128]{2,1,0:T(8,128)(2,1)S(1)}, bf16[32,64,128]{2,1,0:T(8,128)(2,1)S(1)}, bf16[128,128]{1,0:T(8,128)(2,1)S(1)}) custom-call(bf16[2048,128]{1,0:T(8,128)(2,1)S(1)} %get-tuple-element.14.f_ref, bf16[2048,128]{1,0:T(8,128)(2,1)S(1)} %get-tuple-element.15.g_ref), custom_call_target="tpu_custom_call" | custom-call | bytes 2129920 | tf_op jit(solution)/shard_map/pallas_call | solution.py:39
  7.1 0.0 copy-start
  7.1 0.0 collective-permute-done.ahead_ref
  7.1 1.1 %collective-permute-done.1.behind_ref = bf16[192,128]{1,0:T(8,128)(2,1)S(1)} collective-permute-done((bf16[192,128]{1,0:T(8,128)(2,1)S(1)}, bf16[192,128]{1,0:T(8,128)(2,1)S(1)}, u32[]{:S(2)}, u32[]{:S(2)}) %collective-permute-start.1) | collective-permute-done | bytes 49184 | tf_op jit(solution)/shard_map/ppermute | solution.py:285
  8.2 0.1 shard_map.60.edge_ref
  8.3 3.0 %collective-permute-start.2 = (bf16[192,128]{1,0:T(8,128)(2,1)S(1)}, bf16[192,128]{1,0:T(8,128)(2,1)S(1)}, u32[]{:S(2)}, u32[]{:S(2)}) collective-permute-start(bf16[192,128]{1,0:T(8,128)(2,1)S(1)} %shard_map.60.edge_ref), channel_id=1, source_target_pairs={{0,1},{1,2},{2,3},{3,4},{4,5},{5,6},{6,7},{7,8},{8,9},{9,10},{10,1... | collective-permute-start | bytes 147464 | tf_op jit(solution)/shard_map/ppermute | solution.py:295
  11.3 3.6 %collective-permute-start.3 = (bf16[192,128]{1,0:T(8,128)(2,1)S(1)}, bf16[192,128]{1,0:T(8,128)(2,1)S(1)}, u32[]{:S(2)}, u32[]{:S(2)}) collective-permute-start(bf16[192,128]{1,0:T(8,128)(2,1)S(1)} %shard_map.60.edge_ref), channel_id=1, source_target_pairs={{1,0},{2,1},{3,2},{4,3},{5,4},{6,5},{7,6},{8,7},{9,8},{10,9},{11,1... | collective-permute-start | bytes 147464 | tf_op jit(solution)/shard_map/ppermute | solution.py:296
  15.0 0.0 copy-done
  15.0 0.1 copy.13
  15.1 0.1 copy.12
  15.3 0.2 reshape_reshape.3.wa_ref
  15.4 0.1 copy.15.w3_ref
  15.6 0.1 copy.11
  15.7 0.1 copy.14.w_ref
  15.9 0.5 collective-permute-done.2.west_ref
  16.4 0.0 collective-permute-done.3.east_ref
  16.4 3.3 %shard_map.61 = (bf16[32,64,128]{2,1,0:T(8,128)(2,1)S(1)}, bf16[34,64,128]{2,1,0:T(8,128)(2,1)S(1)}, bf16[64,256]{1,0:T(8,128)(2,1)S(1)}, f32[32,1,1152]{2,1,0:T(1,128)S(1)}) custom-call(bf16[32,64,128]{2,1,0:T(8,128)(2,1)S(1)} %get-tuple-element.16.fr_ref, bf16[32,64,128]{2,1,0:T(8,128)(2,1)S(1)} %get-tuple-element.17.gr_ref, ...), custom_call_target="tpu_custom_call" | custom-call | flops 603979776 | bytes 2777088 | tf_op jit(solution)/shard_map/pallas_call | solution.py:39
  19.7 21.5 %all_to_all.15.parts_ref = f32[32,1,1152]{2,1,0:T(1,128)S(1)} all-to-all(f32[32,1,1152]{2,1,0:T(1,128)S(1)} %get-tuple-element.22), channel_id=1, replica_groups=mesh['lat'=16,'z'=8,'side'=2] {'lat','side'}, dimensions={0} | all-to-all | bytes 294912 | tf_op jit(solution)/shard_map/all_to_all | solution.py:321
  41.2 0.1 shard_map.63
  41.3 11.1 %all_to_all.16.after_ref.parts_ref = f32[8,1,1152]{2,1,0:T(1,128)S(1)} all-to-all(f32[8,1,1152]{2,1,0:T(1,128)S(1)} %shard_map.63), channel_id=1, replica_groups=mesh['lat'=16,'z'=8,'side'=2] {'z'}, dimensions={0} | all-to-all | bytes 73728 | tf_op jit(solution)/shard_map/all_to_all | solution.py:323
  52.4 0.7 %shard_map.65 = f32[32,1,1152]{2,1,0:T(1,128)} custom-call(f32[8,1,1152]{2,1,0:T(1,128)S(1)} %all_to_all.16.after_ref.parts_ref), custom_call_target="tpu_custom_call" | custom-call | bytes 184320 | tf_op jit(solution)/shard_map/pallas_call | solution.py:39
  53.1 5.7 %all-to-all-start.2 = ((f32[32,1,1152]{2,1,0:T(1,128)}), f32[32,1,1152]{2,1,0:T(1,128)S(1)}, u32[]{:S(2)}, u32[]{:S(2)}) async-start(f32[32,1,1152]{2,1,0:T(1,128)} %shard_map.65), calls=%async_computation.2 | async-start | bytes 294912 | tf_op jit(solution)/shard_map/all_to_all | solution.py:331
  58.9 0.1 copy.17.wb3_ref
  59.0 0.1 copy.16.wb_ref
  59.1 1.9 %shard_map.62 = bf16[2048,128]{1,0:T(8,128)(2,1)} custom-call(bf16[32,64,128]{2,1,0:T(8,128)(2,1)S(1)} %get-tuple-element.21.rows_ref), custom_call_target="tpu_custom_call" | custom-call | bytes 1048576 | tf_op jit(solution)/shard_map/pallas_call | solution.py:39
  61.0 2.9 %shard_map.64 = bf16[2048,128]{1,0:T(8,128)(2,1)} custom-call(f32[8,1,1152]{2,1,0:T(1,128)S(1)} %all_to_all.16.after_ref.parts_ref, bf16[34,64,128]{2,1,0:T(8,128)(2,1)S(1)} %get-tuple-element.23.delta_ref, bf16[64,256]{1,0:T(8,128)(2,1)S(1)} %get-tuple-element.24.dstrip_ref, bf16[32,64,128]{2,1,0:T(8,128)(2,1)S(1)} %get-tuple-element.17.gr_ref, ...), custom_call_target="tpu_custom_call" | custom-call | flops 301989888 | bytes 1822720 | tf_op jit(solution)/shard_map/pallas_call | solution.py:39
  63.9 2.6 %all-to-all-done.2.parts_ref = f32[32,1,1152]{2,1,0:T(1,128)S(1)} async-done(((f32[32,1,1152]{2,1,0:T(1,128)}), f32[32,1,1152]{2,1,0:T(1,128)S(1)}, u32[]{:S(2)}, u32[]{:S(2)}) %all-to-all-start.2) | async-done | bytes 147488 | tf_op jit(solution)/shard_map/all_to_all | solution.py:331
  66.5 0.9 %shard_map.66 = f32[9,64,64]{2,1,0:T(8,128)} custom-call(f32[32,1,1152]{2,1,0:T(1,128)S(1)} %all-to-all-done.2.parts_ref), custom_call_target="tpu_custom_call" | custom-call | bytes 294912 | tf_op jit(solution)/shard_map/pallas_call | solution.py:39
  (1 shorter events, 0.0 us)
Async XLA Ops:
  2.0 5.1 %collective-permute-start = (bf16[192,128]{1,0:T(8,128)(2,1)S(1)}, bf16[192,128]{1,0:T(8,128)(2,1)S(1)}, u32[]{:S(2)}, u32[]{:S(2)}) collective-permute-start(bf16[192,128]{1,0:T(8,128)(2,1)S(1)} %get-tuple-element.19), channel_id=1, source_target_pairs={{0,16},{1,17},{2,18},{3,19},{4,20},{5,21},{6,22},{7,23},{8,0},{9,1... | collective-permute-start | bytes 147464 | tf_op jit(solution)/shard_map/ppermute | solution.py:284
  4.7 3.5 %collective-permute-start.1 = (bf16[192,128]{1,0:T(8,128)(2,1)S(1)}, bf16[192,128]{1,0:T(8,128)(2,1)S(1)}, u32[]{:S(2)}, u32[]{:S(2)}) collective-permute-start(bf16[192,128]{1,0:T(8,128)(2,1)S(1)} %get-tuple-element.20), channel_id=1, source_target_pairs={{16,0},{17,1},{18,2},{19,3},{20,4},{21,5},{22,6},{23,7},{0,8},{1,9... | collective-permute-start | bytes 147464 | tf_op jit(solution)/shard_map/ppermute | solution.py:285
  7.1 7.9 %copy-start = (bf16[3,3,64,64]{3,2,1,0:T(8,128)(2,1)S(1)}, bf16[3,3,64,64]{3,2,1,0:T(8,128)(2,1)}, u32[]{:S(2)}) copy-start(bf16[3,3,64,64]{3,2,1,0:T(8,128)(2,1)} %param.4) | copy-start | bytes 221188
  8.3 8.0 %collective-permute-start.2 = (bf16[192,128]{1,0:T(8,128)(2,1)S(1)}, bf16[192,128]{1,0:T(8,128)(2,1)S(1)}, u32[]{:S(2)}, u32[]{:S(2)}) collective-permute-start(bf16[192,128]{1,0:T(8,128)(2,1)S(1)} %shard_map.60.edge_ref), channel_id=1, source_target_pairs={{0,1},{1,2},{2,3},{3,4},{4,5},{5,6},{6,7},{7,8},{8,9},{9,10},{10,1... | collective-permute-start | bytes 147464 | tf_op jit(solution)/shard_map/ppermute | solution.py:295
  11.3 5.0 %collective-permute-start.3 = (bf16[192,128]{1,0:T(8,128)(2,1)S(1)}, bf16[192,128]{1,0:T(8,128)(2,1)S(1)}, u32[]{:S(2)}, u32[]{:S(2)}) collective-permute-start(bf16[192,128]{1,0:T(8,128)(2,1)S(1)} %shard_map.60.edge_ref), channel_id=1, source_target_pairs={{1,0},{2,1},{3,2},{4,3},{5,4},{6,5},{7,6},{8,7},{9,8},{10,9},{11,1... | collective-permute-start | bytes 147464 | tf_op jit(solution)/shard_map/ppermute | solution.py:296
  53.1 13.4 %all-to-all-start.2 = ((f32[32,1,1152]{2,1,0:T(1,128)}), f32[32,1,1152]{2,1,0:T(1,128)S(1)}, u32[]{:S(2)}, u32[]{:S(2)}) async-start(f32[32,1,1152]{2,1,0:T(1,128)} %shard_map.65), calls=%async_computation.2 | async-start | bytes 294912 | tf_op jit(solution)/shard_map/all_to_all | solution.py:331

commit v4 on v3

--- a/solution.py
+++ b/solution.py
@@ -47,7 +47,7 @@
     )(*args)
 
 
-def pack_body(f_hbm, g_hbm, ahead_ref, behind_ref, f_ref, g_ref, wide, sems):
+def pack_body(f_hbm, g_hbm, outer_ref, inner_ref, f_ref, g_ref, wide, sems):
     part = CH * ROWS // PIECES
     copies = [
         [
@@ -58,7 +58,7 @@
     ]
     for copy in copies[0] + copies[1]:
         copy.start()
-    rising = lax.axis_index("z") < lax.axis_size("z") // 2
+    even = lax.axis_index("lat") % 2 == 0
     end = ROWS - 1
     slots = (((0, 0, end), (1, 1, end - 1)), ((2, 0, end),))
     for at, src in enumerate((f_ref, g_ref)):
@@ -68,8 +68,8 @@
         for slot, low, high in slots[at]:
             first = wide[pl.ds(low, CH, stride=ROWS), :]
             last = wide[pl.ds(high, CH, stride=ROWS), :]
-            ahead_ref[pl.ds(slot * CH, CH), :] = jnp.where(rising, last, first).astype(bf16)
-            behind_ref[pl.ds(slot * CH, CH), :] = jnp.where(rising, first, last).astype(bf16)
+            outer_ref[pl.ds(slot * CH, CH), :] = jnp.where(even, first, last).astype(bf16)
+            inner_ref[pl.ds(slot * CH, CH), :] = jnp.where(even, last, first).astype(bf16)
 
 
 def turn_body(f_ref, g_ref, fr_ref, gr_ref, edge_ref, wide):
@@ -84,15 +84,15 @@
         edge_ref[pl.ds(at * CH, CH), :] = edge.astype(bf16)
 
 
-def row_halos(ahead_ref, behind_ref):
-    rising = lax.axis_index("z") < lax.axis_size("z") // 2
-    north = jnp.where(rising, ahead_ref[...], behind_ref[...]).astype(f32)
-    south = jnp.where(rising, behind_ref[...], ahead_ref[...]).astype(f32)
+def row_halos(outer_ref, inner_ref):
+    even = lax.axis_index("lat") % 2 == 0
+    north = jnp.where(even, outer_ref[...], inner_ref[...]).astype(f32)
+    south = jnp.where(even, inner_ref[...], outer_ref[...]).astype(f32)
     return [half[i * CH : (i + 1) * CH] for half in (north, south) for i in range(3)]
 
 
-def edge_body(edge_ref, ahead_ref, behind_ref, out_ref):
-    n_near, n_far, n_cot, s_near, s_far, s_cot = row_halos(ahead_ref, behind_ref)
+def edge_body(edge_ref, outer_ref, inner_ref, out_ref):
+    n_near, n_far, n_cot, s_near, s_far, s_cot = row_halos(outer_ref, inner_ref)
     lane = lanes()
     low = jnp.where(lane < 4, roll(s_near, 2), jnp.where(lane < 8, roll(s_far, 6), roll(s_cot, 10)))
     high = jnp.where(
@@ -102,9 +102,12 @@
     out_ref[pl.ds(2 * CH, CH), :] = jnp.where(lane < 64, low, high).astype(bf16)
 
 
-def strip(west_ref, east_ref, part):
+def strip(near_ref, far_ref, part):
     at = pl.ds(part * CH, CH)
-    return jnp.where(lanes() % 4 < 2, west_ref[at, :].astype(f32), east_ref[at, :].astype(f32))
+    near = near_ref[at, :].astype(f32)
+    far = far_ref[at, :].astype(f32)
+    even = lax.axis_index("side") == 0
+    return jnp.where(lanes() % 4 < 2, jnp.where(even, far, near), jnp.where(even, near, far))
 
 
 def stack_taps(out_ref, at, own, halo, lane):
@@ -118,18 +121,18 @@
 
 
 def forward_body(
-    fr_ref, gr_ref, edge_ref, west_ref, east_ref, ahead_ref, behind_ref, w_ref, w3_ref, wa_ref,
+    fr_ref, gr_ref, edge_ref, near_ref, far_ref, outer_ref, inner_ref, w_ref, w3_ref, wa_ref,
     out_ref, delta_ref, dstrip_ref, grad_ref, xs,
 ):
     lat = lax.axis_index("lat")
     at_top = lat == 0
     at_bottom = lat == lax.axis_size("lat") - 1
     lane = lanes()
-    n_near, n_far, n_cot, s_near, s_far, s_cot = row_halos(ahead_ref, behind_ref)
-
-    s = strip(west_ref, east_ref, 0)
-    gs = strip(west_ref, east_ref, 1)
-    beyond = strip(west_ref, east_ref, 2)
+    n_near, n_far, n_cot, s_near, s_far, s_cot = row_halos(outer_ref, inner_ref)
+
+    s = strip(near_ref, far_ref, 0)
+    gs = strip(near_ref, far_ref, 1)
+    beyond = strip(near_ref, far_ref, 2)
     gbeyond = jnp.where(lane < 64, roll(beyond, 120), roll(beyond, 8))
 
     stack_taps(xs, 0, n_far, roll(beyond, -122), lane)
@@ -251,16 +254,16 @@
             out_ref[tap, pl.ds(j * count, count), :] = parts_ref[:, 0, pl.ds(start, CH)]
 
 
-def ring_pairs(lat_count, lon_count):
+def outer_pairs(lat_count, lon_count):
     half = lon_count // 2
     pairs = []
     for l in range(lat_count):
         for m in range(lon_count):
-            if m < half:
-                to = (l + 1, m) if l + 1 < lat_count else (l, m + half)
+            to = l - 1 if l % 2 == 0 else l + 1
+            if 0 <= to < lat_count:
+                pairs.append((l * lon_count + m, to * lon_count + m))
             else:
-                to = (l - 1, m) if l > 0 else (l, m - half)
-            pairs.append((l * lon_count + m, to[0] * lon_count + to[1]))
+                pairs.append((l * lon_count + m, l * lon_count + (m + half) % lon_count))
     return pairs
 
 
@@ -272,7 +275,7 @@
     rows_shape = (ROWS, CH, COLS)
 
     flat_field, flat_cotangent = field.reshape(flat), cotangent.reshape(flat)
-    ahead, behind, f_near, g_near = call(
+    outer, inner, f_near, g_near = call(
         pack_body,
         [((TAPS, COLS), bf16), ((TAPS, COLS), bf16), (flat, bf16), (flat, bf16)],
         (flat_field, flat_cotangent),
@@ -280,9 +283,8 @@
         space=pl.ANY,
         limit=52.5,
     )
-    ring = ring_pairs(lat_count, lon_count)
-    ahead = lax.ppermute(ahead, EVERY, ring)
-    behind = lax.ppermute(behind, EVERY, [(b, a) for a, b in ring])
+    outer = lax.ppermute(outer, EVERY, outer_pairs(lat_count, lon_count))
+    inner = lax.ppermute(inner, "lat", [(i, i ^ 1) for i in range(lat_count)])
     fr, gr, edge = call(
         turn_body,
         [(rows_shape, bf16), (rows_shape, bf16), ((2 * CH, COLS), bf16)],
@@ -290,10 +292,10 @@
         [pltpu.VMEM(flat, f32)],
     )
 
-    (edge,) = call(edge_body, [((TAPS, COLS), bf16)], (edge, ahead, behind))
-    right = [(i, (i + 1) % lon_count) for i in range(lon_count)]
-    west = lax.ppermute(edge, LON, right)
-    east = lax.ppermute(edge, LON, [(b, a) for a, b in right])
+    (edge,) = call(edge_body, [((TAPS, COLS), bf16)], (edge, outer, inner))
+    swaps = [(i, (i + 1 if i % 2 else i - 1) % lon_count) for i in range(lon_count)]
+    far = lax.ppermute(edge, LON, swaps)
+    near = lax.ppermute(edge, "side", [(0, 1), (1, 0)])
 
     w3 = jnp.transpose(kernel, (0, 2, 1, 3)).reshape(3, CH, TAPS)
     w = jnp.transpose(kernel, (2, 0, 1, 3)).reshape(CH, 3 * TAPS)
@@ -310,7 +312,7 @@
             ((CH, 2 * COLS), bf16),
             ((plane, 1, 9 * CH * CH // plane), f32),
         ],
-        (fr, gr, edge, west, east, ahead, behind, w, w3, w3.reshape(TAPS, TAPS)),
+        (fr, gr, edge, near, far, outer, inner, w, w3, w3.reshape(TAPS, TAPS)),
         [pltpu.VMEM((ROWS + 4, TAPS, COLS), bf16)],
         2 * conv_flops,
     )

time: 67.6 us -> 66.7 us (0.987)
  blocking collectives: 32.6 us -> 25.8 us
  waiting for transfers between devices: 4.26 us -> 8.32 us
  starting transfers between devices: 15.7 us -> 17.5 us
    all_to_all x1, blocking collectives: 21.5 us -> 12.7 us  [on_device(): parts = lax.all_to_all(grad, PLANE, 0, 0)]
    ppermute x4, waiting for transfers between devices: 1.62 us -> 5.67 us  [the longest x1 5.02 us: on_device(): far = lax.ppermute(edge, LON, swaps)]
    all_to_all x1, blocking collectives: 11.1 us -> 13.1 us  [on_device(): parts = lax.all_to_all(spread(parts, lax.axis_size('z')), 'z', 0, 0)]
    ppermute x4, starting transfers between devices: 10.1 us -> 11.8 us  [the longest x1 6.09 us: on_device(): inner = lax.ppermute(inner, 'lat', [(i, i ^ 1) for i in range(lat_count)])]
  transfers between devices with their start and end apart: 5 -> 5, of which waited for: 3 -> 3; matrix products, arithmetic and copies ran while one was open for 2% -> 2% of each run, Pallas kernels for 9% -> 10%
where the time goes in v4:
time: 66.7 us; the launch traced here: 66.4 us
  blocking collectives  25.8 us (39%)
  starting transfers between devices  17.5 us (26%)
  Pallas kernels  12.9 us (19%)
  waiting for transfers between devices  8.32 us (12%)
  local copies, waits for them, and re-layouts  1.15 us (2%)
  between operations  0.72 us (1%)
    all_to_all x1, blocking collectives, on_device(): parts = lax.all_to_all(spread(parts, lax.axis_size('z')), 'z', 0, 0)  13.1 us
    pallas_call x9, Pallas kernels, call(): pl.pallas_call(body, out_shape=outs, in_specs=[pl.BlockSpec(memory_space=...  12.9 us
    all_to_all x1, blocking collectives, on_device(): parts = lax.all_to_all(grad, PLANE, 0, 0)  12.7 us
    ppermute x1, starting transfers between devices, on_device(): inner = lax.ppermute(inner, 'lat', [(i, i ^ 1) for i in range(lat_count)])  6.09 us
    all_to_all x1, starting transfers between devices, on_device(): parts = lax.all_to_all(spread(parts, plane), PLANE, 0, 0)  5.67 us
    ppermute x1, waiting for transfers between devices, on_device(): far = lax.ppermute(edge, LON, swaps)  5.02 us
    ppermute x1, starting transfers between devices, on_device(): near = lax.ppermute(edge, 'side', [(0, 1), (1, 0)])  3 us
    ppermute x1, starting transfers between devices, on_device(): outer = lax.ppermute(outer, EVERY, outer_pairs(lat_count, lon_count))  2.69 us
  transfers between devices with their start and end apart: 5, of which 3 were waited for; matrix products, arithmetic and copies ran while one was open for 2% of the time, Pallas kernels for 10%

profile of v4, /device:TPU:1, one launch (start us, length us, event | category | flops | bytes accessed | tf_op | source)
XLA Modules:
  0.0 66.4 jit_solution(3263080034480783534)
XLA Ops:
  0.6 1.4 %shard_map.58 = (bf16[192,128]{1,0:T(8,128)(2,1)S(1)}, bf16[192,128]{1,0:T(8,128)(2,1)S(1)}, bf16[2048,128]{1,0:T(8,128)(2,1)S(1)}, bf16[2048,128]{1,0:T(8,128)(2,1)S(1)}) custom-call(bf16[2048,128]{1,0:T(8,128)(2,1)} %bitcast.23, bf16[2048,128]{1,0:T(8,128)(2,1)} %bitcast.24), custom_call_target="tpu_custom_call" | custom-call | bytes 2195456 | tf_op jit(solution)/shard_map/pallas_call | solution.py:39
  2.0 2.7 %collective-permute-start = (bf16[192,128]{1,0:T(8,128)(2,1)S(1)}, bf16[192,128]{1,0:T(8,128)(2,1)S(1)}, u32[]{:S(2)}, u32[]{:S(2)}) collective-permute-start(bf16[192,128]{1,0:T(8,128)(2,1)S(1)} %get-tuple-element.19), channel_id=1, source_target_pairs={{0,8},{1,9},{2,10},{3,11},{4,12},{5,13},{6,14},{7,15},{8,0},{9,1},... | collective-permute-start | bytes 147464 | tf_op jit(solution)/shard_map/ppermute | solution.py:286
  4.7 6.1 %collective-permute-start.1 = (bf16[192,128]{1,0:T(8,128)(2,1)S(1)}, bf16[192,128]{1,0:T(8,128)(2,1)S(1)}, u32[]{:S(2)}, u32[]{:S(2)}) collective-permute-start(bf16[192,128]{1,0:T(8,128)(2,1)S(1)} %get-tuple-element.20), channel_id=1, source_target_pairs={{0,16},{16,0},{32,48},{48,32},{64,80},{80,64},{96,112},{112,96},{1... | collective-permute-start | bytes 147464 | tf_op jit(solution)/shard_map/ppermute | solution.py:287
  10.8 1.6 %shard_map.59 = (bf16[32,64,128]{2,1,0:T(8,128)(2,1)S(1)}, bf16[32,64,128]{2,1,0:T(8,128)(2,1)S(1)}, bf16[128,128]{1,0:T(8,128)(2,1)S(1)}) custom-call(bf16[2048,128]{1,0:T(8,128)(2,1)S(1)} %get-tuple-element.14.f_ref, bf16[2048,128]{1,0:T(8,128)(2,1)S(1)} %get-tuple-element.15.g_ref), custom_call_target="tpu_custom_call" | custom-call | bytes 2129920 | tf_op jit(solution)/shard_map/pallas_call | solution.py:39
  12.5 0.0 copy-start
  12.5 0.0 collective-permute-done.outer_ref
  12.5 0.0 collective-permute-done.1.inner_ref
  12.5 0.1 shard_map.60.edge_ref
  12.6 3.0 %collective-permute-start.2 = (bf16[192,128]{1,0:T(8,128)(2,1)S(1)}, bf16[192,128]{1,0:T(8,128)(2,1)S(1)}, u32[]{:S(2)}, u32[]{:S(2)}) collective-permute-start(bf16[192,128]{1,0:T(8,128)(2,1)S(1)} %shard_map.60.edge_ref), channel_id=1, source_target_pairs={{0,1},{1,0},{2,3},{3,2},{4,5},{5,4},{6,7},{7,6},{8,9},{9,8},{10,11... | collective-permute-start | bytes 147464 | tf_op jit(solution)/shard_map/ppermute | solution.py:298
  15.6 0.0 collective-permute-start.3
  15.6 0.0 copy-done
  15.6 0.1 copy.13
  15.8 0.1 copy.12
  15.9 0.2 reshape_reshape.3.wa_ref
  16.1 0.1 copy.15.w3_ref
  16.2 0.1 copy.11
  16.4 0.1 copy.14.w_ref
  16.5 0.6 collective-permute-done.2.near_ref
  17.2 5.0 %collective-permute-done.3.far_ref = bf16[192,128]{1,0:T(8,128)(2,1)S(1)} collective-permute-done((bf16[192,128]{1,0:T(8,128)(2,1)S(1)}, bf16[192,128]{1,0:T(8,128)(2,1)S(1)}, u32[]{:S(2)}, u32[]{:S(2)}) %collective-permute-start.3) | collective-permute-done | bytes 49184 | tf_op jit(solution)/shard_map/ppermute | solution.py:297
  22.2 3.4 %shard_map.61 = (bf16[32,64,128]{2,1,0:T(8,128)(2,1)S(1)}, bf16[34,64,128]{2,1,0:T(8,128)(2,1)S(1)}, bf16[64,256]{1,0:T(8,128)(2,1)S(1)}, f32[32,1,1152]{2,1,0:T(1,128)S(1)}) custom-call(bf16[32,64,128]{2,1,0:T(8,128)(2,1)S(1)} %get-tuple-element.16.fr_ref, bf16[32,64,128]{2,1,0:T(8,128)(2,1)S(1)} %get-tuple-element.17.gr_ref, ...), custom_call_target="tpu_custom_call" | custom-call | flops 603979776 | bytes 2777088 | tf_op jit(solution)/shard_map/pallas_call | solution.py:39
  25.5 12.7 %all_to_all.15.parts_ref = f32[32,1,1152]{2,1,0:T(1,128)S(1)} all-to-all(f32[32,1,1152]{2,1,0:T(1,128)S(1)} %get-tuple-element.22), channel_id=1, replica_groups=mesh['lat'=16,'z'=8,'side'=2] {'lat','side'}, dimensions={0} | all-to-all | bytes 294912 | tf_op jit(solution)/shard_map/all_to_all | solution.py:323
  38.3 0.1 shard_map.63
  38.4 13.1 %all_to_all.16.after_ref.parts_ref = f32[8,1,1152]{2,1,0:T(1,128)S(1)} all-to-all(f32[8,1,1152]{2,1,0:T(1,128)S(1)} %shard_map.63), channel_id=1, replica_groups=mesh['lat'=16,'z'=8,'side'=2] {'z'}, dimensions={0} | all-to-all | bytes 73728 | tf_op jit(solution)/shard_map/all_to_all | solution.py:325
  51.5 0.7 %shard_map.65 = f32[32,1,1152]{2,1,0:T(1,128)} custom-call(f32[8,1,1152]{2,1,0:T(1,128)S(1)} %all_to_all.16.after_ref.parts_ref), custom_call_target="tpu_custom_call" | custom-call | bytes 184320 | tf_op jit(solution)/shard_map/pallas_call | solution.py:39
  52.2 5.7 %all-to-all-start.2 = ((f32[32,1,1152]{2,1,0:T(1,128)}), f32[32,1,1152]{2,1,0:T(1,128)S(1)}, u32[]{:S(2)}, u32[]{:S(2)}) async-start(f32[32,1,1152]{2,1,0:T(1,128)} %shard_map.65), calls=%async_computation.2 | async-start | bytes 294912 | tf_op jit(solution)/shard_map/all_to_all | solution.py:333
  57.9 0.1 copy.17.wb3_ref
  58.0 0.1 copy.16.wb_ref
  58.2 1.9 %shard_map.62 = bf16[2048,128]{1,0:T(8,128)(2,1)} custom-call(bf16[32,64,128]{2,1,0:T(8,128)(2,1)S(1)} %get-tuple-element.21.rows_ref), custom_call_target="tpu_custom_call" | custom-call | bytes 1048576 | tf_op jit(solution)/shard_map/pallas_call | solution.py:39
  60.0 2.9 %shard_map.64 = bf16[2048,128]{1,0:T(8,128)(2,1)} custom-call(f32[8,1,1152]{2,1,0:T(1,128)S(1)} %all_to_all.16.after_ref.parts_ref, bf16[34,64,128]{2,1,0:T(8,128)(2,1)S(1)} %get-tuple-element.23.delta_ref, bf16[64,256]{1,0:T(8,128)(2,1)S(1)} %get-tuple-element.24.dstrip_ref, bf16[32,64,128]{2,1,0:T(8,128)(2,1)S(1)} %get-tuple-element.17.gr_ref, ...), custom_call_target="tpu_custom_call" | custom-call | flops 301989888 | bytes 1822720 | tf_op jit(solution)/shard_map/pallas_call | solution.py:39
  62.9 2.6 %all-to-all-done.2.parts_ref = f32[32,1,1152]{2,1,0:T(1,128)S(1)} async-done(((f32[32,1,1152]{2,1,0:T(1,128)}), f32[32,1,1152]{2,1,0:T(1,128)S(1)}, u32[]{:S(2)}, u32[]{:S(2)}) %all-to-all-start.2) | async-done | bytes 147488 | tf_op jit(solution)/shard_map/all_to_all | solution.py:333
  65.6 0.9 %shard_map.66 = f32[9,64,64]{2,1,0:T(8,128)} custom-call(f32[32,1,1152]{2,1,0:T(1,128)S(1)} %all-to-all-done.2.parts_ref), custom_call_target="tpu_custom_call" | custom-call | bytes 294912 | tf_op jit(solution)/shard_map/pallas_call | solution.py:39
  (1 shorter events, 0.0 us)
Async XLA Ops:
  2.0 10.4 %collective-permute-start = (bf16[192,128]{1,0:T(8,128)(2,1)S(1)}, bf16[192,128]{1,0:T(8,128)(2,1)S(1)}, u32[]{:S(2)}, u32[]{:S(2)}) collective-permute-start(bf16[192,128]{1,0:T(8,128)(2,1)S(1)} %get-tuple-element.19), channel_id=1, source_target_pairs={{0,8},{1,9},{2,10},{3,11},{4,12},{5,13},{6,14},{7,15},{8,0},{9,1},... | collective-permute-start | bytes 147464 | tf_op jit(solution)/shard_map/ppermute | solution.py:286
  4.7 7.8 %collective-permute-start.1 = (bf16[192,128]{1,0:T(8,128)(2,1)S(1)}, bf16[192,128]{1,0:T(8,128)(2,1)S(1)}, u32[]{:S(2)}, u32[]{:S(2)}) collective-permute-start(bf16[192,128]{1,0:T(8,128)(2,1)S(1)} %get-tuple-element.20), channel_id=1, source_target_pairs={{0,16},{16,0},{32,48},{48,32},{64,80},{80,64},{96,112},{112,96},{1... | collective-permute-start | bytes 147464 | tf_op jit(solution)/shard_map/ppermute | solution.py:287
  12.5 3.2 %copy-start = (bf16[3,3,64,64]{3,2,1,0:T(8,128)(2,1)S(1)}, bf16[3,3,64,64]{3,2,1,0:T(8,128)(2,1)}, u32[]{:S(2)}) copy-start(bf16[3,3,64,64]{3,2,1,0:T(8,128)(2,1)} %param.4) | copy-start | bytes 221188
  12.6 4.5 %collective-permute-start.2 = (bf16[192,128]{1,0:T(8,128)(2,1)S(1)}, bf16[192,128]{1,0:T(8,128)(2,1)S(1)}, u32[]{:S(2)}, u32[]{:S(2)}) collective-permute-start(bf16[192,128]{1,0:T(8,128)(2,1)S(1)} %shard_map.60.edge_ref), channel_id=1, source_target_pairs={{0,1},{1,0},{2,3},{3,2},{4,5},{5,4},{6,7},{7,6},{8,9},{9,8},{10,11... | collective-permute-start | bytes 147464 | tf_op jit(solution)/shard_map/ppermute | solution.py:298
  15.6 6.6 %collective-permute-start.3 = (bf16[192,128]{1,0:T(8,128)(2,1)S(1)}, bf16[192,128]{1,0:T(8,128)(2,1)S(1)}, u32[]{:S(2)}, u32[]{:S(2)}) collective-permute-start(bf16[192,128]{1,0:T(8,128)(2,1)S(1)} %shard_map.60.edge_ref), channel_id=1, source_target_pairs={{0,15},{1,2},{2,1},{3,4},{4,3},{5,6},{6,5},{7,8},{8,7},{9,10},{10,... | collective-permute-start | bytes 147464 | tf_op jit(solution)/shard_map/ppermute | solution.py:297
  52.2 13.4 %all-to-all-start.2 = ((f32[32,1,1152]{2,1,0:T(1,128)}), f32[32,1,1152]{2,1,0:T(1,128)S(1)}, u32[]{:S(2)}, u32[]{:S(2)}) async-start(f32[32,1,1152]{2,1,0:T(1,128)} %shard_map.65), calls=%async_computation.2 | async-start | bytes 294912 | tf_op jit(solution)/shard_map/all_to_all | solution.py:333

commit v5 on v4

--- a/solution.py
+++ b/solution.py
@@ -14,8 +14,10 @@
 PIECES = 4
 f32, bf16 = jnp.float32, jnp.bfloat16
 LON = ("z", "side")
-PLANE = ("lat", "side")
-EVERY = ("lat", "z", "side")
+LAT = ("low", "x", "core")
+EVERY = LAT + LON
+NEAR = ("x", "core")
+ACROSS = ("low", "side")
 
 
 def gelu_parts(hidden):
@@ -58,7 +60,7 @@
     ]
     for copy in copies[0] + copies[1]:
         copy.start()
-    even = lax.axis_index("lat") % 2 == 0
+    even = lax.axis_index("core") == 0
     end = ROWS - 1
     slots = (((0, 0, end), (1, 1, end - 1)), ((2, 0, end),))
     for at, src in enumerate((f_ref, g_ref)):
@@ -85,7 +87,7 @@
 
 
 def row_halos(outer_ref, inner_ref):
-    even = lax.axis_index("lat") % 2 == 0
+    even = lax.axis_index("core") == 0
     north = jnp.where(even, outer_ref[...], inner_ref[...]).astype(f32)
     south = jnp.where(even, inner_ref[...], outer_ref[...]).astype(f32)
     return [half[i * CH : (i + 1) * CH] for half in (north, south) for i in range(3)]
@@ -121,12 +123,12 @@
 
 
 def forward_body(
-    fr_ref, gr_ref, edge_ref, near_ref, far_ref, outer_ref, inner_ref, w_ref, w3_ref, wa_ref,
+    fr_ref, gr_ref, edge_ref, far_ref, near_ref, outer_ref, inner_ref, w_ref, w3_ref, wa_ref,
     out_ref, delta_ref, dstrip_ref, grad_ref, xs,
 ):
-    lat = lax.axis_index("lat")
+    lat = lax.axis_index(LAT)
     at_top = lat == 0
-    at_bottom = lat == lax.axis_size("lat") - 1
+    at_bottom = lat == lax.axis_size(LAT) - 1
     lane = lanes()
     n_near, n_far, n_cot, s_near, s_far, s_cot = row_halos(outer_ref, inner_ref)
 
@@ -197,20 +199,21 @@
             grad_ref[:, 0, pl.ds(start, width)] = piece[j * count : (j + 1) * count]
 
 
-def restore_body(rows_ref, out_ref, wide):
+def restore_body(rows_ref, out_ref, token_ref, wide):
     for r in range(ROWS):
         wide[pl.ds(r, CH, stride=ROWS), :] = rows_ref[r].astype(f32)
     out_ref[...] = wide[...].astype(bf16)
+    token_ref[...] = jnp.zeros(token_ref.shape, f32)
 
 
 def grad_scale():
     return float(ROWS * COLS * lax.axis_size(EVERY)) ** (-0.5)
 
 
-def backward_body(after_ref, delta_ref, dstrip_ref, gr_ref, wb_ref, wb3_ref, out_ref, xs, wide):
-    lat = lax.axis_index("lat")
+def backward_body(after_ref, delta_ref, dstrip_ref, gr_ref, wb_ref, wb3_ref, out_ref, token_ref, xs, wide):
+    lat = lax.axis_index(LAT)
     at_top = lat == 0
-    at_bottom = lat == lax.axis_size("lat") - 1
+    at_bottom = lat == lax.axis_size(LAT) - 1
     lane = lanes()
     s = dstrip_ref[:, :COLS].astype(f32)
     beyond = dstrip_ref[:, COLS:].astype(f32)
@@ -236,12 +239,29 @@
         put(r, back[:, :COLS])
         put(r + 1, back[:, COLS:])
     out_ref[...] = wide[...].astype(bf16)
-
-
-def fold_body(parts_ref, out_ref):
+    token_ref[...] = jnp.zeros(token_ref.shape, f32)
+
+
+def scatter_body(parts_ref, *rest):
+    out_ref = rest[-1]
+    total = jnp.sum(parts_ref[...], 0)
+    width = out_ref.shape[2]
+    for i in range(out_ref.shape[0]):
+        out_ref[i] = total[:, i * width : (i + 1) * width]
+
+
+def spread_body(parts_ref, *rest):
+    out_ref = rest[-1]
     total = jnp.sum(parts_ref[...], 0)
     for i in range(out_ref.shape[0]):
         out_ref[i] = total
+
+
+def join_body(parts_ref, out_ref):
+    width = parts_ref.shape[2]
+    for i in range(out_ref.shape[0]):
+        for j in range(parts_ref.shape[0]):
+            out_ref[i, :, pl.ds(j * width, width)] = parts_ref[j]
 
 
 def unpack_body(parts_ref, out_ref):
@@ -268,9 +288,9 @@
 
 
 def on_device(field, kernel, cotangent):
-    lat_count = lax.axis_size("lat")
+    lat_count = lax.axis_size(LAT)
     lon_count = lax.axis_size(LON)
-    plane = lax.axis_size(PLANE)
+    near_count = lax.axis_size(NEAR)
     flat = (CH * ROWS, COLS)
     rows_shape = (ROWS, CH, COLS)
 
@@ -284,7 +304,7 @@
         limit=52.5,
     )
     outer = lax.ppermute(outer, EVERY, outer_pairs(lat_count, lon_count))
-    inner = lax.ppermute(inner, "lat", [(i, i ^ 1) for i in range(lat_count)])
+    inner = lax.ppermute(inner, "core", [(0, 1), (1, 0)])
     fr, gr, edge = call(
         turn_body,
         [(rows_shape, bf16), (rows_shape, bf16), ((2 * CH, COLS), bf16)],
@@ -310,27 +330,33 @@
             (rows_shape, bf16),
             ((ROWS + 2, CH, COLS), bf16),
             ((CH, 2 * COLS), bf16),
-            ((plane, 1, 9 * CH * CH // plane), f32),
+            ((near_count, 1, 9 * CH * CH // near_count), f32),
         ],
-        (fr, gr, edge, near, far, outer, inner, w, w3, w3.reshape(TAPS, TAPS)),
+        (fr, gr, edge, far, near, outer, inner, w, w3, w3.reshape(TAPS, TAPS)),
         [pltpu.VMEM((ROWS + 4, TAPS, COLS), bf16)],
         2 * conv_flops,
     )
 
-    def spread(parts, count):
-        return call(fold_body, [((count,) + parts.shape[1:], f32)], (parts,))[0]
-
-    parts = lax.all_to_all(grad, PLANE, 0, 0)
-    (output,) = call(restore_body, [(flat, bf16)], (out_rows,), [pltpu.VMEM(flat, f32)])
-    parts = lax.all_to_all(spread(parts, lax.axis_size("z")), "z", 0, 0)
-    (grad_input,) = call(
+    def exchange(body, count, width, axes, *args):
+        (parts,) = call(body, [((count, 1, width), f32)], args)
+        return lax.all_to_all(parts, axes, 0, 0)
+
+    token = ((8, COLS), f32)
+    across, deep = lax.axis_size(ACROSS), lax.axis_size("z")
+    piece = grad.shape[2] // across
+    parts = lax.all_to_all(grad, NEAR, 0, 0)
+    output, done = call(restore_body, [(flat, bf16), token], (out_rows,), [pltpu.VMEM(flat, f32)])
+    parts = exchange(scatter_body, across, piece, ACROSS, parts, done)
+    grad_input, done = call(
         backward_body,
-        [(flat, bf16)],
+        [(flat, bf16), token],
         (parts, delta, dstrip, gr, wb, wb3),
         [pltpu.VMEM((ROWS + 2, TAPS, COLS), bf16), pltpu.VMEM(flat, f32)],
         conv_flops,
     )
-    parts = lax.all_to_all(spread(parts, plane), PLANE, 0, 0)
+    parts = exchange(spread_body, deep, piece, "z", parts)
+    parts = exchange(spread_body, across, piece, ACROSS, parts, done)
+    parts = exchange(join_body, near_count, piece * across, NEAR, parts)
     (grad_kernel,) = call(unpack_body, [((9, CH, CH), f32)], (parts,))
     shape = field.shape
     return (output.reshape(shape), grad_input.reshape(shape), grad_kernel.reshape(kernel.shape))
@@ -338,8 +364,9 @@
 
 def solution(mesh):
     lat_count, lon_count = mesh.devices.shape
-    split = Mesh(mesh.devices.reshape(lat_count, lon_count // 2, 2), EVERY)
-    block = P(None, None, "lat", LON)
+    x = min(4, lat_count // 2)
+    split = Mesh(mesh.devices.reshape(lat_count // (2 * x), x, 2, lon_count // 2, 2), EVERY)
+    block = P(None, None, LAT, LON)
     return jax.shard_map(
         on_device,
         mesh=split,

time: 66.7 us -> 76.1 us (1.14)
  starting transfers between devices: 17.5 us -> 25 us
  waiting for transfers between devices: 8.32 us -> 10 us
    all_to_all x1 -> x2, starting transfers between devices: 5.67 us -> 12.7 us  [the longest x1 9.39 us: on_device(): parts = lax.all_to_all(grad, NEAR, 0, 0)]
    all_to_all x1 -> x2, waiting for transfers between devices: 2.65 us -> 7.27 us  [the longest x1 3.7 us: exchange(): return lax.all_to_all(parts, axes, 0, 0)]
    ppermute x1, waiting for transfers between devices: 5.02 us -> 2.26 us  [on_device(): far = lax.ppermute(edge, LON, swaps)]
    ppermute x1, starting transfers between devices: 0.01 us -> 2.55 us  [on_device(): far = lax.ppermute(edge, LON, swaps)]
    ppermute x1, starting transfers between devices: 3 us -> 0.97 us  [on_device(): near = lax.ppermute(edge, 'side', [(0, 1), (1, 0)])]
    pallas_call x9 -> x11, Pallas kernels: 12.9 us -> 13.6 us  [call(): pl.pallas_call(body, out_shape=outs, in_specs=[pl.BlockSpec(memory_space=...]
    all_to_all x2 -> x3, blocking collectives: 25.8 us -> 25.2 us  [exchange(): return lax.all_to_all(parts, axes, 0, 0)]
  transfers between devices with their start and end apart: 5 -> 6, of which waited for: 3 -> 4; matrix products, arithmetic and copies ran while one was open for 2% -> 2% of each run, Pallas kernels for 10% -> 8%
where the time goes in v5:
time: 76.1 us; the launch traced here: 75.7 us
  blocking collectives  25.2 us (33%)
  starting transfers between devices  25 us (33%)
  Pallas kernels  13.6 us (18%)
  waiting for transfers between devices  10 us (13%)
  local copies, waits for them, and re-layouts  1.15 us (2%)
    all_to_all x3, blocking collectives, exchange(): return lax.all_to_all(parts, axes, 0, 0)  25.2 us
    pallas_call x11, Pallas kernels, call(): pl.pallas_call(body, out_shape=outs, in_specs=[pl.BlockSpec(memory_space=...  13.6 us
    all_to_all x1, starting transfers between devices, on_device(): parts = lax.all_to_all(grad, NEAR, 0, 0)  9.39 us
    ppermute x1, starting transfers between devices, on_device(): inner = lax.ppermute(inner, 'core', [(0, 1), (1, 0)])  6.09 us
    all_to_all x1, waiting for transfers between devices, exchange(): return lax.all_to_all(parts, axes, 0, 0)  3.7 us
    all_to_all x1, waiting for transfers between devices, on_device(): parts = lax.all_to_all(grad, NEAR, 0, 0)  3.57 us
    all_to_all x1, starting transfers between devices, exchange(): return lax.all_to_all(parts, axes, 0, 0)  3.34 us
    ppermute x1, starting transfers between devices, on_device(): outer = lax.ppermute(outer, EVERY, outer_pairs(lat_count, lon_count))  2.69 us
  transfers between devices with their start and end apart: 6, of which 4 were waited for; matrix products, arithmetic and copies ran while one was open for 2% of the time, Pallas kernels for 8%

profile of v5, /device:TPU:1, one launch (start us, length us, event | category | flops | bytes accessed | tf_op | source)
XLA Modules:
  0.0 75.7 jit_solution(1818709720368084290)
XLA Ops:
  0.6 1.4 %shard_map.58 = (bf16[192,128]{1,0:T(8,128)(2,1)S(1)}, bf16[192,128]{1,0:T(8,128)(2,1)S(1)}, bf16[2048,128]{1,0:T(8,128)(2,1)S(1)}, bf16[2048,128]{1,0:T(8,128)(2,1)S(1)}) custom-call(bf16[2048,128]{1,0:T(8,128)(2,1)} %bitcast.22, bf16[2048,128]{1,0:T(8,128)(2,1)} %bitcast.23), custom_call_target="tpu_custom_call" | custom-call | bytes 2195456 | tf_op jit(solution)/shard_map/pallas_call | solution.py:41
  2.0 2.7 %collective-permute-start = (bf16[192,128]{1,0:T(8,128)(2,1)S(1)}, bf16[192,128]{1,0:T(8,128)(2,1)S(1)}, u32[]{:S(2)}, u32[]{:S(2)}) collective-permute-start(bf16[192,128]{1,0:T(8,128)(2,1)S(1)} %get-tuple-element.23), channel_id=1, source_target_pairs={{0,8},{1,9},{2,10},{3,11},{4,12},{5,13},{6,14},{7,15},{8,0},{9,1},... | collective-permute-start | bytes 147464 | tf_op jit(solution)/shard_map/ppermute | solution.py:306
  4.7 6.1 %collective-permute-start.1 = (bf16[192,128]{1,0:T(8,128)(2,1)S(1)}, bf16[192,128]{1,0:T(8,128)(2,1)S(1)}, u32[]{:S(2)}, u32[]{:S(2)}) collective-permute-start(bf16[192,128]{1,0:T(8,128)(2,1)S(1)} %get-tuple-element.24), channel_id=1, source_target_pairs={{0,16},{16,0},{1,17},{17,1},{2,18},{18,2},{3,19},{19,3},{4,20},{20... | collective-permute-start | bytes 147464 | tf_op jit(solution)/shard_map/ppermute | solution.py:307
  10.8 1.6 %shard_map.59 = (bf16[32,64,128]{2,1,0:T(8,128)(2,1)S(1)}, bf16[32,64,128]{2,1,0:T(8,128)(2,1)S(1)}, bf16[128,128]{1,0:T(8,128)(2,1)S(1)}) custom-call(bf16[2048,128]{1,0:T(8,128)(2,1)S(1)} %get-tuple-element.18.f_ref, bf16[2048,128]{1,0:T(8,128)(2,1)S(1)} %get-tuple-element.19.g_ref), custom_call_target="tpu_custom_call" | custom-call | bytes 2129920 | tf_op jit(solution)/shard_map/pallas_call | solution.py:41
  12.5 0.0 copy-start
  12.5 0.0 collective-permute-done.outer_ref
  12.5 0.0 collective-permute-done.1.inner_ref
  12.5 0.1 shard_map.60.edge_ref
  12.6 2.5 %collective-permute-start.2 = (bf16[192,128]{1,0:T(8,128)(2,1)S(1)}, bf16[192,128]{1,0:T(8,128)(2,1)S(1)}, u32[]{:S(2)}, u32[]{:S(2)}) collective-permute-start(bf16[192,128]{1,0:T(8,128)(2,1)S(1)} %shard_map.60.edge_ref), channel_id=1, source_target_pairs={{0,15},{1,2},{2,1},{3,4},{4,3},{5,6},{6,5},{7,8},{8,7},{9,10},{10,... | collective-permute-start | bytes 147464 | tf_op jit(solution)/shard_map/ppermute | solution.py:317
  15.2 1.0 %collective-permute-start.3 = (bf16[192,128]{1,0:T(8,128)(2,1)S(1)}, bf16[192,128]{1,0:T(8,128)(2,1)S(1)}, u32[]{:S(2)}, u32[]{:S(2)}) collective-permute-start(bf16[192,128]{1,0:T(8,128)(2,1)S(1)} %shard_map.60.edge_ref), channel_id=1, source_target_pairs={{0,1},{1,0},{2,3},{3,2},{4,5},{5,4},{6,7},{7,6},{8,9},{9,8},{10,11... | collective-permute-start | bytes 147464 | tf_op jit(solution)/shard_map/ppermute | solution.py:318
  16.1 0.0 copy-done
  16.1 0.1 copy.13
  16.3 0.1 copy.12
  16.4 0.2 reshape_reshape.3.wa_ref
  16.6 0.1 copy.15.w3_ref
  16.7 0.1 copy.11
  16.9 0.1 copy.14.w_ref
  17.0 2.3 %collective-permute-done.2.far_ref = bf16[192,128]{1,0:T(8,128)(2,1)S(1)} collective-permute-done((bf16[192,128]{1,0:T(8,128)(2,1)S(1)}, bf16[192,128]{1,0:T(8,128)(2,1)S(1)}, u32[]{:S(2)}, u32[]{:S(2)}) %collective-permute-start.2) | collective-permute-done | bytes 49184 | tf_op jit(solution)/shard_map/ppermute | solution.py:317
  19.3 0.5 collective-permute-done.3.near_ref
  19.8 4.1 %shard_map.61 = (bf16[32,64,128]{2,1,0:T(8,128)(2,1)S(1)}, bf16[34,64,128]{2,1,0:T(8,128)(2,1)S(1)}, bf16[64,256]{1,0:T(8,128)(2,1)S(1)}, f32[8,1,4608]{2,1,0:T(1,128)}) custom-call(bf16[32,64,128]{2,1,0:T(8,128)(2,1)S(1)} %get-tuple-element.20.fr_ref, bf16[32,64,128]{2,1,0:T(8,128)(2,1)S(1)} %get-tuple-element.21.gr_ref, ...), custom_call_target="tpu_custom_call" | custom-call | flops 603979776 | bytes 2777088 | tf_op jit(solution)/shard_map/pallas_call | solution.py:41
  23.9 9.4 %all-to-all-start = ((f32[8,1,4608]{2,1,0:T(1,128)}), f32[8,1,4608]{2,1,0:T(1,128)S(1)}, u32[]{:S(2)}, u32[]{:S(2)}) async-start(f32[8,1,4608]{2,1,0:T(1,128)} %get-tuple-element.27), calls=%async_computation | async-start | bytes 294912 | tf_op jit(solution)/shard_map/all_to_all | solution.py:347
  33.2 1.9 %shard_map.62 = (bf16[2048,128]{1,0:T(8,128)(2,1)}, f32[8,128]{1,0:T(8,128)S(1)}) custom-call(bf16[32,64,128]{2,1,0:T(8,128)(2,1)S(1)} %get-tuple-element.25.rows_ref), custom_call_target="tpu_custom_call" | custom-call | bytes 1052672 | tf_op jit(solution)/shard_map/pallas_call | solution.py:41
  35.1 3.6 %all-to-all-done.parts_ref = f32[8,1,4608]{2,1,0:T(1,128)S(1)} async-done(((f32[8,1,4608]{2,1,0:T(1,128)}), f32[8,1,4608]{2,1,0:T(1,128)S(1)}, u32[]{:S(2)}, u32[]{:S(2)}) %all-to-all-start) | async-done | bytes 147488 | tf_op jit(solution)/shard_map/all_to_all | solution.py:347
  38.7 0.1 shard_map.63
  38.8 6.5 %all_to_all.25.after_ref.parts_ref = f32[4,1,1152]{2,1,0:T(1,128)S(1)} all-to-all(f32[4,1,1152]{2,1,0:T(1,128)S(1)} %shard_map.63), channel_id=1, replica_groups=mesh['low'=2,'x'=4,'core'=2,'z'=8,'side'=2] {'low','side'}, dimensions={0} | all-to-all | bytes 36864 | tf_op jit(solution)/shard_map/all_to_all | solution.py:342
  45.3 0.6 shard_map.65
  46.0 3.3 %all-to-all-start.2 = ((f32[8,1,1152]{2,1,0:T(1,128)}), f32[8,1,1152]{2,1,0:T(1,128)S(1)}, u32[]{:S(2)}, u32[]{:S(2)}) async-start(f32[8,1,1152]{2,1,0:T(1,128)} %shard_map.65), calls=%async_computation.2 | async-start | bytes 73728 | tf_op jit(solution)/shard_map/all_to_all | solution.py:342
  49.3 0.1 copy.17.wb3_ref
  49.5 0.1 copy.16.wb_ref
  49.6 2.8 %shard_map.64 = (bf16[2048,128]{1,0:T(8,128)(2,1)}, f32[8,128]{1,0:T(8,128)S(1)}) custom-call(f32[4,1,1152]{2,1,0:T(1,128)S(1)} %all_to_all.25.after_ref.parts_ref, bf16[34,64,128]{2,1,0:T(8,128)(2,1)S(1)} %get-tuple-element.29.delta_ref, bf16[64,256]{1,0:T(8,128)(2,1)S(1)} %get-tuple-element.30.dstrip_ref, ...), custom_call_target="tpu_custom_call" | custom-call | flops 301989888 | bytes 1808384 | tf_op jit(solution)/shard_map/pallas_call | solution.py:41
  52.4 3.7 %all-to-all-done.2.parts_ref = f32[8,1,1152]{2,1,0:T(1,128)S(1)} async-done(((f32[8,1,1152]{2,1,0:T(1,128)}), f32[8,1,1152]{2,1,0:T(1,128)S(1)}, u32[]{:S(2)}, u32[]{:S(2)}) %all-to-all-start.2) | async-done | bytes 36896 | tf_op jit(solution)/shard_map/all_to_all | solution.py:342
  56.2 6.5 %all_to_all.26.parts_ref = f32[4,1,1152]{2,1,0:T(1,128)S(1)} all-to-all(f32[4,1,1152]{2,1,0:T(1,128)S(1)} %shard_map.66), channel_id=1, replica_groups=mesh['low'=2,'x'=4,'core'=2,'z'=8,'side'=2] {'low','side'}, dimensions={0} | all-to-all | bytes 36864 | tf_op jit(solution)/shard_map/all_to_all | solution.py:342
  62.7 12.1 %all_to_all.27.parts_ref = f32[8,1,4608]{2,1,0:T(1,128)S(1)} all-to-all(f32[8,1,4608]{2,1,0:T(1,128)S(1)} %shard_map.67), channel_id=1, replica_groups=mesh['low'=2,'x'=4,'core'=2,'z'=8,'side'=2] {'x','core'}, dimensions={0} | all-to-all | bytes 294912 | tf_op jit(solution)/shard_map/all_to_all | solution.py:342
  74.9 0.9 %shard_map.68 = f32[9,64,64]{2,1,0:T(8,128)} custom-call(f32[8,1,4608]{2,1,0:T(1,128)S(1)} %all_to_all.27.parts_ref), custom_call_target="tpu_custom_call" | custom-call | bytes 294912 | tf_op jit(solution)/shard_map/pallas_call | solution.py:41
  (3 shorter events, 0.1 us)
Async XLA Ops:
  2.0 10.4 %collective-permute-start = (bf16[192,128]{1,0:T(8,128)(2,1)S(1)}, bf16[192,128]{1,0:T(8,128)(2,1)S(1)}, u32[]{:S(2)}, u32[]{:S(2)}) collective-permute-start(bf16[192,128]{1,0:T(8,128)(2,1)S(1)} %get-tuple-element.23), channel_id=1, source_target_pairs={{0,8},{1,9},{2,10},{3,11},{4,12},{5,13},{6,14},{7,15},{8,0},{9,1},... | collective-permute-start | bytes 147464 | tf_op jit(solution)/shard_map/ppermute | solution.py:306
  4.7 7.8 %collective-permute-start.1 = (bf16[192,128]{1,0:T(8,128)(2,1)S(1)}, bf16[192,128]{1,0:T(8,128)(2,1)S(1)}, u32[]{:S(2)}, u32[]{:S(2)}) collective-permute-start(bf16[192,128]{1,0:T(8,128)(2,1)S(1)} %get-tuple-element.24), channel_id=1, source_target_pairs={{0,16},{16,0},{1,17},{17,1},{2,18},{18,2},{3,19},{19,3},{4,20},{20... | collective-permute-start | bytes 147464 | tf_op jit(solution)/shard_map/ppermute | solution.py:307
  12.5 3.7 %copy-start = (bf16[3,3,64,64]{3,2,1,0:T(8,128)(2,1)S(1)}, bf16[3,3,64,64]{3,2,1,0:T(8,128)(2,1)}, u32[]{:S(2)}) copy-start(bf16[3,3,64,64]{3,2,1,0:T(8,128)(2,1)} %param.4) | copy-start | bytes 221188
  12.6 6.7 %collective-permute-start.2 = (bf16[192,128]{1,0:T(8,128)(2,1)S(1)}, bf16[192,128]{1,0:T(8,128)(2,1)S(1)}, u32[]{:S(2)}, u32[]{:S(2)}) collective-permute-start(bf16[192,128]{1,0:T(8,128)(2,1)S(1)} %shard_map.60.edge_ref), channel_id=1, source_target_pairs={{0,15},{1,2},{2,1},{3,4},{4,3},{5,6},{6,5},{7,8},{8,7},{9,10},{10,... | collective-permute-start | bytes 147464 | tf_op jit(solution)/shard_map/ppermute | solution.py:317
  15.2 4.6 %collective-permute-start.3 = (bf16[192,128]{1,0:T(8,128)(2,1)S(1)}, bf16[192,128]{1,0:T(8,128)(2,1)S(1)}, u32[]{:S(2)}, u32[]{:S(2)}) collective-permute-start(bf16[192,128]{1,0:T(8,128)(2,1)S(1)} %shard_map.60.edge_ref), channel_id=1, source_target_pairs={{0,1},{1,0},{2,3},{3,2},{4,5},{5,4},{6,7},{7,6},{8,9},{9,8},{10,11... | collective-permute-start | bytes 147464 | tf_op jit(solution)/shard_map/ppermute | solution.py:318
  23.9 14.8 %all-to-all-start = ((f32[8,1,4608]{2,1,0:T(1,128)}), f32[8,1,4608]{2,1,0:T(1,128)S(1)}, u32[]{:S(2)}, u32[]{:S(2)}) async-start(f32[8,1,4608]{2,1,0:T(1,128)} %get-tuple-element.27), calls=%async_computation | async-start | bytes 294912 | tf_op jit(solution)/shard_map/all_to_all | solution.py:347
  46.0 10.2 %all-to-all-start.2 = ((f32[8,1,1152]{2,1,0:T(1,128)}), f32[8,1,1152]{2,1,0:T(1,128)S(1)}, u32[]{:S(2)}, u32[]{:S(2)}) async-start(f32[8,1,1152]{2,1,0:T(1,128)} %shard_map.65), calls=%async_computation.2 | async-start | bytes 73728 | tf_op jit(solution)/shard_map/all_to_all | solution.py:342

commit v6 on v4

--- a/solution.py
+++ b/solution.py
@@ -91,7 +91,7 @@
     return [half[i * CH : (i + 1) * CH] for half in (north, south) for i in range(3)]
 
 
-def edge_body(edge_ref, outer_ref, inner_ref, out_ref):
+def edge_body(edge_ref, outer_ref, inner_ref, token_ref, out_ref):
     n_near, n_far, n_cot, s_near, s_far, s_cot = row_halos(outer_ref, inner_ref)
     lane = lanes()
     low = jnp.where(lane < 4, roll(s_near, 2), jnp.where(lane < 8, roll(s_far, 6), roll(s_cot, 10)))
@@ -120,9 +120,41 @@
     return jnp.dot(a, b, preferred_element_type=f32)
 
 
-def forward_body(
-    fr_ref, gr_ref, edge_ref, near_ref, far_ref, outer_ref, inner_ref, w_ref, w3_ref, wa_ref,
-    out_ref, delta_ref, dstrip_ref, grad_ref, xs,
+def interior_body(fr_ref, gr_ref, w_ref, out_ref, delta_ref, grad_ref, token_ref, xs):
+    lane = lanes()
+    inner = (lane > 0) & (lane < COLS - 1)
+    none = jnp.zeros((CH, COLS), f32)
+    for r in range(ROWS):
+        stack_taps(xs, r, fr_ref[r].astype(f32), none, lane)
+    weights = w_ref[...]
+    for r in range(1, ROWS - 1, 2):
+        window = jnp.concatenate(
+            [xs[r - 1 : r + 2].reshape(3 * TAPS, COLS), xs[r : r + 3].reshape(3 * TAPS, COLS)], 1
+        )
+        value, slope = gelu_parts(dot(weights, window))
+        for k in range(2):
+            cut = slice(k * COLS, (k + 1) * COLS)
+            out_ref[r + k - 1] = (fr_ref[r + k].astype(f32) + value[:, cut]).astype(bf16)
+            delta = gr_ref[r + k].astype(f32) * slope[:, cut]
+            delta_ref[r + k - 1] = jnp.where(inner, delta, 0.0).astype(bf16)
+    total = None
+    group = 10
+    for r in range(0, ROWS - 2, group):
+        left = jnp.concatenate([delta_ref[r + k] for k in range(group)], 1)
+        right = jnp.concatenate([xs[r + k : r + k + 3].reshape(3 * TAPS, COLS) for k in range(group)], 1)
+        term = dot_lanes(left, right)
+        total = term if total is None else total + term
+    grad_ref[...] = total
+    token_ref[...] = jnp.zeros(token_ref.shape, f32)
+
+
+def dot_lanes(a, b):
+    return lax.dot_general(a, b, (((1,), (1,)), ((), ())), preferred_element_type=f32)
+
+
+def border_body(
+    fr_ref, gr_ref, edge_ref, far_ref, near_ref, outer_ref, inner_ref, w_ref, wa_ref, part_ref,
+    out_ref, outstrip_ref, delta_ref, dstrip_ref, grad_ref, xs,
 ):
     lat = lax.axis_index("lat")
     at_top = lat == 0
@@ -135,58 +167,64 @@
     beyond = strip(near_ref, far_ref, 2)
     gbeyond = jnp.where(lane < 64, roll(beyond, 120), roll(beyond, 8))
 
+    end = ROWS - 1
     stack_taps(xs, 0, n_far, roll(beyond, -122), lane)
     stack_taps(xs, 1, n_near, roll(beyond, -126), lane)
-    for r in range(ROWS):
-        stack_taps(xs, r + 2, fr_ref[r].astype(f32), roll(s, -(4 * r + 2)), lane)
-    stack_taps(xs, ROWS + 2, s_near, roll(beyond, -2), lane)
-    stack_taps(xs, ROWS + 3, s_far, roll(beyond, -6), lane)
+    for at, r in ((2, 0), (3, 1), (4, end - 1), (5, end)):
+        stack_taps(xs, at, fr_ref[r].astype(f32), roll(s, -(4 * r + 2)), lane)
+    stack_taps(xs, 6, s_near, roll(beyond, -2), lane)
+    stack_taps(xs, 7, s_far, roll(beyond, -6), lane)
 
     weights = w_ref[...]
-    for r in range(0, ROWS, 2):
-        window = jnp.concatenate(
-            [xs[r + 1 : r + 4].reshape(3 * TAPS, COLS), xs[r + 2 : r + 5].reshape(3 * TAPS, COLS)], 1
-        )
-        value, slope = gelu_parts(dot(weights, window))
-        for k in range(2):
-            cut = slice(k * COLS, (k + 1) * COLS)
-            out_ref[r + k] = (fr_ref[r + k].astype(f32) + value[:, cut]).astype(bf16)
-            delta_ref[r + k + 1] = (gr_ref[r + k].astype(f32) * slope[:, cut]).astype(bf16)
-
-    def outer(inside, near, far, flip, cot, up):
-        ends = (far, inside) if up else (inside, far)
-        first = jnp.where(flip, xs[ends[1]], xs[ends[0]])
-        last = jnp.where(flip, xs[ends[0]], xs[ends[1]])
-        total = dot(w3_ref[0], first) + dot(w3_ref[1], xs[near]) + dot(w3_ref[2], last)
-        return (cot * gelu_parts(total)[1]).astype(bf16)
-
-    delta_ref[0] = outer(2, 1, 0, at_top, n_cot, True)
-    delta_ref[ROWS + 1] = outer(ROWS + 1, ROWS + 2, ROWS + 3, at_bottom, s_cot, False)
-
+    window = jnp.concatenate([xs[1:4].reshape(3 * TAPS, COLS), xs[4:7].reshape(3 * TAPS, COLS)], 1)
+    value, slope = gelu_parts(dot(weights, window))
+    deltas = []
+    for k, r in enumerate((0, end)):
+        cut = slice(k * COLS, (k + 1) * COLS)
+        out_ref[k] = (fr_ref[r].astype(f32) + value[:, cut]).astype(bf16)
+        deltas.append((gr_ref[r].astype(f32) * slope[:, cut]).astype(bf16))
+        delta_ref[k + 1] = deltas[k]
+
+    def turned(flip, low):
+        first = jnp.where(flip, xs[low + 2], xs[low])
+        last = jnp.where(flip, xs[low], xs[low + 2])
+        return jnp.concatenate([first, xs[low + 1], last], 0)
+
+    outside = jnp.concatenate([turned(at_top, 0), turned(at_bottom, 5)], 1)
+    slope = gelu_parts(dot(weights, outside))[1]
+    delta_ref[0] = (n_cot * slope[:, :COLS]).astype(bf16)
+    delta_ref[3] = (s_cot * slope[:, COLS:]).astype(bf16)
+
+    edge = edge_ref[pl.ds(0, CH), :].astype(f32)
     halo = jnp.concatenate([s, beyond], 1)
-    own = jnp.concatenate(
-        [edge_ref[pl.ds(0, CH), :].astype(f32), edge_ref[pl.ds(2 * CH, CH), :].astype(f32)], 1
-    )
+    own = jnp.concatenate([edge, edge_ref[pl.ds(2 * CH, CH), :].astype(f32)], 1)
     wide_lane = lanes(2 * COLS)
     kind = wide_lane % 4
-    columns = jnp.concatenate(
+    small = lane % 4
+    outer_taps = jnp.concatenate(
         [roll(jnp.where(kind == 0, halo, own), 1), halo, roll(jnp.where(kind == 3, halo, own), -1)], 0
-    ).astype(bf16)
-    y = dot(wa_ref[...], columns)
-    y0, y1, y2 = [y[i * CH : (i + 1) * CH] for i in range(3)]
+    )
+    inner_taps = jnp.concatenate(
+        [roll(jnp.where(small == 1, s, edge), 1), edge, roll(jnp.where(small == 2, s, edge), -1)], 0
+    )
+    y = dot(wa_ref[...], jnp.concatenate([outer_taps, inner_taps], 1).astype(bf16))
+    y0, y1, y2 = [y[i * CH : (i + 1) * CH, : 2 * COLS] for i in range(3)]
     straight = roll(y0, 4) + y1 + roll(y2, -4)
-    turned = roll(y2, 4) + y1 + roll(y0, -4)
+    backward = roll(y2, 4) + y1 + roll(y0, -4)
     flip = ((wide_lane >= 252) & at_top) | ((wide_lane >= 128) & (wide_lane < 132) & at_bottom)
-    slope = gelu_parts(jnp.where(flip, turned, straight))[1]
-    dstrip_ref[...] = (jnp.concatenate([gs, gbeyond], 1) * slope).astype(bf16)
-
-    total = None
-    group = 8
-    for r in range(0, ROWS, group):
-        left = jnp.concatenate([delta_ref[r + k + 1] for k in range(group)], 1)
-        right = jnp.concatenate([xs[r + k + 1 : r + k + 4].reshape(3 * TAPS, COLS) for k in range(group)], 1)
-        term = lax.dot_general(left, right, (((1,), (1,)), ((), ())), preferred_element_type=f32)
-        total = term if total is None else total + term
+    y0, y1, y2 = [y[i * CH : (i + 1) * CH, 2 * COLS :] for i in range(3)]
+    packed = [jnp.where(flip, backward, straight), roll(y0, 4) + y1 + roll(y2, -4)]
+    value, slope = gelu_parts(jnp.concatenate(packed, 1))
+    own_cot = edge_ref[pl.ds(CH, CH), :].astype(f32)
+    outstrip_ref[...] = (edge + value[:, 2 * COLS :]).astype(bf16)
+    dstrip = jnp.concatenate([gs, gbeyond, own_cot], 1) * slope
+    dstrip_ref[...] = dstrip.astype(bf16)
+
+    used = ((small == 1) | (small == 2)) & (lane >= 4) & (lane < 4 * end)
+    side = jnp.where(used, dstrip[:, 2 * COLS :], 0.0).astype(bf16)
+    shifted = jnp.concatenate([roll(inner_taps, 4), inner_taps, roll(inner_taps, -4)], 0).astype(bf16)
+    left = jnp.concatenate([deltas[0], deltas[1], side], 1)
+    total = part_ref[...] + dot_lanes(left, jnp.concatenate([window, shifted], 1))
     total = total * grad_scale()
     pieces = [total[:, p * COLS : (p + 1) * COLS] for p in range(4)] + [total[:, 4 * COLS :]]
     count = grad_ref.shape[0]
@@ -197,9 +235,17 @@
             grad_ref[:, 0, pl.ds(start, width)] = piece[j * count : (j + 1) * count]
 
 
-def restore_body(rows_ref, out_ref, wide):
-    for r in range(ROWS):
-        wide[pl.ds(r, CH, stride=ROWS), :] = rows_ref[r].astype(f32)
+def patched(row, packed, r, lane):
+    return jnp.where((lane == 0) | (lane == COLS - 1), roll(packed, -(4 * r + 2)), row.astype(f32))
+
+
+def restore_body(mid_ref, rim_ref, strip_ref, out_ref, wide):
+    lane = lanes()
+    packed = strip_ref[...].astype(f32)
+    wide[pl.ds(0, CH, stride=ROWS), :] = rim_ref[0].astype(f32)
+    for r in range(1, ROWS - 1):
+        wide[pl.ds(r, CH, stride=ROWS), :] = patched(mid_ref[r - 1], packed, r, lane)
+    wide[pl.ds(ROWS - 1, CH, stride=ROWS), :] = rim_ref[1].astype(f32)
     out_ref[...] = wide[...].astype(bf16)
 
 
@@ -207,17 +253,20 @@
     return float(ROWS * COLS * lax.axis_size(EVERY)) ** (-0.5)
 
 
-def backward_body(after_ref, delta_ref, dstrip_ref, gr_ref, wb_ref, wb3_ref, out_ref, xs, wide):
+def backward_body(after_ref, mid_ref, rim_ref, dstrip_ref, gr_ref, wb_ref, wb3_ref, out_ref, xs, wide):
     lat = lax.axis_index("lat")
     at_top = lat == 0
     at_bottom = lat == lax.axis_size("lat") - 1
     lane = lanes()
     s = dstrip_ref[:, :COLS].astype(f32)
-    beyond = dstrip_ref[:, COLS:].astype(f32)
-    stack_taps(xs, 0, delta_ref[0].astype(f32), roll(beyond, -126), lane)
-    for r in range(ROWS):
-        stack_taps(xs, r + 1, delta_ref[r + 1].astype(f32), roll(s, -(4 * r + 2)), lane)
-    stack_taps(xs, ROWS + 1, delta_ref[ROWS + 1].astype(f32), roll(beyond, -2), lane)
+    beyond = dstrip_ref[:, COLS : 2 * COLS].astype(f32)
+    own = dstrip_ref[:, 2 * COLS :].astype(f32)
+    stack_taps(xs, 0, rim_ref[0].astype(f32), roll(beyond, -126), lane)
+    stack_taps(xs, 1, rim_ref[1].astype(f32), roll(s, -2), lane)
+    for r in range(1, ROWS - 1):
+        stack_taps(xs, r + 1, patched(mid_ref[r - 1], own, r, lane), roll(s, -(4 * r + 2)), lane)
+    stack_taps(xs, ROWS, rim_ref[2].astype(f32), roll(s, -(4 * ROWS - 2)), lane)
+    stack_taps(xs, ROWS + 1, rim_ref[3].astype(f32), roll(beyond, -2), lane)
     weights = wb_ref[...]
 
     def put(r, back):
@@ -292,41 +341,54 @@
         [pltpu.VMEM(flat, f32)],
     )
 
-    (edge,) = call(edge_body, [((TAPS, COLS), bf16)], (edge, outer, inner))
-    swaps = [(i, (i + 1 if i % 2 else i - 1) % lon_count) for i in range(lon_count)]
-    far = lax.ppermute(edge, LON, swaps)
-    near = lax.ppermute(edge, "side", [(0, 1), (1, 0)])
-
-    w3 = jnp.transpose(kernel, (0, 2, 1, 3)).reshape(3, CH, TAPS)
+    w3 = jnp.transpose(kernel, (0, 2, 1, 3)).reshape(TAPS, TAPS)
     w = jnp.transpose(kernel, (2, 0, 1, 3)).reshape(CH, 3 * TAPS)
     turned = kernel[::-1, ::-1]
     wb3 = jnp.transpose(turned, (0, 3, 1, 2)).reshape(3, CH, TAPS)
     wb = jnp.transpose(turned, (3, 0, 1, 2)).reshape(CH, 3 * TAPS)
-
     conv_flops = 2 * 9 * CH * CH * ROWS * COLS
-    out_rows, delta, dstrip, grad = call(
-        forward_body,
+    out_mid, delta_mid, grad_mid, token = call(
+        interior_body,
         [
-            (rows_shape, bf16),
-            ((ROWS + 2, CH, COLS), bf16),
-            ((CH, 2 * COLS), bf16),
+            ((ROWS - 2, CH, COLS), bf16),
+            ((ROWS - 2, CH, COLS), bf16),
+            ((CH, 3 * TAPS), f32),
+            ((8, COLS), f32),
+        ],
+        (fr, gr, w),
+        [pltpu.VMEM((ROWS, TAPS, COLS), bf16)],
+        2 * conv_flops,
+    )
+
+    (edge,) = call(edge_body, [((TAPS, COLS), bf16)], (edge, outer, inner, token))
+    swaps = [(i, (i + 1 if i % 2 else i - 1) % lon_count) for i in range(lon_count)]
+    far = lax.ppermute(edge, LON, swaps)
+    near = lax.ppermute(edge, "side", [(0, 1), (1, 0)])
+
+    out_rim, out_strip, delta_rim, dstrip, grad = call(
+        border_body,
+        [
+            ((2, CH, COLS), bf16),
+            ((CH, COLS), bf16),
+            ((4, CH, COLS), bf16),
+            ((CH, 3 * COLS), bf16),
             ((plane, 1, 9 * CH * CH // plane), f32),
         ],
-        (fr, gr, edge, near, far, outer, inner, w, w3, w3.reshape(TAPS, TAPS)),
-        [pltpu.VMEM((ROWS + 4, TAPS, COLS), bf16)],
-        2 * conv_flops,
+        (fr, gr, edge, far, near, outer, inner, w, w3, grad_mid),
+        [pltpu.VMEM((8, TAPS, COLS), bf16)],
+        conv_flops // 4,
     )
 
     def spread(parts, count):
         return call(fold_body, [((count,) + parts.shape[1:], f32)], (parts,))[0]
 
     parts = lax.all_to_all(grad, PLANE, 0, 0)
-    (output,) = call(restore_body, [(flat, bf16)], (out_rows,), [pltpu.VMEM(flat, f32)])
+    (output,) = call(restore_body, [(flat, bf16)], (out_mid, out_rim, out_strip), [pltpu.VMEM(flat, f32)])
     parts = lax.all_to_all(spread(parts, lax.axis_size("z")), "z", 0, 0)
     (grad_input,) = call(
         backward_body,
         [(flat, bf16)],
-        (parts, delta, dstrip, gr, wb, wb3),
+        (parts, delta_mid, delta_rim, dstrip, gr, wb, wb3),
         [pltpu.VMEM((ROWS + 2, TAPS, COLS), bf16), pltpu.VMEM(flat, f32)],
         conv_flops,
     )

time: 66.7 us -> 63.8 us (0.957)
  waiting for transfers between devices: 8.32 us -> 6.11 us
  blocking collectives: 25.8 us -> 24.2 us
  Pallas kernels: 12.9 us -> 13.6 us
    ppermute x1, starting transfers between devices: 0.01 us -> 2.55 us  [on_device(): far = lax.ppermute(edge, LON, swaps)]
    all_to_all x1, blocking collectives: 13.1 us -> 10.9 us  [on_device(): parts = lax.all_to_all(spread(parts, lax.axis_size('z')), 'z', 0, 0)]
    ppermute x1, starting transfers between devices: 3 us -> 0.97 us  [on_device(): near = lax.ppermute(edge, 'side', [(0, 1), (1, 0)])]
    ppermute x1, waiting for transfers between devices: 5.02 us -> 3.26 us  [on_device(): far = lax.ppermute(edge, LON, swaps)]
    pallas_call x9 -> x10, Pallas kernels: 12.9 us -> 13.6 us  [call(): pl.pallas_call(body, out_shape=outs, in_specs=[pl.BlockSpec(memory_space=...]
  transfers between devices with their start and end apart: 5 -> 5, of which waited for: 3 -> 3; matrix products, arithmetic and copies ran while one was open for 2% -> 1% of each run, Pallas kernels for 10% -> 15%
where the time goes in v6:
time: 63.8 us; the launch traced here: 63.5 us
  blocking collectives  24.2 us (38%)
  starting transfers between devices  18 us (28%)
  Pallas kernels  13.6 us (21%)
  waiting for transfers between devices  6.11 us (10%)
  local copies, waits for them, and re-layouts  0.87 us (1%)
  between operations  0.72 us (1%)
    pallas_call x10, Pallas kernels, call(): pl.pallas_call(body, out_shape=outs, in_specs=[pl.BlockSpec(memory_space=...  13.6 us
    all_to_all x1, blocking collectives, on_device(): parts = lax.all_to_all(grad, PLANE, 0, 0)  13.3 us
    all_to_all x1, blocking collectives, on_device(): parts = lax.all_to_all(spread(parts, lax.axis_size('z')), 'z', 0, 0)  10.9 us
    ppermute x1, starting transfers between devices, on_device(): inner = lax.ppermute(inner, 'lat', [(i, i ^ 1) for i in range(lat_count)])  6.09 us
    all_to_all x1, starting transfers between devices, on_device(): parts = lax.all_to_all(spread(parts, plane), PLANE, 0, 0)  5.68 us
    ppermute x1, waiting for transfers between devices, on_device(): far = lax.ppermute(edge, LON, swaps)  3.26 us
    ppermute x1, starting transfers between devices, on_device(): outer = lax.ppermute(outer, EVERY, outer_pairs(lat_count, lon_count))  2.69 us
    ppermute x1, starting transfers between devices, on_device(): far = lax.ppermute(edge, LON, swaps)  2.55 us
  transfers between devices with their start and end apart: 5, of which 3 were waited for; matrix products, arithmetic and copies ran while one was open for 1% of the time, Pallas kernels for 15%

profile of v6, /device:TPU:1, one launch (start us, length us, event | category | flops | bytes accessed | tf_op | source)
XLA Modules:
  0.0 63.5 jit_solution(12149868117024462416)
XLA Ops:
  0.6 0.0 copy-start
  0.6 1.4 %shard_map.58 = (bf16[192,128]{1,0:T(8,128)(2,1)S(1)}, bf16[192,128]{1,0:T(8,128)(2,1)S(1)}, bf16[2048,128]{1,0:T(8,128)(2,1)S(1)}, bf16[2048,128]{1,0:T(8,128)(2,1)S(1)}) custom-call(bf16[2048,128]{1,0:T(8,128)(2,1)} %bitcast.20, bf16[2048,128]{1,0:T(8,128)(2,1)} %bitcast.21), custom_call_target="tpu_custom_call" | custom-call | bytes 2195456 | tf_op jit(solution)/shard_map/pallas_call | solution.py:39
  2.1 2.7 %collective-permute-start = (bf16[192,128]{1,0:T(8,128)(2,1)S(1)}, bf16[192,128]{1,0:T(8,128)(2,1)S(1)}, u32[]{:S(2)}, u32[]{:S(2)}) collective-permute-start(bf16[192,128]{1,0:T(8,128)(2,1)S(1)} %get-tuple-element.25), channel_id=1, source_target_pairs={{0,8},{1,9},{2,10},{3,11},{4,12},{5,13},{6,14},{7,15},{8,0},{9,1},... | collective-permute-start | bytes 147464 | tf_op jit(solution)/shard_map/ppermute | solution.py:335
  4.8 6.1 %collective-permute-start.1 = (bf16[192,128]{1,0:T(8,128)(2,1)S(1)}, bf16[192,128]{1,0:T(8,128)(2,1)S(1)}, u32[]{:S(2)}, u32[]{:S(2)}) collective-permute-start(bf16[192,128]{1,0:T(8,128)(2,1)S(1)} %get-tuple-element.26), channel_id=1, source_target_pairs={{0,16},{16,0},{32,48},{48,32},{64,80},{80,64},{96,112},{112,96},{1... | collective-permute-start | bytes 147464 | tf_op jit(solution)/shard_map/ppermute | solution.py:336
  10.9 0.0 copy-done
  10.9 0.1 copy.10
  11.0 0.1 copy.11.w_ref
  11.2 1.7 %shard_map.59 = (bf16[32,64,128]{2,1,0:T(8,128)(2,1)S(1)}, bf16[32,64,128]{2,1,0:T(8,128)(2,1)S(1)}, bf16[128,128]{1,0:T(8,128)(2,1)S(1)}) custom-call(bf16[2048,128]{1,0:T(8,128)(2,1)S(1)} %get-tuple-element.19.f_ref, bf16[2048,128]{1,0:T(8,128)(2,1)S(1)} %get-tuple-element.20.g_ref), custom_call_target="tpu_custom_call" | custom-call | bytes 2129920 | tf_op jit(solution)/shard_map/pallas_call | solution.py:39
  12.8 2.7 %shard_map.60 = (bf16[30,64,128]{2,1,0:T(8,128)(2,1)S(1)}, bf16[30,64,128]{2,1,0:T(8,128)(2,1)S(1)}, f32[64,576]{1,0:T(8,128)S(1)}, f32[8,128]{1,0:T(8,128)S(1)}) custom-call(bf16[32,64,128]{2,1,0:T(8,128)(2,1)S(1)} %get-tuple-element.21.fr_ref, bf16[32,64,128]{2,1,0:T(8,128)(2,1)S(1)} %get-tuple-element.22.gr_ref, bf16[64,576]{1,0:T(8,128)(2,1)S(1)} %copy.11.w_ref), custom_call_target="tpu_custom_call" | custom-call | flops 603979776 | bytes 2256896 | tf_op jit(solution)/shard_map/pallas_call | solution.py:39
  15.5 0.0 collective-permute-done.outer_ref
  15.5 0.0 collective-permute-done.1.inner_ref
  15.5 0.1 shard_map.61.edge_ref
  15.6 2.5 %collective-permute-start.2 = (bf16[192,128]{1,0:T(8,128)(2,1)S(1)}, bf16[192,128]{1,0:T(8,128)(2,1)S(1)}, u32[]{:S(2)}, u32[]{:S(2)}) collective-permute-start(bf16[192,128]{1,0:T(8,128)(2,1)S(1)} %shard_map.61.edge_ref), channel_id=1, source_target_pairs={{0,15},{1,2},{2,1},{3,4},{4,3},{5,6},{6,5},{7,8},{8,7},{9,10},{10,... | collective-permute-start | bytes 147464 | tf_op jit(solution)/shard_map/ppermute | solution.py:365
  18.2 1.0 %collective-permute-start.3 = (bf16[192,128]{1,0:T(8,128)(2,1)S(1)}, bf16[192,128]{1,0:T(8,128)(2,1)S(1)}, u32[]{:S(2)}, u32[]{:S(2)}) collective-permute-start(bf16[192,128]{1,0:T(8,128)(2,1)S(1)} %shard_map.61.edge_ref), channel_id=1, source_target_pairs={{0,1},{1,0},{2,3},{3,2},{4,5},{5,4},{6,7},{7,6},{8,9},{9,8},{10,11... | collective-permute-start | bytes 147464 | tf_op jit(solution)/shard_map/ppermute | solution.py:366
  19.1 0.1 copy.12
  19.3 0.2 reshape.36.wa_ref
  19.4 3.3 %collective-permute-done.2.far_ref = bf16[192,128]{1,0:T(8,128)(2,1)S(1)} collective-permute-done((bf16[192,128]{1,0:T(8,128)(2,1)S(1)}, bf16[192,128]{1,0:T(8,128)(2,1)S(1)}, u32[]{:S(2)}, u32[]{:S(2)}) %collective-permute-start.2) | collective-permute-done | bytes 49184 | tf_op jit(solution)/shard_map/ppermute | solution.py:365
  22.7 0.6 collective-permute-done.3.near_ref
  23.3 0.9 %shard_map.62 = (bf16[2,64,128]{2,1,0:T(8,128)(2,1)S(1)}, bf16[64,128]{1,0:T(8,128)(2,1)S(1)}, bf16[4,64,128]{2,1,0:T(8,128)(2,1)S(1)}, bf16[64,384]{1,0:T(8,128)(2,1)S(1)}, f32[32,1,1152]{2,1,0:T(1,128)S(1)}) custom-call(bf16[32,64,128]{2,1,0:T(8,128)(2,1)S(1)} %get-tuple-element.21.fr_ref, bf16[32,64,128]{2,1,0:T(8,128)(2,1)S(1)} %get-tuple-element.22.gr_ref, ...), custom_call_target="tpu_custom_call" | custom-call | flops 75497472 | bytes 1900544 | tf_op jit(solution)/shard_map/pallas_call | solution.py:39
  24.3 13.3 %all_to_all.15.parts_ref = f32[32,1,1152]{2,1,0:T(1,128)S(1)} all-to-all(f32[32,1,1152]{2,1,0:T(1,128)S(1)} %get-tuple-element.31), channel_id=1, replica_groups=mesh['lat'=16,'z'=8,'side'=2] {'lat','side'}, dimensions={0} | all-to-all | bytes 294912 | tf_op jit(solution)/shard_map/all_to_all | solution.py:385
  37.6 0.1 shard_map.64
  37.7 10.9 %all_to_all.16.after_ref.parts_ref = f32[8,1,1152]{2,1,0:T(1,128)S(1)} all-to-all(f32[8,1,1152]{2,1,0:T(1,128)S(1)} %shard_map.64), channel_id=1, replica_groups=mesh['lat'=16,'z'=8,'side'=2] {'z'}, dimensions={0} | all-to-all | bytes 73728 | tf_op jit(solution)/shard_map/all_to_all | solution.py:387
  48.6 0.7 %shard_map.66 = f32[32,1,1152]{2,1,0:T(1,128)} custom-call(f32[8,1,1152]{2,1,0:T(1,128)S(1)} %all_to_all.16.after_ref.parts_ref), custom_call_target="tpu_custom_call" | custom-call | bytes 184320 | tf_op jit(solution)/shard_map/pallas_call | solution.py:39
  49.3 5.7 %all-to-all-start.2 = ((f32[32,1,1152]{2,1,0:T(1,128)}), f32[32,1,1152]{2,1,0:T(1,128)S(1)}, u32[]{:S(2)}, u32[]{:S(2)}) async-start(f32[32,1,1152]{2,1,0:T(1,128)} %shard_map.66), calls=%async_computation.2 | async-start | bytes 294912 | tf_op jit(solution)/shard_map/all_to_all | solution.py:395
  55.0 0.1 copy.15.wb3_ref
  55.1 0.1 copy.14.wb_ref
  55.3 1.9 %shard_map.63 = bf16[2048,128]{1,0:T(8,128)(2,1)} custom-call(bf16[30,64,128]{2,1,0:T(8,128)(2,1)S(1)} %get-tuple-element.23.mid_ref, bf16[2,64,128]{2,1,0:T(8,128)(2,1)S(1)} %get-tuple-element.29.rim_ref, bf16[64,128]{1,0:T(8,128)(2,1)S(1)} %get-tuple-element.30.strip_ref), custom_call_target="tpu_custom_call" | custom-call | bytes 1064960 | tf_op jit(solution)/shard_map/pallas_call | solution.py:39
  57.2 3.2 %shard_map.65 = bf16[2048,128]{1,0:T(8,128)(2,1)} custom-call(f32[8,1,1152]{2,1,0:T(1,128)S(1)} %all_to_all.16.after_ref.parts_ref, bf16[30,64,128]{2,1,0:T(8,128)(2,1)S(1)} %get-tuple-element.32.mid_ref, bf16[4,64,128]{2,1,0:T(8,128)(2,1)S(1)} %get-tuple-element.33.rim_ref, bf16[64,384]{1,0:T(8,128)(2,1)S(1)} %get-tuple-element.34.dstrip_ref, ...), custom_call_target="tpu_custom_call" | custom-call | flops 301989888 | bytes 1839104 | tf_op jit(solution)/shard_map/pallas_call | solution.py:39
  60.4 2.2 %all-to-all-done.2.parts_ref = f32[32,1,1152]{2,1,0:T(1,128)S(1)} async-done(((f32[32,1,1152]{2,1,0:T(1,128)}), f32[32,1,1152]{2,1,0:T(1,128)S(1)}, u32[]{:S(2)}, u32[]{:S(2)}) %all-to-all-start.2) | async-done | bytes 147488 | tf_op jit(solution)/shard_map/all_to_all | solution.py:395
  62.7 0.9 %shard_map.67 = f32[9,64,64]{2,1,0:T(8,128)} custom-call(f32[32,1,1152]{2,1,0:T(1,128)S(1)} %all-to-all-done.2.parts_ref), custom_call_target="tpu_custom_call" | custom-call | bytes 294912 | tf_op jit(solution)/shard_map/pallas_call | solution.py:39
  (1 shorter events, 0.0 us)
Async XLA Ops:
  0.6 10.2 %copy-start = (bf16[3,3,64,64]{3,2,1,0:T(8,128)(2,1)S(1)}, bf16[3,3,64,64]{3,2,1,0:T(8,128)(2,1)}, u32[]{:S(2)}) copy-start(bf16[3,3,64,64]{3,2,1,0:T(8,128)(2,1)} %param.4) | copy-start | bytes 221188
  2.1 13.4 %collective-permute-start = (bf16[192,128]{1,0:T(8,128)(2,1)S(1)}, bf16[192,128]{1,0:T(8,128)(2,1)S(1)}, u32[]{:S(2)}, u32[]{:S(2)}) collective-permute-start(bf16[192,128]{1,0:T(8,128)(2,1)S(1)} %get-tuple-element.25), channel_id=1, source_target_pairs={{0,8},{1,9},{2,10},{3,11},{4,12},{5,13},{6,14},{7,15},{8,0},{9,1},... | collective-permute-start | bytes 147464 | tf_op jit(solution)/shard_map/ppermute | solution.py:335
  4.8 10.7 %collective-permute-start.1 = (bf16[192,128]{1,0:T(8,128)(2,1)S(1)}, bf16[192,128]{1,0:T(8,128)(2,1)S(1)}, u32[]{:S(2)}, u32[]{:S(2)}) collective-permute-start(bf16[192,128]{1,0:T(8,128)(2,1)S(1)} %get-tuple-element.26), channel_id=1, source_target_pairs={{0,16},{16,0},{32,48},{48,32},{64,80},{80,64},{96,112},{112,96},{1... | collective-permute-start | bytes 147464 | tf_op jit(solution)/shard_map/ppermute | solution.py:336
  15.6 7.1 %collective-permute-start.2 = (bf16[192,128]{1,0:T(8,128)(2,1)S(1)}, bf16[192,128]{1,0:T(8,128)(2,1)S(1)}, u32[]{:S(2)}, u32[]{:S(2)}) collective-permute-start(bf16[192,128]{1,0:T(8,128)(2,1)S(1)} %shard_map.61.edge_ref), channel_id=1, source_target_pairs={{0,15},{1,2},{2,1},{3,4},{4,3},{5,6},{6,5},{7,8},{8,7},{9,10},{10,... | collective-permute-start | bytes 147464 | tf_op jit(solution)/shard_map/ppermute | solution.py:365
  18.2 5.1 %collective-permute-start.3 = (bf16[192,128]{1,0:T(8,128)(2,1)S(1)}, bf16[192,128]{1,0:T(8,128)(2,1)S(1)}, u32[]{:S(2)}, u32[]{:S(2)}) collective-permute-start(bf16[192,128]{1,0:T(8,128)(2,1)S(1)} %shard_map.61.edge_ref), channel_id=1, source_target_pairs={{0,1},{1,0},{2,3},{3,2},{4,5},{5,4},{6,7},{7,6},{8,9},{9,8},{10,11... | collective-permute-start | bytes 147464 | tf_op jit(solution)/shard_map/ppermute | solution.py:366
  49.3 13.4 %all-to-all-start.2 = ((f32[32,1,1152]{2,1,0:T(1,128)}), f32[32,1,1152]{2,1,0:T(1,128)S(1)}, u32[]{:S(2)}, u32[]{:S(2)}) async-start(f32[32,1,1152]{2,1,0:T(1,128)} %shard_map.66), calls=%async_computation.2 | async-start | bytes 294912 | tf_op jit(solution)/shard_map/all_to_all | solution.py:395

commit v7 on v6

--- a/solution.py
+++ b/solution.py
@@ -33,14 +33,14 @@
     return lax.broadcasted_iota(jnp.int32, (CH, width), 1)
 
 
-def call(body, out_shape, args, scratch=(), flops=0, space=pltpu.VMEM, limit=24):
+def call(body, out_shape, args, scratch=(), flops=0, space=pltpu.VMEM, out_space=pltpu.VMEM, limit=24):
     outs = [jax.ShapeDtypeStruct(s, d) for s, d in out_shape]
     size = sum(a.size * a.dtype.itemsize for a in list(args) + outs)
     return pl.pallas_call(
         body,
         out_shape=outs,
         in_specs=[pl.BlockSpec(memory_space=space)] * len(args),
-        out_specs=[pl.BlockSpec(memory_space=pltpu.VMEM)] * len(outs),
+        out_specs=[pl.BlockSpec(memory_space=out_space)] * len(outs),
         scratch_shapes=list(scratch),
         cost_estimate=pl.CostEstimate(flops=flops, bytes_accessed=size, transcendentals=0),
         compiler_params=pltpu.CompilerParams(vmem_limit_bytes=int(limit * 2**20)),
@@ -91,23 +91,51 @@
     return [half[i * CH : (i + 1) * CH] for half in (north, south) for i in range(3)]
 
 
-def edge_body(edge_ref, outer_ref, inner_ref, token_ref, out_ref):
-    n_near, n_far, n_cot, s_near, s_far, s_cot = row_halos(outer_ref, inner_ref)
-    lane = lanes()
-    low = jnp.where(lane < 4, roll(s_near, 2), jnp.where(lane < 8, roll(s_far, 6), roll(s_cot, 10)))
-    high = jnp.where(
-        lane >= 124, roll(n_near, 126), jnp.where(lane >= 120, roll(n_far, 122), roll(n_cot, 118))
-    )
-    out_ref[pl.ds(0, 2 * CH), :] = edge_ref[...]
-    out_ref[pl.ds(2 * CH, CH), :] = jnp.where(lane < 64, low, high).astype(bf16)
-
-
-def strip(near_ref, far_ref, part):
-    at = pl.ds(part * CH, CH)
-    near = near_ref[at, :].astype(f32)
-    far = far_ref[at, :].astype(f32)
+CORNERS = (
+    ("s_near", 0, 0), ("s_near", 0, 1), ("s_cot", 0, 2), ("s_far", 4, 0), ("s_far", 4, 1),
+    ("n_far", 120, 0), ("n_far", 120, 1), ("n_near", 124, 0), ("n_near", 124, 1), ("n_cot", 124, 2),
+)
+
+
+def edge_body(edge_ref, outer_ref, inner_ref, token_ref, far_ref, near_ref):
+    names = ("n_near", "n_far", "n_cot", "s_near", "s_far", "s_cot")
+    halos = dict(zip(names, row_halos(outer_ref, inner_ref)))
+    kind = lanes() % 4
+    lane = lanes()
+    field = edge_ref[pl.ds(0, CH), :].astype(f32)
+    cot = edge_ref[pl.ds(CH, CH), :].astype(f32)
+    east = jnp.where(kind < 2, field, roll(cot, 1))
+    west = jnp.where(kind >= 2, field, roll(cot, -1))
+    for slot, (row, _, column) in enumerate(CORNERS):
+        value = halos[row]
+        to = 4 * slot + 3
+        east = jnp.where(lane == to, roll(value, to - (126, 127, 127)[column]), east)
+        to = 4 * slot
+        west = jnp.where(lane == to, roll(value, to - (0, 1, 0)[column]), west)
     even = lax.axis_index("side") == 0
-    return jnp.where(lanes() % 4 < 2, jnp.where(even, far, near), jnp.where(even, near, far))
+    far_ref[...] = jnp.where(even, west, east).astype(bf16)
+    near_ref[...] = jnp.where(even, east, west).astype(bf16)
+
+
+def column_halos(far_ref, near_ref):
+    even = lax.axis_index("side") == 0
+    far = far_ref[...].astype(f32)
+    near = near_ref[...].astype(f32)
+    west = jnp.where(even, far, near)
+    east = jnp.where(even, near, far)
+    lane = lanes()
+    low = lane % 4 < 2
+    field = jnp.where(low, west, east)
+    cot = jnp.where(low, roll(west, -1), roll(east, 1))
+    beyond = [jnp.zeros((CH, COLS), f32), jnp.zeros((CH, COLS), f32)]
+    for slot, (_, base, column) in enumerate(CORNERS):
+        at = column // 2
+        for src, start, to in (
+            (west, 4 * slot + 3, base + (0, 1, 1)[column]),
+            (east, 4 * slot, base + (2, 3, 2)[column]),
+        ):
+            beyond[at] = jnp.where(lane == to, roll(src, to - start), beyond[at])
+    return field, cot, beyond[0], beyond[1]
 
 
 def stack_taps(out_ref, at, own, halo, lane):
@@ -162,10 +190,7 @@
     lane = lanes()
     n_near, n_far, n_cot, s_near, s_far, s_cot = row_halos(outer_ref, inner_ref)
 
-    s = strip(near_ref, far_ref, 0)
-    gs = strip(near_ref, far_ref, 1)
-    beyond = strip(near_ref, far_ref, 2)
-    gbeyond = jnp.where(lane < 64, roll(beyond, 120), roll(beyond, 8))
+    s, gs, beyond, gbeyond = column_halos(far_ref, near_ref)
 
     end = ROWS - 1
     stack_taps(xs, 0, n_far, roll(beyond, -122), lane)
@@ -197,7 +222,9 @@
 
     edge = edge_ref[pl.ds(0, CH), :].astype(f32)
     halo = jnp.concatenate([s, beyond], 1)
-    own = jnp.concatenate([edge, edge_ref[pl.ds(2 * CH, CH), :].astype(f32)], 1)
+    low = jnp.where(lane < 4, roll(s_near, 2), roll(s_far, 6))
+    high = jnp.where(lane >= 124, roll(n_near, 126), roll(n_far, 122))
+    own = jnp.concatenate([edge, jnp.where(lane < 64, low, high)], 1)
     wide_lane = lanes(2 * COLS)
     kind = wide_lane % 4
     small = lane % 4
@@ -293,14 +320,19 @@
         out_ref[i] = total
 
 
-def unpack_body(parts_ref, out_ref):
+def unpack_body(parts_ref, out_hbm, out_ref, sems):
     count = parts_ref.shape[0]
+    copies = []
     for tap in range(9):
         at = tap // 2
         width = min(COLS, 9 * CH - at * COLS)
         for j in range(CH // count):
             start = at * COLS * CH // count + j * width + (tap % 2) * CH
             out_ref[tap, pl.ds(j * count, count), :] = parts_ref[:, 0, pl.ds(start, CH)]
+        copies.append(pltpu.make_async_copy(out_ref.at[tap], out_hbm.at[tap], sems.at[tap]))
+        copies[-1].start()
+    for copy in copies:
+        copy.wait()
 
 
 def outer_pairs(lat_count, lon_count):
@@ -360,10 +392,10 @@
         2 * conv_flops,
     )
 
-    (edge,) = call(edge_body, [((TAPS, COLS), bf16)], (edge, outer, inner, token))
+    far, near = call(edge_body, [((CH, COLS), bf16)] * 2, (edge, outer, inner, token))
     swaps = [(i, (i + 1 if i % 2 else i - 1) % lon_count) for i in range(lon_count)]
-    far = lax.ppermute(edge, LON, swaps)
-    near = lax.ppermute(edge, "side", [(0, 1), (1, 0)])
+    far = lax.ppermute(far, LON, swaps)
+    near = lax.ppermute(near, "side", [(0, 1), (1, 0)])
 
     out_rim, out_strip, delta_rim, dstrip, grad = call(
         border_body,
@@ -393,7 +425,13 @@
         conv_flops,
     )
     parts = lax.all_to_all(spread(parts, plane), PLANE, 0, 0)
-    (grad_kernel,) = call(unpack_body, [((9, CH, CH), f32)], (parts,))
+    (grad_kernel,) = call(
+        unpack_body,
+        [((9, CH, CH), f32)],
+        (parts,),
+        [pltpu.VMEM((9, CH, CH), f32), pltpu.SemaphoreType.DMA((9,))],
+        out_space=pl.ANY,
+    )
     shape = field.shape
     return (output.reshape(shape), grad_input.reshape(shape), grad_kernel.reshape(kernel.shape))
 

time: 63.8 us -> 63.6 us (level)
  waiting for transfers between devices: 6.11 us -> 5.36 us
    ppermute x2, waiting for transfers between devices: 3.89 us -> 3.14 us  [the longest x1 2.48 us: on_device(): far = lax.ppermute(far, LON, swaps)]
where the time goes in v7:
time: 63.6 us; the launch traced here: 63.4 us
  blocking collectives  24.6 us (39%)
  starting transfers between devices  18 us (28%)
  Pallas kernels  13.8 us (22%)
  waiting for transfers between devices  5.36 us (8%)
  local copies, waits for them, and re-layouts  0.87 us (1%)
  between operations  0.72 us (1%)
    pallas_call x10, Pallas kernels, call(): pl.pallas_call(body, out_shape=outs, in_specs=[pl.BlockSpec(memory_space=...  13.8 us
    all_to_all x1, blocking collectives, on_device(): parts = lax.all_to_all(grad, PLANE, 0, 0)  13.7 us
    all_to_all x1, blocking collectives, on_device(): parts = lax.all_to_all(spread(parts, lax.axis_size('z')), 'z', 0, 0)  10.9 us
    ppermute x1, starting transfers between devices, on_device(): inner = lax.ppermute(inner, 'lat', [(i, i ^ 1) for i in range(lat_count)])  6.09 us
    all_to_all x1, starting transfers between devices, on_device(): parts = lax.all_to_all(spread(parts, plane), PLANE, 0, 0)  5.67 us
    ppermute x1, starting transfers between devices, on_device(): outer = lax.ppermute(outer, EVERY, outer_pairs(lat_count, lon_count))  2.69 us
    ppermute x1, starting transfers between devices, on_device(): far = lax.ppermute(far, LON, swaps)  2.55 us
    ppermute x1, waiting for transfers between devices, on_device(): far = lax.ppermute(far, LON, swaps)  2.48 us
  transfers between devices with their start and end apart: 5, of which 3 were waited for; matrix products, arithmetic and copies ran while one was open for 1% of the time, Pallas kernels for 15%

profile of v7, /device:TPU:1, one launch (start us, length us, event | category | flops | bytes accessed | tf_op | source)
XLA Modules:
  0.0 63.4 jit_solution(1205070247862024860)
XLA Ops:
  0.6 0.0 copy-start
  0.6 1.4 %shard_map.58 = (bf16[192,128]{1,0:T(8,128)(2,1)S(1)}, bf16[192,128]{1,0:T(8,128)(2,1)S(1)}, bf16[2048,128]{1,0:T(8,128)(2,1)S(1)}, bf16[2048,128]{1,0:T(8,128)(2,1)S(1)}) custom-call(bf16[2048,128]{1,0:T(8,128)(2,1)} %bitcast.20, bf16[2048,128]{1,0:T(8,128)(2,1)} %bitcast.21), custom_call_target="tpu_custom_call" | custom-call | bytes 2195456 | tf_op jit(solution)/shard_map/pallas_call | solution.py:39
  2.1 2.7 %collective-permute-start = (bf16[192,128]{1,0:T(8,128)(2,1)S(1)}, bf16[192,128]{1,0:T(8,128)(2,1)S(1)}, u32[]{:S(2)}, u32[]{:S(2)}) collective-permute-start(bf16[192,128]{1,0:T(8,128)(2,1)S(1)} %get-tuple-element.27), channel_id=1, source_target_pairs={{0,8},{1,9},{2,10},{3,11},{4,12},{5,13},{6,14},{7,15},{8,0},{9,1},... | collective-permute-start | bytes 147464 | tf_op jit(solution)/shard_map/ppermute | solution.py:367
  4.8 6.1 %collective-permute-start.1 = (bf16[192,128]{1,0:T(8,128)(2,1)S(1)}, bf16[192,128]{1,0:T(8,128)(2,1)S(1)}, u32[]{:S(2)}, u32[]{:S(2)}) collective-permute-start(bf16[192,128]{1,0:T(8,128)(2,1)S(1)} %get-tuple-element.28), channel_id=1, source_target_pairs={{0,16},{16,0},{32,48},{48,32},{64,80},{80,64},{96,112},{112,96},{1... | collective-permute-start | bytes 147464 | tf_op jit(solution)/shard_map/ppermute | solution.py:368
  10.9 0.0 copy-done
  10.9 0.1 copy.10
  11.0 0.1 copy.11.w_ref
  11.2 1.7 %shard_map.59 = (bf16[32,64,128]{2,1,0:T(8,128)(2,1)S(1)}, bf16[32,64,128]{2,1,0:T(8,128)(2,1)S(1)}, bf16[128,128]{1,0:T(8,128)(2,1)S(1)}) custom-call(bf16[2048,128]{1,0:T(8,128)(2,1)S(1)} %get-tuple-element.21.f_ref, bf16[2048,128]{1,0:T(8,128)(2,1)S(1)} %get-tuple-element.22.g_ref), custom_call_target="tpu_custom_call" | custom-call | bytes 2129920 | tf_op jit(solution)/shard_map/pallas_call | solution.py:39
  12.8 2.7 %shard_map.60 = (bf16[30,64,128]{2,1,0:T(8,128)(2,1)S(1)}, bf16[30,64,128]{2,1,0:T(8,128)(2,1)S(1)}, f32[64,576]{1,0:T(8,128)S(1)}, f32[8,128]{1,0:T(8,128)S(1)}) custom-call(bf16[32,64,128]{2,1,0:T(8,128)(2,1)S(1)} %get-tuple-element.23.fr_ref, bf16[32,64,128]{2,1,0:T(8,128)(2,1)S(1)} %get-tuple-element.24.gr_ref, bf16[64,576]{1,0:T(8,128)(2,1)S(1)} %copy.11.w_ref), custom_call_target="tpu_custom_call" | custom-call | flops 603979776 | bytes 2256896 | tf_op jit(solution)/shard_map/pallas_call | solution.py:39
  15.5 0.0 collective-permute-done.outer_ref
  15.5 0.0 collective-permute-done.1.inner_ref
  15.5 0.2 shard_map.61
  15.7 2.5 %collective-permute-start.2 = (bf16[64,128]{1,0:T(8,128)(2,1)S(1)}, bf16[64,128]{1,0:T(8,128)(2,1)S(1)}, u32[]{:S(2)}, u32[]{:S(2)}) collective-permute-start(bf16[64,128]{1,0:T(8,128)(2,1)S(1)} %get-tuple-element.30), channel_id=1, source_target_pairs={{0,15},{1,2},{2,1},{3,4},{4,3},{5,6},{6,5},{7,8},{8,7},{9,10},{10,... | collective-permute-start | bytes 49160 | tf_op jit(solution)/shard_map/ppermute | solution.py:397
  18.2 1.0 %collective-permute-start.3 = (bf16[64,128]{1,0:T(8,128)(2,1)S(1)}, bf16[64,128]{1,0:T(8,128)(2,1)S(1)}, u32[]{:S(2)}, u32[]{:S(2)}) collective-permute-start(bf16[64,128]{1,0:T(8,128)(2,1)S(1)} %get-tuple-element.31), channel_id=1, source_target_pairs={{0,1},{1,0},{2,3},{3,2},{4,5},{5,4},{6,7},{7,6},{8,9},{9,8},{10,11... | collective-permute-start | bytes 49160 | tf_op jit(solution)/shard_map/ppermute | solution.py:398
  19.2 0.1 copy.12
  19.3 0.2 reshape.36.wa_ref
  19.5 2.5 %collective-permute-done.2.far_ref = bf16[64,128]{1,0:T(8,128)(2,1)S(1)} collective-permute-done((bf16[64,128]{1,0:T(8,128)(2,1)S(1)}, bf16[64,128]{1,0:T(8,128)(2,1)S(1)}, u32[]{:S(2)}, u32[]{:S(2)}) %collective-permute-start.2) | collective-permute-done | bytes 16416 | tf_op jit(solution)/shard_map/ppermute | solution.py:397
  22.0 0.7 %collective-permute-done.3.near_ref = bf16[64,128]{1,0:T(8,128)(2,1)S(1)} collective-permute-done((bf16[64,128]{1,0:T(8,128)(2,1)S(1)}, bf16[64,128]{1,0:T(8,128)(2,1)S(1)}, u32[]{:S(2)}, u32[]{:S(2)}) %collective-permute-start.3) | collective-permute-done | bytes 16416 | tf_op jit(solution)/shard_map/ppermute | solution.py:398
  22.6 1.1 %shard_map.62 = (bf16[2,64,128]{2,1,0:T(8,128)(2,1)S(1)}, bf16[64,128]{1,0:T(8,128)(2,1)S(1)}, bf16[4,64,128]{2,1,0:T(8,128)(2,1)S(1)}, bf16[64,384]{1,0:T(8,128)(2,1)S(1)}, f32[32,1,1152]{2,1,0:T(1,128)S(1)}) custom-call(bf16[32,64,128]{2,1,0:T(8,128)(2,1)S(1)} %get-tuple-element.23.fr_ref, bf16[32,64,128]{2,1,0:T(8,128)(2,1)S(1)} %get-tuple-element.24.gr_ref, ...), custom_call_target="tpu_custom_call" | custom-call | flops 75497472 | bytes 1818624 | tf_op jit(solution)/shard_map/pallas_call | solution.py:39
  23.7 13.7 %all_to_all.15.parts_ref = f32[32,1,1152]{2,1,0:T(1,128)S(1)} all-to-all(f32[32,1,1152]{2,1,0:T(1,128)S(1)} %get-tuple-element.35), channel_id=1, replica_groups=mesh['lat'=16,'z'=8,'side'=2] {'lat','side'}, dimensions={0} | all-to-all | bytes 294912 | tf_op jit(solution)/shard_map/all_to_all | solution.py:417
  37.4 0.1 shard_map.64
  37.5 10.9 %all_to_all.16.after_ref.parts_ref = f32[8,1,1152]{2,1,0:T(1,128)S(1)} all-to-all(f32[8,1,1152]{2,1,0:T(1,128)S(1)} %shard_map.64), channel_id=1, replica_groups=mesh['lat'=16,'z'=8,'side'=2] {'z'}, dimensions={0} | all-to-all | bytes 73728 | tf_op jit(solution)/shard_map/all_to_all | solution.py:419
  48.4 0.7 %shard_map.66 = f32[32,1,1152]{2,1,0:T(1,128)} custom-call(f32[8,1,1152]{2,1,0:T(1,128)S(1)} %all_to_all.16.after_ref.parts_ref), custom_call_target="tpu_custom_call" | custom-call | bytes 184320 | tf_op jit(solution)/shard_map/pallas_call | solution.py:39
  49.1 5.7 %all-to-all-start.2 = ((f32[32,1,1152]{2,1,0:T(1,128)}), f32[32,1,1152]{2,1,0:T(1,128)S(1)}, u32[]{:S(2)}, u32[]{:S(2)}) async-start(f32[32,1,1152]{2,1,0:T(1,128)} %shard_map.66), calls=%async_computation.2 | async-start | bytes 294912 | tf_op jit(solution)/shard_map/all_to_all | solution.py:427
  54.8 0.1 copy.15.wb3_ref
  55.0 0.1 copy.14.wb_ref
  55.1 1.9 %shard_map.63 = bf16[2048,128]{1,0:T(8,128)(2,1)} custom-call(bf16[30,64,128]{2,1,0:T(8,128)(2,1)S(1)} %get-tuple-element.25.mid_ref, bf16[2,64,128]{2,1,0:T(8,128)(2,1)S(1)} %get-tuple-element.33.rim_ref, bf16[64,128]{1,0:T(8,128)(2,1)S(1)} %get-tuple-element.34.strip_ref), custom_call_target="tpu_custom_call" | custom-call | bytes 1064960 | tf_op jit(solution)/shard_map/pallas_call | solution.py:39
  57.1 3.2 %shard_map.65 = bf16[2048,128]{1,0:T(8,128)(2,1)} custom-call(f32[8,1,1152]{2,1,0:T(1,128)S(1)} %all_to_all.16.after_ref.parts_ref, bf16[30,64,128]{2,1,0:T(8,128)(2,1)S(1)} %get-tuple-element.36.mid_ref, bf16[4,64,128]{2,1,0:T(8,128)(2,1)S(1)} %get-tuple-element.37.rim_ref, bf16[64,384]{1,0:T(8,128)(2,1)S(1)} %get-tuple-element.38.dstrip_ref, ...), custom_call_target="tpu_custom_call" | custom-call | flops 301989888 | bytes 1839104 | tf_op jit(solution)/shard_map/pallas_call | solution.py:39
  60.3 2.2 %all-to-all-done.2.parts_ref = f32[32,1,1152]{2,1,0:T(1,128)S(1)} async-done(((f32[32,1,1152]{2,1,0:T(1,128)}), f32[32,1,1152]{2,1,0:T(1,128)S(1)}, u32[]{:S(2)}, u32[]{:S(2)}) %all-to-all-start.2) | async-done | bytes 147488 | tf_op jit(solution)/shard_map/all_to_all | solution.py:427
  62.5 0.9 %shard_map.67 = f32[9,64,64]{2,1,0:T(8,128)} custom-call(f32[32,1,1152]{2,1,0:T(1,128)S(1)} %all-to-all-done.2.parts_ref), custom_call_target="tpu_custom_call" | custom-call | bytes 294912 | tf_op jit(solution)/shard_map/pallas_call | solution.py:39
  (1 shorter events, 0.0 us)
Async XLA Ops:
  0.6 10.2 %copy-start = (bf16[3,3,64,64]{3,2,1,0:T(8,128)(2,1)S(1)}, bf16[3,3,64,64]{3,2,1,0:T(8,128)(2,1)}, u32[]{:S(2)}) copy-start(bf16[3,3,64,64]{3,2,1,0:T(8,128)(2,1)} %param.4) | copy-start | bytes 221188
  2.1 13.4 %collective-permute-start = (bf16[192,128]{1,0:T(8,128)(2,1)S(1)}, bf16[192,128]{1,0:T(8,128)(2,1)S(1)}, u32[]{:S(2)}, u32[]{:S(2)}) collective-permute-start(bf16[192,128]{1,0:T(8,128)(2,1)S(1)} %get-tuple-element.27), channel_id=1, source_target_pairs={{0,8},{1,9},{2,10},{3,11},{4,12},{5,13},{6,14},{7,15},{8,0},{9,1},... | collective-permute-start | bytes 147464 | tf_op jit(solution)/shard_map/ppermute | solution.py:367
  4.8 10.7 %collective-permute-start.1 = (bf16[192,128]{1,0:T(8,128)(2,1)S(1)}, bf16[192,128]{1,0:T(8,128)(2,1)S(1)}, u32[]{:S(2)}, u32[]{:S(2)}) collective-permute-start(bf16[192,128]{1,0:T(8,128)(2,1)S(1)} %get-tuple-element.28), channel_id=1, source_target_pairs={{0,16},{16,0},{32,48},{48,32},{64,80},{80,64},{96,112},{112,96},{1... | collective-permute-start | bytes 147464 | tf_op jit(solution)/shard_map/ppermute | solution.py:368
  15.7 6.3 %collective-permute-start.2 = (bf16[64,128]{1,0:T(8,128)(2,1)S(1)}, bf16[64,128]{1,0:T(8,128)(2,1)S(1)}, u32[]{:S(2)}, u32[]{:S(2)}) collective-permute-start(bf16[64,128]{1,0:T(8,128)(2,1)S(1)} %get-tuple-element.30), channel_id=1, source_target_pairs={{0,15},{1,2},{2,1},{3,4},{4,3},{5,6},{6,5},{7,8},{8,7},{9,10},{10,... | collective-permute-start | bytes 49160 | tf_op jit(solution)/shard_map/ppermute | solution.py:397
  18.2 4.4 %collective-permute-start.3 = (bf16[64,128]{1,0:T(8,128)(2,1)S(1)}, bf16[64,128]{1,0:T(8,128)(2,1)S(1)}, u32[]{:S(2)}, u32[]{:S(2)}) collective-permute-start(bf16[64,128]{1,0:T(8,128)(2,1)S(1)} %get-tuple-element.31), channel_id=1, source_target_pairs={{0,1},{1,0},{2,3},{3,2},{4,5},{5,4},{6,7},{7,6},{8,9},{9,8},{10,11... | collective-permute-start | bytes 49160 | tf_op jit(solution)/shard_map/ppermute | solution.py:398
  49.1 13.4 %all-to-all-start.2 = ((f32[32,1,1152]{2,1,0:T(1,128)}), f32[32,1,1152]{2,1,0:T(1,128)S(1)}, u32[]{:S(2)}, u32[]{:S(2)}) async-start(f32[32,1,1152]{2,1,0:T(1,128)} %shard_map.66), calls=%async_computation.2 | async-start | bytes 294912 | tf_op jit(solution)/shard_map/all_to_all | solution.py:427

commit v8 on v7

--- a/solution.py
+++ b/solution.py
@@ -253,34 +253,50 @@
     left = jnp.concatenate([deltas[0], deltas[1], side], 1)
     total = part_ref[...] + dot_lanes(left, jnp.concatenate([window, shifted], 1))
     total = total * grad_scale()
-    pieces = [total[:, p * COLS : (p + 1) * COLS] for p in range(4)] + [total[:, 4 * COLS :]]
     count = grad_ref.shape[0]
-    for at, piece in enumerate(pieces):
-        for j in range(CH // count):
-            width = piece.shape[1]
-            start = at * COLS * CH // count + j * width
-            grad_ref[:, 0, pl.ds(start, width)] = piece[j * count : (j + 1) * count]
+    pieces = []
+    for p in range(5):
+        piece = total[:, p * COLS : (p + 1) * COLS]
+        pieces.append([piece[j * count : (j + 1) * count] for j in range(CH // count)])
+    tiles = [piece[j] for j in range(CH // count) for piece in pieces[:4]]
+    last = pieces[4]
+    for j in range(0, len(last), 2):
+        tiles.append(jnp.concatenate(last[j : j + 2], 1))
+    for q, tile in enumerate(tiles):
+        grad_ref[:, 0, pl.ds(q * COLS, COLS)] = tile
 
 
 def patched(row, packed, r, lane):
     return jnp.where((lane == 0) | (lane == COLS - 1), roll(packed, -(4 * r + 2)), row.astype(f32))
 
 
-def restore_body(mid_ref, rim_ref, strip_ref, out_ref, wide):
+def write_out(wide, out_hbm, out_ref, sems):
+    part = CH * ROWS // PIECES
+    copies = []
+    for i in range(PIECES):
+        at = pl.ds(i * part, part)
+        out_ref[at, :] = wide[at, :].astype(bf16)
+        copies.append(pltpu.make_async_copy(out_ref.at[at], out_hbm.at[at], sems.at[i]))
+        copies[-1].start()
+    for copy in copies:
+        copy.wait()
+
+
+def restore_body(mid_ref, rim_ref, strip_ref, out_hbm, wide, out_ref, sems):
     lane = lanes()
     packed = strip_ref[...].astype(f32)
     wide[pl.ds(0, CH, stride=ROWS), :] = rim_ref[0].astype(f32)
     for r in range(1, ROWS - 1):
         wide[pl.ds(r, CH, stride=ROWS), :] = patched(mid_ref[r - 1], packed, r, lane)
     wide[pl.ds(ROWS - 1, CH, stride=ROWS), :] = rim_ref[1].astype(f32)
-    out_ref[...] = wide[...].astype(bf16)
+    write_out(wide, out_hbm, out_ref, sems)
 
 
 def grad_scale():
     return float(ROWS * COLS * lax.axis_size(EVERY)) ** (-0.5)
 
 
-def backward_body(after_ref, mid_ref, rim_ref, dstrip_ref, gr_ref, wb_ref, wb3_ref, out_ref, xs, wide):
+def backward_body(after_ref, mid_ref, rim_ref, dstrip_ref, gr_ref, wb_ref, wb3_ref, out_hbm, xs, wide, out_ref, sems):
     lat = lax.axis_index("lat")
     at_top = lat == 0
     at_bottom = lat == lax.axis_size("lat") - 1
@@ -311,24 +327,35 @@
         back = dot(weights, window)
         put(r, back[:, :COLS])
         put(r + 1, back[:, COLS:])
-    out_ref[...] = wide[...].astype(bf16)
+    write_out(wide, out_hbm, out_ref, sems)
 
 
 def fold_body(parts_ref, out_ref):
     total = jnp.sum(parts_ref[...], 0)
+    if out_ref.shape[1] == 2:
+        width = out_ref.shape[2]
+        rest = jnp.zeros((1, 2 * width - total.shape[1]), f32)
+        total = jnp.concatenate([total, rest], 1)
+        total = jnp.concatenate([total[:, :width], total[:, width:]], 0)
+    total = total.astype(out_ref.dtype)
     for i in range(out_ref.shape[0]):
         out_ref[i] = total
 
 
 def unpack_body(parts_ref, out_hbm, out_ref, sems):
     count = parts_ref.shape[0]
+    half = parts_ref.shape[2] // COLS
+    tiles = []
+    for q in range(2 * half):
+        tiles.append(parts_ref[:, q // half, pl.ds(q % half * COLS, COLS)].astype(f32))
     copies = []
     for tap in range(9):
-        at = tap // 2
-        width = min(COLS, 9 * CH - at * COLS)
         for j in range(CH // count):
-            start = at * COLS * CH // count + j * width + (tap % 2) * CH
-            out_ref[tap, pl.ds(j * count, count), :] = parts_ref[:, 0, pl.ds(start, CH)]
+            if tap < 8:
+                tile, at = tiles[4 * j + tap // 2], tap % 2
+            else:
+                tile, at = tiles[4 * (CH // count) + j // 2], j % 2
+            out_ref[tap, pl.ds(j * count, count), :] = tile[:, at * CH : (at + 1) * CH]
         copies.append(pltpu.make_async_copy(out_ref.at[tap], out_hbm.at[tap], sems.at[tap]))
         copies[-1].start()
     for copy in copies:
@@ -378,6 +405,7 @@
     turned = kernel[::-1, ::-1]
     wb3 = jnp.transpose(turned, (0, 3, 1, 2)).reshape(3, CH, TAPS)
     wb = jnp.transpose(turned, (3, 0, 1, 2)).reshape(CH, 3 * TAPS)
+    piece = 9 * CH * CH // plane
     conv_flops = 2 * 9 * CH * CH * ROWS * COLS
     out_mid, delta_mid, grad_mid, token = call(
         interior_body,
@@ -404,27 +432,29 @@
             ((CH, COLS), bf16),
             ((4, CH, COLS), bf16),
             ((CH, 3 * COLS), bf16),
-            ((plane, 1, 9 * CH * CH // plane), f32),
+            ((plane, 1, piece), f32),
         ],
         (fr, gr, edge, far, near, outer, inner, w, w3, grad_mid),
         [pltpu.VMEM((8, TAPS, COLS), bf16)],
         conv_flops // 4,
     )
 
-    def spread(parts, count):
-        return call(fold_body, [((count,) + parts.shape[1:], f32)], (parts,))[0]
-
+    def spread(parts, shape, dtype):
+        return call(fold_body, [(shape, dtype)], (parts,))[0]
+
+    writing = [pltpu.VMEM(flat, f32), pltpu.VMEM(flat, bf16), pltpu.SemaphoreType.DMA((PIECES,))]
     parts = lax.all_to_all(grad, PLANE, 0, 0)
-    (output,) = call(restore_body, [(flat, bf16)], (out_mid, out_rim, out_strip), [pltpu.VMEM(flat, f32)])
-    parts = lax.all_to_all(spread(parts, lax.axis_size("z")), "z", 0, 0)
+    (output,) = call(restore_body, [(flat, bf16)], (out_mid, out_rim, out_strip), writing, out_space=pl.ANY)
+    parts = lax.all_to_all(spread(parts, (lax.axis_size("z"), 1, piece), f32), "z", 0, 0)
     (grad_input,) = call(
         backward_body,
         [(flat, bf16)],
         (parts, delta_mid, delta_rim, dstrip, gr, wb, wb3),
-        [pltpu.VMEM((ROWS + 2, TAPS, COLS), bf16), pltpu.VMEM(flat, f32)],
+        [pltpu.VMEM((ROWS + 2, TAPS, COLS), bf16)] + writing,
         conv_flops,
-    )
-    parts = lax.all_to_all(spread(parts, plane), PLANE, 0, 0)
+        out_space=pl.ANY,
+    )
+    parts = lax.all_to_all(spread(parts, (plane, 2, -(-piece // (2 * COLS)) * COLS), bf16), PLANE, 0, 0)
     (grad_kernel,) = call(
         unpack_body,
         [((9, CH, CH), f32)],

time: 63.6 us -> 63.2 us (level)
  no operation moved by 1% of the time
where the time goes in v8:
time: 63.2 us; the launch traced here: 62.9 us
  blocking collectives  24.6 us (39%)
  starting transfers between devices  18 us (28%)
  Pallas kernels  13.7 us (22%)
  waiting for transfers between devices  5.05 us (8%)
  local copies, waits for them, and re-layouts  0.87 us (1%)
  between operations  0.74 us (1%)
    all_to_all x1, blocking collectives, on_device(): parts = lax.all_to_all(grad, PLANE, 0, 0)  13.7 us
    pallas_call x10, Pallas kernels, call(): pl.pallas_call(body, out_shape=outs, in_specs=[pl.BlockSpec(memory_space=...  13.7 us
    all_to_all x1, blocking collectives, on_device(): lax.all_to_all(spread(parts, (lax.axis_size('z'), 1, piece), f32), 'z', 0...  10.9 us
    ppermute x1, starting transfers between devices, on_device(): inner = lax.ppermute(inner, 'lat', [(i, i ^ 1) for i in range(lat_count)])  6.09 us
    all_to_all x1, starting transfers between devices, on_device(): lax.all_to_all(spread(parts, (plane, 2, -(-piece // (2 * COLS)) * COLS),...  5.67 us
    ppermute x1, starting transfers between devices, on_device(): outer = lax.ppermute(outer, EVERY, outer_pairs(lat_count, lon_count))  2.69 us
    ppermute x1, starting transfers between devices, on_device(): far = lax.ppermute(far, LON, swaps)  2.55 us
    ppermute x1, waiting for transfers between devices, on_device(): far = lax.ppermute(far, LON, swaps)  2.48 us
  transfers between devices with their start and end apart: 5, of which 3 were waited for; matrix products, arithmetic and copies ran while one was open for 1% of the time, Pallas kernels for 15%

profile of v8, /device:TPU:1, one launch (start us, length us, event | category | flops | bytes accessed | tf_op | source)
XLA Modules:
  0.0 62.9 jit_solution(9245848203397561967)
XLA Ops:
  0.6 0.0 copy-start
  0.6 1.4 %shard_map.58 = (bf16[192,128]{1,0:T(8,128)(2,1)S(1)}, bf16[192,128]{1,0:T(8,128)(2,1)S(1)}, bf16[2048,128]{1,0:T(8,128)(2,1)S(1)}, bf16[2048,128]{1,0:T(8,128)(2,1)S(1)}) custom-call(bf16[2048,128]{1,0:T(8,128)(2,1)} %bitcast.20, bf16[2048,128]{1,0:T(8,128)(2,1)} %bitcast.21), custom_call_target="tpu_custom_call" | custom-call | bytes 2195456 | tf_op jit(solution)/shard_map/pallas_call | solution.py:39
  2.1 2.7 %collective-permute-start = (bf16[192,128]{1,0:T(8,128)(2,1)S(1)}, bf16[192,128]{1,0:T(8,128)(2,1)S(1)}, u32[]{:S(2)}, u32[]{:S(2)}) collective-permute-start(bf16[192,128]{1,0:T(8,128)(2,1)S(1)} %get-tuple-element.27), channel_id=1, source_target_pairs={{0,8},{1,9},{2,10},{3,11},{4,12},{5,13},{6,14},{7,15},{8,0},{9,1},... | collective-permute-start | bytes 147464 | tf_op jit(solution)/shard_map/ppermute | solution.py:394
  4.8 6.1 %collective-permute-start.1 = (bf16[192,128]{1,0:T(8,128)(2,1)S(1)}, bf16[192,128]{1,0:T(8,128)(2,1)S(1)}, u32[]{:S(2)}, u32[]{:S(2)}) collective-permute-start(bf16[192,128]{1,0:T(8,128)(2,1)S(1)} %get-tuple-element.28), channel_id=1, source_target_pairs={{0,16},{16,0},{32,48},{48,32},{64,80},{80,64},{96,112},{112,96},{1... | collective-permute-start | bytes 147464 | tf_op jit(solution)/shard_map/ppermute | solution.py:395
  10.9 0.0 copy-done
  10.9 0.1 copy.10
  11.0 0.1 copy.11.w_ref
  11.2 1.7 %shard_map.59 = (bf16[32,64,128]{2,1,0:T(8,128)(2,1)S(1)}, bf16[32,64,128]{2,1,0:T(8,128)(2,1)S(1)}, bf16[128,128]{1,0:T(8,128)(2,1)S(1)}) custom-call(bf16[2048,128]{1,0:T(8,128)(2,1)S(1)} %get-tuple-element.21.f_ref, bf16[2048,128]{1,0:T(8,128)(2,1)S(1)} %get-tuple-element.22.g_ref), custom_call_target="tpu_custom_call" | custom-call | bytes 2129920 | tf_op jit(solution)/shard_map/pallas_call | solution.py:39
  12.8 2.7 %shard_map.60 = (bf16[30,64,128]{2,1,0:T(8,128)(2,1)S(1)}, bf16[30,64,128]{2,1,0:T(8,128)(2,1)S(1)}, f32[64,576]{1,0:T(8,128)S(1)}, f32[8,128]{1,0:T(8,128)S(1)}) custom-call(bf16[32,64,128]{2,1,0:T(8,128)(2,1)S(1)} %get-tuple-element.23.fr_ref, bf16[32,64,128]{2,1,0:T(8,128)(2,1)S(1)} %get-tuple-element.24.gr_ref, bf16[64,576]{1,0:T(8,128)(2,1)S(1)} %copy.11.w_ref), custom_call_target="tpu_custom_call" | custom-call | flops 603979776 | bytes 2256896 | tf_op jit(solution)/shard_map/pallas_call | solution.py:39
  15.5 0.0 collective-permute-done.outer_ref
  15.5 0.0 collective-permute-done.1.inner_ref
  15.5 0.2 shard_map.61
  15.7 2.5 %collective-permute-start.2 = (bf16[64,128]{1,0:T(8,128)(2,1)S(1)}, bf16[64,128]{1,0:T(8,128)(2,1)S(1)}, u32[]{:S(2)}, u32[]{:S(2)}) collective-permute-start(bf16[64,128]{1,0:T(8,128)(2,1)S(1)} %get-tuple-element.30), channel_id=1, source_target_pairs={{0,15},{1,2},{2,1},{3,4},{4,3},{5,6},{6,5},{7,8},{8,7},{9,10},{10,... | collective-permute-start | bytes 49160 | tf_op jit(solution)/shard_map/ppermute | solution.py:425
  18.2 1.0 %collective-permute-start.3 = (bf16[64,128]{1,0:T(8,128)(2,1)S(1)}, bf16[64,128]{1,0:T(8,128)(2,1)S(1)}, u32[]{:S(2)}, u32[]{:S(2)}) collective-permute-start(bf16[64,128]{1,0:T(8,128)(2,1)S(1)} %get-tuple-element.31), channel_id=1, source_target_pairs={{0,1},{1,0},{2,3},{3,2},{4,5},{5,4},{6,7},{7,6},{8,9},{9,8},{10,11... | collective-permute-start | bytes 49160 | tf_op jit(solution)/shard_map/ppermute | solution.py:426
  19.2 0.1 copy.12
  19.3 0.2 reshape.36.wa_ref
  19.5 2.5 %collective-permute-done.2.far_ref = bf16[64,128]{1,0:T(8,128)(2,1)S(1)} collective-permute-done((bf16[64,128]{1,0:T(8,128)(2,1)S(1)}, bf16[64,128]{1,0:T(8,128)(2,1)S(1)}, u32[]{:S(2)}, u32[]{:S(2)}) %collective-permute-start.2) | collective-permute-done | bytes 16416 | tf_op jit(solution)/shard_map/ppermute | solution.py:425
  22.0 0.7 %collective-permute-done.3.near_ref = bf16[64,128]{1,0:T(8,128)(2,1)S(1)} collective-permute-done((bf16[64,128]{1,0:T(8,128)(2,1)S(1)}, bf16[64,128]{1,0:T(8,128)(2,1)S(1)}, u32[]{:S(2)}, u32[]{:S(2)}) %collective-permute-start.3) | collective-permute-done | bytes 16416 | tf_op jit(solution)/shard_map/ppermute | solution.py:426
  22.6 1.0 %shard_map.62 = (bf16[2,64,128]{2,1,0:T(8,128)(2,1)S(1)}, bf16[64,128]{1,0:T(8,128)(2,1)S(1)}, bf16[4,64,128]{2,1,0:T(8,128)(2,1)S(1)}, bf16[64,384]{1,0:T(8,128)(2,1)S(1)}, f32[32,1,1152]{2,1,0:T(1,128)S(1)}) custom-call(bf16[32,64,128]{2,1,0:T(8,128)(2,1)S(1)} %get-tuple-element.23.fr_ref, bf16[32,64,128]{2,1,0:T(8,128)(2,1)S(1)} %get-tuple-element.24.gr_ref, ...), custom_call_target="tpu_custom_call" | custom-call | flops 75497472 | bytes 1818624 | tf_op jit(solution)/shard_map/pallas_call | solution.py:39
  23.7 13.7 %all_to_all.15.parts_ref = f32[32,1,1152]{2,1,0:T(1,128)S(1)} all-to-all(f32[32,1,1152]{2,1,0:T(1,128)S(1)} %get-tuple-element.35), channel_id=1, replica_groups=mesh['lat'=16,'z'=8,'side'=2] {'lat','side'}, dimensions={0} | all-to-all | bytes 294912 | tf_op jit(solution)/shard_map/all_to_all | solution.py:446
  37.4 0.1 shard_map.64
  37.5 10.9 %all_to_all.16.after_ref.parts_ref = f32[8,1,1152]{2,1,0:T(1,128)S(1)} all-to-all(f32[8,1,1152]{2,1,0:T(1,128)S(1)} %shard_map.64), channel_id=1, replica_groups=mesh['lat'=16,'z'=8,'side'=2] {'z'}, dimensions={0} | all-to-all | bytes 73728 | tf_op jit(solution)/shard_map/all_to_all | solution.py:448
  48.4 0.7 %shard_map.66 = bf16[32,2,640]{2,1,0:T(2,128)(2,1)} custom-call(f32[8,1,1152]{2,1,0:T(1,128)S(1)} %all_to_all.16.after_ref.parts_ref), custom_call_target="tpu_custom_call" | custom-call | bytes 118784 | tf_op jit(solution)/shard_map/pallas_call | solution.py:39
  49.1 5.7 %all-to-all-start.2 = ((bf16[32,2,640]{2,1,0:T(2,128)(2,1)}), bf16[32,2,640]{2,1,0:T(2,128)(2,1)S(1)}, u32[]{:S(2)}, u32[]{:S(2)}) async-start(bf16[32,2,640]{2,1,0:T(2,128)(2,1)} %shard_map.66), calls=%async_computation.2 | async-start | bytes 163840 | tf_op jit(solution)/shard_map/all_to_all | solution.py:457
  54.8 0.1 copy.15.wb3_ref
  54.9 0.1 copy.14.wb_ref
  55.0 1.8 %shard_map.63 = bf16[2048,128]{1,0:T(8,128)(2,1)} custom-call(bf16[30,64,128]{2,1,0:T(8,128)(2,1)S(1)} %get-tuple-element.25.mid_ref, bf16[2,64,128]{2,1,0:T(8,128)(2,1)S(1)} %get-tuple-element.33.rim_ref, bf16[64,128]{1,0:T(8,128)(2,1)S(1)} %get-tuple-element.34.strip_ref), custom_call_target="tpu_custom_call" | custom-call | bytes 1064960 | tf_op jit(solution)/shard_map/pallas_call | solution.py:39
  56.9 3.2 %shard_map.65 = bf16[2048,128]{1,0:T(8,128)(2,1)} custom-call(f32[8,1,1152]{2,1,0:T(1,128)S(1)} %all_to_all.16.after_ref.parts_ref, bf16[30,64,128]{2,1,0:T(8,128)(2,1)S(1)} %get-tuple-element.36.mid_ref, bf16[4,64,128]{2,1,0:T(8,128)(2,1)S(1)} %get-tuple-element.37.rim_ref, bf16[64,384]{1,0:T(8,128)(2,1)S(1)} %get-tuple-element.38.dstrip_ref, ...), custom_call_target="tpu_custom_call" | custom-call | flops 301989888 | bytes 1839104 | tf_op jit(solution)/shard_map/pallas_call | solution.py:39
  60.1 1.9 %all-to-all-done.2.parts_ref = bf16[32,2,640]{2,1,0:T(2,128)(2,1)S(1)} async-done(((bf16[32,2,640]{2,1,0:T(2,128)(2,1)}), bf16[32,2,640]{2,1,0:T(2,128)(2,1)S(1)}, u32[]{:S(2)}, u32[]{:S(2)}) %all-to-all-start.2) | async-done | bytes 81952 | tf_op jit(solution)/shard_map/all_to_all | solution.py:457
  62.0 0.9 %shard_map.67 = f32[9,64,64]{2,1,0:T(8,128)} custom-call(bf16[32,2,640]{2,1,0:T(2,128)(2,1)S(1)} %all-to-all-done.2.parts_ref), custom_call_target="tpu_custom_call" | custom-call | bytes 229376 | tf_op jit(solution)/shard_map/pallas_call | solution.py:39
  (1 shorter events, 0.0 us)
Async XLA Ops:
  0.6 10.2 %copy-start = (bf16[3,3,64,64]{3,2,1,0:T(8,128)(2,1)S(1)}, bf16[3,3,64,64]{3,2,1,0:T(8,128)(2,1)}, u32[]{:S(2)}) copy-start(bf16[3,3,64,64]{3,2,1,0:T(8,128)(2,1)} %param.4) | copy-start | bytes 221188
  2.1 13.4 %collective-permute-start = (bf16[192,128]{1,0:T(8,128)(2,1)S(1)}, bf16[192,128]{1,0:T(8,128)(2,1)S(1)}, u32[]{:S(2)}, u32[]{:S(2)}) collective-permute-start(bf16[192,128]{1,0:T(8,128)(2,1)S(1)} %get-tuple-element.27), channel_id=1, source_target_pairs={{0,8},{1,9},{2,10},{3,11},{4,12},{5,13},{6,14},{7,15},{8,0},{9,1},... | collective-permute-start | bytes 147464 | tf_op jit(solution)/shard_map/ppermute | solution.py:394
  4.8 10.7 %collective-permute-start.1 = (bf16[192,128]{1,0:T(8,128)(2,1)S(1)}, bf16[192,128]{1,0:T(8,128)(2,1)S(1)}, u32[]{:S(2)}, u32[]{:S(2)}) collective-permute-start(bf16[192,128]{1,0:T(8,128)(2,1)S(1)} %get-tuple-element.28), channel_id=1, source_target_pairs={{0,16},{16,0},{32,48},{48,32},{64,80},{80,64},{96,112},{112,96},{1... | collective-permute-start | bytes 147464 | tf_op jit(solution)/shard_map/ppermute | solution.py:395
  15.7 6.3 %collective-permute-start.2 = (bf16[64,128]{1,0:T(8,128)(2,1)S(1)}, bf16[64,128]{1,0:T(8,128)(2,1)S(1)}, u32[]{:S(2)}, u32[]{:S(2)}) collective-permute-start(bf16[64,128]{1,0:T(8,128)(2,1)S(1)} %get-tuple-element.30), channel_id=1, source_target_pairs={{0,15},{1,2},{2,1},{3,4},{4,3},{5,6},{6,5},{7,8},{8,7},{9,10},{10,... | collective-permute-start | bytes 49160 | tf_op jit(solution)/shard_map/ppermute | solution.py:425
  18.2 4.4 %collective-permute-start.3 = (bf16[64,128]{1,0:T(8,128)(2,1)S(1)}, bf16[64,128]{1,0:T(8,128)(2,1)S(1)}, u32[]{:S(2)}, u32[]{:S(2)}) collective-permute-start(bf16[64,128]{1,0:T(8,128)(2,1)S(1)} %get-tuple-element.31), channel_id=1, source_target_pairs={{0,1},{1,0},{2,3},{3,2},{4,5},{5,4},{6,7},{7,6},{8,9},{9,8},{10,11... | collective-permute-start | bytes 49160 | tf_op jit(solution)/shard_map/ppermute | solution.py:426
  49.1 13.0 %all-to-all-start.2 = ((bf16[32,2,640]{2,1,0:T(2,128)(2,1)}), bf16[32,2,640]{2,1,0:T(2,128)(2,1)S(1)}, u32[]{:S(2)}, u32[]{:S(2)}) async-start(bf16[32,2,640]{2,1,0:T(2,128)(2,1)} %shard_map.66), calls=%async_computation.2 | async-start | bytes 163840 | tf_op jit(solution)/shard_map/all_to_all | solution.py:457

commit v9 on v8

--- a/solution.py
+++ b/solution.py
@@ -40,7 +40,7 @@
         body,
         out_shape=outs,
         in_specs=[pl.BlockSpec(memory_space=space)] * len(args),
-        out_specs=[pl.BlockSpec(memory_space=out_space)] * len(outs),
+        out_specs=[pl.BlockSpec(memory_space=out_space if i == 0 else pltpu.VMEM) for i in range(len(outs))],
         scratch_shapes=list(scratch),
         cost_estimate=pl.CostEstimate(flops=flops, bytes_accessed=size, transcendentals=0),
         compiler_params=pltpu.CompilerParams(vmem_limit_bytes=int(limit * 2**20)),
@@ -282,7 +282,7 @@
         copy.wait()
 
 
-def restore_body(mid_ref, rim_ref, strip_ref, out_hbm, wide, out_ref, sems):
+def restore_body(mid_ref, rim_ref, strip_ref, out_hbm, token_ref, wide, out_ref, sems):
     lane = lanes()
     packed = strip_ref[...].astype(f32)
     wide[pl.ds(0, CH, stride=ROWS), :] = rim_ref[0].astype(f32)
@@ -290,13 +290,14 @@
         wide[pl.ds(r, CH, stride=ROWS), :] = patched(mid_ref[r - 1], packed, r, lane)
     wide[pl.ds(ROWS - 1, CH, stride=ROWS), :] = rim_ref[1].astype(f32)
     write_out(wide, out_hbm, out_ref, sems)
+    token_ref[...] = jnp.zeros(token_ref.shape, f32)
 
 
 def grad_scale():
     return float(ROWS * COLS * lax.axis_size(EVERY)) ** (-0.5)
 
 
-def backward_body(after_ref, mid_ref, rim_ref, dstrip_ref, gr_ref, wb_ref, wb3_ref, out_hbm, xs, wide, out_ref, sems):
+def backward_body(after_ref, mid_ref, rim_ref, dstrip_ref, gr_ref, wb_ref, wb3_ref, out_hbm, token_ref, xs, wide, out_ref, sems):
     lat = lax.axis_index("lat")
     at_top = lat == 0
     at_bottom = lat == lax.axis_size("lat") - 1
@@ -328,9 +329,10 @@
         put(r, back[:, :COLS])
         put(r + 1, back[:, COLS:])
     write_out(wide, out_hbm, out_ref, sems)
-
-
-def fold_body(parts_ref, out_ref):
+    token_ref[...] = jnp.zeros(token_ref.shape, f32)
+
+
+def fold_body(parts_ref, token_ref, out_ref):
     total = jnp.sum(parts_ref[...], 0)
     if out_ref.shape[1] == 2:
         width = out_ref.shape[2]
@@ -439,22 +441,27 @@
         conv_flops // 4,
     )
 
-    def spread(parts, shape, dtype):
-        return call(fold_body, [(shape, dtype)], (parts,))[0]
-
+    def spread(parts, done, shape, dtype):
+        return call(fold_body, [(shape, dtype)], (parts, done))[0]
+
+    token = ((8, COLS), f32)
     writing = [pltpu.VMEM(flat, f32), pltpu.VMEM(flat, bf16), pltpu.SemaphoreType.DMA((PIECES,))]
     parts = lax.all_to_all(grad, PLANE, 0, 0)
-    (output,) = call(restore_body, [(flat, bf16)], (out_mid, out_rim, out_strip), writing, out_space=pl.ANY)
-    parts = lax.all_to_all(spread(parts, (lax.axis_size("z"), 1, piece), f32), "z", 0, 0)
-    (grad_input,) = call(
+    output, done = call(
+        restore_body, [(flat, bf16), token], (out_mid, out_rim, out_strip), writing, out_space=pl.ANY
+    )
+    deep = spread(parts, done, (lax.axis_size("z"), 1, piece), f32)
+    grad_input, done = call(
         backward_body,
-        [(flat, bf16)],
+        [(flat, bf16), token],
         (parts, delta_mid, delta_rim, dstrip, gr, wb, wb3),
         [pltpu.VMEM((ROWS + 2, TAPS, COLS), bf16)] + writing,
         conv_flops,
         out_space=pl.ANY,
     )
-    parts = lax.all_to_all(spread(parts, (plane, 2, -(-piece // (2 * COLS)) * COLS), bf16), PLANE, 0, 0)
+    parts = lax.all_to_all(deep, "z", 0, 0)
+    parts = spread(parts, done, (plane, 2, -(-piece // (2 * COLS)) * COLS), bf16)
+    parts = lax.all_to_all(parts, PLANE, 0, 0)
     (grad_kernel,) = call(
         unpack_body,
         [((9, CH, CH), f32)],

time: 63.2 us -> 63.6 us (level)
  blocking collectives: 24.6 us -> 12.3 us
  waiting for transfers between devices: 5.05 us -> 12.4 us
  starting transfers between devices: 18 us -> 22.7 us
    all_to_all x2 -> x1, blocking collectives: 24.6 us -> 12.3 us  [on_device(): parts = lax.all_to_all(parts, PLANE, 0, 0)]
    all_to_all x1 -> x2, waiting for transfers between devices: 1.9 us -> 9.24 us  [the longest x1 5.83 us: on_device(): parts = lax.all_to_all(grad, PLANE, 0, 0)]
    all_to_all x1 -> x2, starting transfers between devices: 5.67 us -> 10.4 us  [the longest x1 6.55 us: on_device(): parts = lax.all_to_all(grad, PLANE, 0, 0)]
  transfers between devices with their start and end apart: 5 -> 6, of which waited for: 3 -> 4; matrix products, arithmetic and copies ran while one was open for 1% -> 1% of each run, Pallas kernels for 15% -> 15%
where the time goes in v9:
time: 63.6 us; the launch traced here: 63.3 us
  starting transfers between devices  22.7 us (36%)
  Pallas kernels  14.3 us (22%)
  waiting for transfers between devices  12.4 us (19%)
  blocking collectives  12.3 us (19%)
  local copies, waits for them, and re-layouts  0.87 us (1%)
  between operations  0.73 us (1%)
    pallas_call x10, Pallas kernels, call(): pl.pallas_call(body, out_shape=outs, in_specs=[pl.BlockSpec(memory_space=...  14.3 us
    all_to_all x1, blocking collectives, on_device(): parts = lax.all_to_all(parts, PLANE, 0, 0)  12.3 us
    all_to_all x1, starting transfers between devices, on_device(): parts = lax.all_to_all(grad, PLANE, 0, 0)  6.55 us
    ppermute x1, starting transfers between devices, on_device(): inner = lax.ppermute(inner, 'lat', [(i, i ^ 1) for i in range(lat_count)])  6.09 us
    all_to_all x1, waiting for transfers between devices, on_device(): parts = lax.all_to_all(grad, PLANE, 0, 0)  5.83 us
    all_to_all x1, starting transfers between devices, on_device(): parts = lax.all_to_all(deep, 'z', 0, 0)  3.87 us
    all_to_all x1, waiting for transfers between devices, on_device(): parts = lax.all_to_all(deep, 'z', 0, 0)  3.41 us
    ppermute x1, starting transfers between devices, on_device(): outer = lax.ppermute(outer, EVERY, outer_pairs(lat_count, lon_count))  2.69 us
  transfers between devices with their start and end apart: 6, of which 4 were waited for; matrix products, arithmetic and copies ran while one was open for 1% of the time, Pallas kernels for 15%

profile of v9, /device:TPU:1, one launch (start us, length us, event | category | flops | bytes accessed | tf_op | source)
XLA Modules:
  0.0 63.3 jit_solution(18079487358819571791)
XLA Ops:
  0.6 0.0 copy-start
  0.6 1.4 %shard_map.58 = (bf16[192,128]{1,0:T(8,128)(2,1)S(1)}, bf16[192,128]{1,0:T(8,128)(2,1)S(1)}, bf16[2048,128]{1,0:T(8,128)(2,1)S(1)}, bf16[2048,128]{1,0:T(8,128)(2,1)S(1)}) custom-call(bf16[2048,128]{1,0:T(8,128)(2,1)} %bitcast.19, bf16[2048,128]{1,0:T(8,128)(2,1)} %bitcast.20), custom_call_target="tpu_custom_call" | custom-call | bytes 2195456 | tf_op jit(solution)/shard_map/pallas_call | solution.py:39
  2.1 2.7 %collective-permute-start = (bf16[192,128]{1,0:T(8,128)(2,1)S(1)}, bf16[192,128]{1,0:T(8,128)(2,1)S(1)}, u32[]{:S(2)}, u32[]{:S(2)}) collective-permute-start(bf16[192,128]{1,0:T(8,128)(2,1)S(1)} %get-tuple-element.31), channel_id=1, source_target_pairs={{0,8},{1,9},{2,10},{3,11},{4,12},{5,13},{6,14},{7,15},{8,0},{9,1},... | collective-permute-start | bytes 147464 | tf_op jit(solution)/shard_map/ppermute | solution.py:396
  4.8 6.1 %collective-permute-start.1 = (bf16[192,128]{1,0:T(8,128)(2,1)S(1)}, bf16[192,128]{1,0:T(8,128)(2,1)S(1)}, u32[]{:S(2)}, u32[]{:S(2)}) collective-permute-start(bf16[192,128]{1,0:T(8,128)(2,1)S(1)} %get-tuple-element.32), channel_id=1, source_target_pairs={{0,16},{16,0},{32,48},{48,32},{64,80},{80,64},{96,112},{112,96},{1... | collective-permute-start | bytes 147464 | tf_op jit(solution)/shard_map/ppermute | solution.py:397
  10.9 0.0 copy-done
  10.9 0.1 copy.10
  11.0 0.1 copy.11.w_ref
  11.2 1.7 %shard_map.59 = (bf16[32,64,128]{2,1,0:T(8,128)(2,1)S(1)}, bf16[32,64,128]{2,1,0:T(8,128)(2,1)S(1)}, bf16[128,128]{1,0:T(8,128)(2,1)S(1)}) custom-call(bf16[2048,128]{1,0:T(8,128)(2,1)S(1)} %get-tuple-element.25.f_ref, bf16[2048,128]{1,0:T(8,128)(2,1)S(1)} %get-tuple-element.26.g_ref), custom_call_target="tpu_custom_call" | custom-call | bytes 2129920 | tf_op jit(solution)/shard_map/pallas_call | solution.py:39
  12.8 2.7 %shard_map.60 = (bf16[30,64,128]{2,1,0:T(8,128)(2,1)S(1)}, bf16[30,64,128]{2,1,0:T(8,128)(2,1)S(1)}, f32[64,576]{1,0:T(8,128)S(1)}, f32[8,128]{1,0:T(8,128)S(1)}) custom-call(bf16[32,64,128]{2,1,0:T(8,128)(2,1)S(1)} %get-tuple-element.27.fr_ref, bf16[32,64,128]{2,1,0:T(8,128)(2,1)S(1)} %get-tuple-element.28.gr_ref, bf16[64,576]{1,0:T(8,128)(2,1)S(1)} %copy.11.w_ref), custom_call_target="tpu_custom_call" | custom-call | flops 603979776 | bytes 2256896 | tf_op jit(solution)/shard_map/pallas_call | solution.py:39
  15.5 0.0 collective-permute-done.outer_ref
  15.5 0.0 collective-permute-done.1.inner_ref
  15.5 0.2 shard_map.61
  15.7 2.5 %collective-permute-start.2 = (bf16[64,128]{1,0:T(8,128)(2,1)S(1)}, bf16[64,128]{1,0:T(8,128)(2,1)S(1)}, u32[]{:S(2)}, u32[]{:S(2)}) collective-permute-start(bf16[64,128]{1,0:T(8,128)(2,1)S(1)} %get-tuple-element.34), channel_id=1, source_target_pairs={{0,15},{1,2},{2,1},{3,4},{4,3},{5,6},{6,5},{7,8},{8,7},{9,10},{10,... | collective-permute-start | bytes 49160 | tf_op jit(solution)/shard_map/ppermute | solution.py:427
  18.2 1.0 %collective-permute-start.3 = (bf16[64,128]{1,0:T(8,128)(2,1)S(1)}, bf16[64,128]{1,0:T(8,128)(2,1)S(1)}, u32[]{:S(2)}, u32[]{:S(2)}) collective-permute-start(bf16[64,128]{1,0:T(8,128)(2,1)S(1)} %get-tuple-element.35), channel_id=1, source_target_pairs={{0,1},{1,0},{2,3},{3,2},{4,5},{5,4},{6,7},{7,6},{8,9},{9,8},{10,11... | collective-permute-start | bytes 49160 | tf_op jit(solution)/shard_map/ppermute | solution.py:428
  19.2 0.1 copy.12
  19.3 0.2 reshape.36.wa_ref
  19.5 2.5 %collective-permute-done.2.far_ref = bf16[64,128]{1,0:T(8,128)(2,1)S(1)} collective-permute-done((bf16[64,128]{1,0:T(8,128)(2,1)S(1)}, bf16[64,128]{1,0:T(8,128)(2,1)S(1)}, u32[]{:S(2)}, u32[]{:S(2)}) %collective-permute-start.2) | collective-permute-done | bytes 16416 | tf_op jit(solution)/shard_map/ppermute | solution.py:427
  22.0 0.7 %collective-permute-done.3.near_ref = bf16[64,128]{1,0:T(8,128)(2,1)S(1)} collective-permute-done((bf16[64,128]{1,0:T(8,128)(2,1)S(1)}, bf16[64,128]{1,0:T(8,128)(2,1)S(1)}, u32[]{:S(2)}, u32[]{:S(2)}) %collective-permute-start.3) | collective-permute-done | bytes 16416 | tf_op jit(solution)/shard_map/ppermute | solution.py:428
  22.6 1.7 %shard_map.62 = (bf16[2,64,128]{2,1,0:T(8,128)(2,1)S(1)}, bf16[64,128]{1,0:T(8,128)(2,1)S(1)}, bf16[4,64,128]{2,1,0:T(8,128)(2,1)S(1)}, bf16[64,384]{1,0:T(8,128)(2,1)S(1)}, f32[32,1,1152]{2,1,0:T(1,128)}) custom-call(bf16[32,64,128]{2,1,0:T(8,128)(2,1)S(1)} %get-tuple-element.27.fr_ref, bf16[32,64,128]{2,1,0:T(8,128)(2,1)S(1)} %get-tuple-element.28.gr_ref, ...), custom_call_target="tpu_custom_call" | custom-call | flops 75497472 | bytes 1818624 | tf_op jit(solution)/shard_map/pallas_call | solution.py:39
  24.3 6.5 %all-to-all-start = ((f32[32,1,1152]{2,1,0:T(1,128)}), f32[32,1,1152]{2,1,0:T(1,128)S(1)}, u32[]{:S(2)}, u32[]{:S(2)}) async-start(f32[32,1,1152]{2,1,0:T(1,128)} %get-tuple-element.40), calls=%async_computation | async-start | bytes 294912 | tf_op jit(solution)/shard_map/all_to_all | solution.py:449
  30.9 1.8 %shard_map.63 = (bf16[2048,128]{1,0:T(8,128)(2,1)}, f32[8,128]{1,0:T(8,128)S(1)}) custom-call(bf16[30,64,128]{2,1,0:T(8,128)(2,1)S(1)} %get-tuple-element.29.mid_ref, bf16[2,64,128]{2,1,0:T(8,128)(2,1)S(1)} %get-tuple-element.37.rim_ref, bf16[64,128]{1,0:T(8,128)(2,1)S(1)} %get-tuple-element.38.strip_ref), custom_call_target="tpu_custom_call" | custom-call | bytes 1069056 | tf_op jit(solution)/shard_map/pallas_call | solution.py:39
  32.7 5.8 %all-to-all-done.after_ref.parts_ref = f32[32,1,1152]{2,1,0:T(1,128)S(1)} async-done(((f32[32,1,1152]{2,1,0:T(1,128)}), f32[32,1,1152]{2,1,0:T(1,128)S(1)}, u32[]{:S(2)}, u32[]{:S(2)}) %all-to-all-start) | async-done | bytes 147488 | tf_op jit(solution)/shard_map/all_to_all | solution.py:449
  38.6 0.7 %shard_map.65 = f32[8,1,1152]{2,1,0:T(1,128)} custom-call(f32[32,1,1152]{2,1,0:T(1,128)S(1)} %all-to-all-done.after_ref.parts_ref, f32[8,128]{1,0:T(8,128)S(1)} %get-tuple-element.45.token_ref), custom_call_target="tpu_custom_call" | custom-call | bytes 188416 | tf_op jit(solution)/shard_map/pallas_call | solution.py:39
  39.3 3.9 %all-to-all-start.1 = ((f32[8,1,1152]{2,1,0:T(1,128)}), f32[8,1,1152]{2,1,0:T(1,128)S(1)}, u32[]{:S(2)}, u32[]{:S(2)}) async-start(f32[8,1,1152]{2,1,0:T(1,128)} %shard_map.65), calls=%async_computation.1 | async-start | bytes 73728 | tf_op jit(solution)/shard_map/all_to_all | solution.py:462
  43.2 0.1 copy.15.wb3_ref
  43.3 0.1 copy.14.wb_ref
  43.4 3.2 %shard_map.64 = (bf16[2048,128]{1,0:T(8,128)(2,1)}, f32[8,128]{1,0:T(8,128)S(1)}) custom-call(f32[32,1,1152]{2,1,0:T(1,128)S(1)} %all-to-all-done.after_ref.parts_ref, bf16[30,64,128]{2,1,0:T(8,128)(2,1)S(1)} %get-tuple-element.41.mid_ref, bf16[4,64,128]{2,1,0:T(8,128)(2,1)S(1)} %get-tuple-element.42.rim_ref, ...), custom_call_target="tpu_custom_call" | custom-call | flops 301989888 | bytes 1953792 | tf_op jit(solution)/shard_map/pallas_call | solution.py:39
  46.7 3.4 %all-to-all-done.1.parts_ref = f32[8,1,1152]{2,1,0:T(1,128)S(1)} async-done(((f32[8,1,1152]{2,1,0:T(1,128)}), f32[8,1,1152]{2,1,0:T(1,128)S(1)}, u32[]{:S(2)}, u32[]{:S(2)}) %all-to-all-start.1) | async-done | bytes 36896 | tf_op jit(solution)/shard_map/all_to_all | solution.py:462
  50.1 12.3 %all_to_all.15.parts_ref = bf16[32,2,640]{2,1,0:T(2,128)(2,1)S(1)} all-to-all(bf16[32,2,640]{2,1,0:T(2,128)(2,1)S(1)} %shard_map.66), channel_id=1, replica_groups=mesh['lat'=16,'z'=8,'side'=2] {'lat','side'}, dimensions={0} | all-to-all | bytes 163840 | tf_op jit(solution)/shard_map/all_to_all | solution.py:464
  62.4 0.9 %shard_map.67 = f32[9,64,64]{2,1,0:T(8,128)} custom-call(bf16[32,2,640]{2,1,0:T(2,128)(2,1)S(1)} %all_to_all.15.parts_ref), custom_call_target="tpu_custom_call" | custom-call | bytes 229376 | tf_op jit(solution)/shard_map/pallas_call | solution.py:39
  (2 shorter events, 0.1 us)
Async XLA Ops:
  0.6 10.2 %copy-start = (bf16[3,3,64,64]{3,2,1,0:T(8,128)(2,1)S(1)}, bf16[3,3,64,64]{3,2,1,0:T(8,128)(2,1)}, u32[]{:S(2)}) copy-start(bf16[3,3,64,64]{3,2,1,0:T(8,128)(2,1)} %param.4) | copy-start | bytes 221188
  2.1 13.4 %collective-permute-start = (bf16[192,128]{1,0:T(8,128)(2,1)S(1)}, bf16[192,128]{1,0:T(8,128)(2,1)S(1)}, u32[]{:S(2)}, u32[]{:S(2)}) collective-permute-start(bf16[192,128]{1,0:T(8,128)(2,1)S(1)} %get-tuple-element.31), channel_id=1, source_target_pairs={{0,8},{1,9},{2,10},{3,11},{4,12},{5,13},{6,14},{7,15},{8,0},{9,1},... | collective-permute-start | bytes 147464 | tf_op jit(solution)/shard_map/ppermute | solution.py:396
  4.8 10.7 %collective-permute-start.1 = (bf16[192,128]{1,0:T(8,128)(2,1)S(1)}, bf16[192,128]{1,0:T(8,128)(2,1)S(1)}, u32[]{:S(2)}, u32[]{:S(2)}) collective-permute-start(bf16[192,128]{1,0:T(8,128)(2,1)S(1)} %get-tuple-element.32), channel_id=1, source_target_pairs={{0,16},{16,0},{32,48},{48,32},{64,80},{80,64},{96,112},{112,96},{1... | collective-permute-start | bytes 147464 | tf_op jit(solution)/shard_map/ppermute | solution.py:397
  15.7 6.3 %collective-permute-start.2 = (bf16[64,128]{1,0:T(8,128)(2,1)S(1)}, bf16[64,128]{1,0:T(8,128)(2,1)S(1)}, u32[]{:S(2)}, u32[]{:S(2)}) collective-permute-start(bf16[64,128]{1,0:T(8,128)(2,1)S(1)} %get-tuple-element.34), channel_id=1, source_target_pairs={{0,15},{1,2},{2,1},{3,4},{4,3},{5,6},{6,5},{7,8},{8,7},{9,10},{10,... | collective-permute-start | bytes 49160 | tf_op jit(solution)/shard_map/ppermute | solution.py:427
  18.2 4.4 %collective-permute-start.3 = (bf16[64,128]{1,0:T(8,128)(2,1)S(1)}, bf16[64,128]{1,0:T(8,128)(2,1)S(1)}, u32[]{:S(2)}, u32[]{:S(2)}) collective-permute-start(bf16[64,128]{1,0:T(8,128)(2,1)S(1)} %get-tuple-element.35), channel_id=1, source_target_pairs={{0,1},{1,0},{2,3},{3,2},{4,5},{5,4},{6,7},{7,6},{8,9},{9,8},{10,11... | collective-permute-start | bytes 49160 | tf_op jit(solution)/shard_map/ppermute | solution.py:428
  24.3 14.2 %all-to-all-start = ((f32[32,1,1152]{2,1,0:T(1,128)}), f32[32,1,1152]{2,1,0:T(1,128)S(1)}, u32[]{:S(2)}, u32[]{:S(2)}) async-start(f32[32,1,1152]{2,1,0:T(1,128)} %get-tuple-element.40), calls=%async_computation | async-start | bytes 294912 | tf_op jit(solution)/shard_map/all_to_all | solution.py:449
  39.3 10.8 %all-to-all-start.1 = ((f32[8,1,1152]{2,1,0:T(1,128)}), f32[8,1,1152]{2,1,0:T(1,128)S(1)}, u32[]{:S(2)}, u32[]{:S(2)}) async-start(f32[8,1,1152]{2,1,0:T(1,128)} %shard_map.65), calls=%async_computation.1 | async-start | bytes 73728 | tf_op jit(solution)/shard_map/all_to_all | solution.py:462

commit v10 on v8

--- a/solution.py
+++ b/solution.py
@@ -439,13 +439,18 @@
         conv_flops // 4,
     )
 
+    def exchange(parts, axes, first):
+        count = lax.axis_size(axes)
+        order = [(first + i) % count for i in range(count)]
+        return lax.all_to_all(parts, axes, 0, 0, axis_index_groups=[order])
+
     def spread(parts, shape, dtype):
         return call(fold_body, [(shape, dtype)], (parts,))[0]
 
     writing = [pltpu.VMEM(flat, f32), pltpu.VMEM(flat, bf16), pltpu.SemaphoreType.DMA((PIECES,))]
-    parts = lax.all_to_all(grad, PLANE, 0, 0)
+    parts = exchange(grad, PLANE, plane // 4 + 1)
     (output,) = call(restore_body, [(flat, bf16)], (out_mid, out_rim, out_strip), writing, out_space=pl.ANY)
-    parts = lax.all_to_all(spread(parts, (lax.axis_size("z"), 1, piece), f32), "z", 0, 0)
+    parts = exchange(spread(parts, (lax.axis_size("z"), 1, piece), f32), "z", lax.axis_size("z") // 2)
     (grad_input,) = call(
         backward_body,
         [(flat, bf16)],
@@ -454,7 +459,8 @@
         conv_flops,
         out_space=pl.ANY,
     )
-    parts = lax.all_to_all(spread(parts, (plane, 2, -(-piece // (2 * COLS)) * COLS), bf16), PLANE, 0, 0)
+    packed = (plane, 2, -(-piece // (2 * COLS)) * COLS)
+    parts = exchange(spread(parts, packed, bf16), PLANE, plane // 4 + 1)
     (grad_kernel,) = call(
         unpack_body,
         [((9, CH, CH), f32)],

time: 63.2 us -> 62.2 us (0.984)
  starting transfers between devices: 18 us -> 22 us
  blocking collectives: 24.6 us -> 21.4 us
  waiting for transfers between devices: 5.05 us -> 3.14 us
    all_to_all x1, starting transfers between devices: 5.67 us -> 9.75 us  [exchange(): return lax.all_to_all(parts, axes, 0, 0, axis_index_groups=[order])]
    all_to_all x2, blocking collectives: 24.6 us -> 21.4 us  [exchange(): return lax.all_to_all(parts, axes, 0, 0, axis_index_groups=[order])]
    all_to_all x1, waiting for transfers between devices: 1.9 us -> 0.01 us  [exchange(): return lax.all_to_all(parts, axes, 0, 0, axis_index_groups=[order])]
  transfers between devices with their start and end apart: 5 -> 5, of which waited for: 3 -> 2; matrix products, arithmetic and copies ran while one was open for 1% -> 1% of each run, Pallas kernels for 15% -> 15%
where the time goes in v10:
time: 62.2 us; the launch traced here: 61.9 us
  starting transfers between devices  22 us (35%)
  blocking collectives  21.4 us (34%)
  Pallas kernels  13.7 us (22%)
  waiting for transfers between devices  3.14 us (5%)
  local copies, waits for them, and re-layouts  0.87 us (1%)
  between operations  0.75 us (1%)
    all_to_all x2, blocking collectives, exchange(): return lax.all_to_all(parts, axes, 0, 0, axis_index_groups=[order])  21.4 us
    pallas_call x10, Pallas kernels, call(): pl.pallas_call(body, out_shape=outs, in_specs=[pl.BlockSpec(memory_space=...  13.7 us
    all_to_all x1, starting transfers between devices, exchange(): return lax.all_to_all(parts, axes, 0, 0, axis_index_groups=[order])  9.75 us
    ppermute x1, starting transfers between devices, on_device(): inner = lax.ppermute(inner, 'lat', [(i, i ^ 1) for i in range(lat_count)])  6.09 us
    ppermute x1, starting transfers between devices, on_device(): outer = lax.ppermute(outer, EVERY, outer_pairs(lat_count, lon_count))  2.69 us
    ppermute x1, starting transfers between devices, on_device(): far = lax.ppermute(far, LON, swaps)  2.55 us
    ppermute x1, waiting for transfers between devices, on_device(): far = lax.ppermute(far, LON, swaps)  2.48 us
  transfers between devices with their start and end apart: 5, of which 2 were waited for; matrix products, arithmetic and copies ran while one was open for 1% of the time, Pallas kernels for 15%

profile of v10, /device:TPU:1, one launch (start us, length us, event | category | flops | bytes accessed | tf_op | source)
XLA Modules:
  0.0 61.9 jit_solution(10173966460187519456)
XLA Ops:
  0.6 0.0 copy-start
  0.6 1.4 %shard_map.58 = (bf16[192,128]{1,0:T(8,128)(2,1)S(1)}, bf16[192,128]{1,0:T(8,128)(2,1)S(1)}, bf16[2048,128]{1,0:T(8,128)(2,1)S(1)}, bf16[2048,128]{1,0:T(8,128)(2,1)S(1)}) custom-call(bf16[2048,128]{1,0:T(8,128)(2,1)} %bitcast.20, bf16[2048,128]{1,0:T(8,128)(2,1)} %bitcast.21), custom_call_target="tpu_custom_call" | custom-call | bytes 2195456 | tf_op jit(solution)/shard_map/pallas_call | solution.py:39
  2.1 2.7 %collective-permute-start = (bf16[192,128]{1,0:T(8,128)(2,1)S(1)}, bf16[192,128]{1,0:T(8,128)(2,1)S(1)}, u32[]{:S(2)}, u32[]{:S(2)}) collective-permute-start(bf16[192,128]{1,0:T(8,128)(2,1)S(1)} %get-tuple-element.27), channel_id=1, source_target_pairs={{0,8},{1,9},{2,10},{3,11},{4,12},{5,13},{6,14},{7,15},{8,0},{9,1},... | collective-permute-start | bytes 147464 | tf_op jit(solution)/shard_map/ppermute | solution.py:394
  4.8 6.1 %collective-permute-start.1 = (bf16[192,128]{1,0:T(8,128)(2,1)S(1)}, bf16[192,128]{1,0:T(8,128)(2,1)S(1)}, u32[]{:S(2)}, u32[]{:S(2)}) collective-permute-start(bf16[192,128]{1,0:T(8,128)(2,1)S(1)} %get-tuple-element.28), channel_id=1, source_target_pairs={{0,16},{16,0},{32,48},{48,32},{64,80},{80,64},{96,112},{112,96},{1... | collective-permute-start | bytes 147464 | tf_op jit(solution)/shard_map/ppermute | solution.py:395
  10.9 0.0 copy-done
  10.9 0.1 copy.10
  11.0 0.1 copy.11.w_ref
  11.2 1.7 %shard_map.59 = (bf16[32,64,128]{2,1,0:T(8,128)(2,1)S(1)}, bf16[32,64,128]{2,1,0:T(8,128)(2,1)S(1)}, bf16[128,128]{1,0:T(8,128)(2,1)S(1)}) custom-call(bf16[2048,128]{1,0:T(8,128)(2,1)S(1)} %get-tuple-element.21.f_ref, bf16[2048,128]{1,0:T(8,128)(2,1)S(1)} %get-tuple-element.22.g_ref), custom_call_target="tpu_custom_call" | custom-call | bytes 2129920 | tf_op jit(solution)/shard_map/pallas_call | solution.py:39
  12.8 2.7 %shard_map.60 = (bf16[30,64,128]{2,1,0:T(8,128)(2,1)S(1)}, bf16[30,64,128]{2,1,0:T(8,128)(2,1)S(1)}, f32[64,576]{1,0:T(8,128)S(1)}, f32[8,128]{1,0:T(8,128)S(1)}) custom-call(bf16[32,64,128]{2,1,0:T(8,128)(2,1)S(1)} %get-tuple-element.23.fr_ref, bf16[32,64,128]{2,1,0:T(8,128)(2,1)S(1)} %get-tuple-element.24.gr_ref, bf16[64,576]{1,0:T(8,128)(2,1)S(1)} %copy.11.w_ref), custom_call_target="tpu_custom_call" | custom-call | flops 603979776 | bytes 2256896 | tf_op jit(solution)/shard_map/pallas_call | solution.py:39
  15.5 0.0 collective-permute-done.outer_ref
  15.5 0.0 collective-permute-done.1.inner_ref
  15.5 0.2 shard_map.61
  15.7 2.5 %collective-permute-start.2 = (bf16[64,128]{1,0:T(8,128)(2,1)S(1)}, bf16[64,128]{1,0:T(8,128)(2,1)S(1)}, u32[]{:S(2)}, u32[]{:S(2)}) collective-permute-start(bf16[64,128]{1,0:T(8,128)(2,1)S(1)} %get-tuple-element.30), channel_id=1, source_target_pairs={{0,15},{1,2},{2,1},{3,4},{4,3},{5,6},{6,5},{7,8},{8,7},{9,10},{10,... | collective-permute-start | bytes 49160 | tf_op jit(solution)/shard_map/ppermute | solution.py:425
  18.2 1.0 %collective-permute-start.3 = (bf16[64,128]{1,0:T(8,128)(2,1)S(1)}, bf16[64,128]{1,0:T(8,128)(2,1)S(1)}, u32[]{:S(2)}, u32[]{:S(2)}) collective-permute-start(bf16[64,128]{1,0:T(8,128)(2,1)S(1)} %get-tuple-element.31), channel_id=1, source_target_pairs={{0,1},{1,0},{2,3},{3,2},{4,5},{5,4},{6,7},{7,6},{8,9},{9,8},{10,11... | collective-permute-start | bytes 49160 | tf_op jit(solution)/shard_map/ppermute | solution.py:426
  19.2 0.1 copy.12
  19.3 0.2 reshape.36.wa_ref
  19.5 2.5 %collective-permute-done.2.far_ref = bf16[64,128]{1,0:T(8,128)(2,1)S(1)} collective-permute-done((bf16[64,128]{1,0:T(8,128)(2,1)S(1)}, bf16[64,128]{1,0:T(8,128)(2,1)S(1)}, u32[]{:S(2)}, u32[]{:S(2)}) %collective-permute-start.2) | collective-permute-done | bytes 16416 | tf_op jit(solution)/shard_map/ppermute | solution.py:425
  22.0 0.7 %collective-permute-done.3.near_ref = bf16[64,128]{1,0:T(8,128)(2,1)S(1)} collective-permute-done((bf16[64,128]{1,0:T(8,128)(2,1)S(1)}, bf16[64,128]{1,0:T(8,128)(2,1)S(1)}, u32[]{:S(2)}, u32[]{:S(2)}) %collective-permute-start.3) | collective-permute-done | bytes 16416 | tf_op jit(solution)/shard_map/ppermute | solution.py:426
  22.6 1.0 %shard_map.62 = (bf16[2,64,128]{2,1,0:T(8,128)(2,1)S(1)}, bf16[64,128]{1,0:T(8,128)(2,1)S(1)}, bf16[4,64,128]{2,1,0:T(8,128)(2,1)S(1)}, bf16[64,384]{1,0:T(8,128)(2,1)S(1)}, f32[32,1,1152]{2,1,0:T(1,128)S(1)}) custom-call(bf16[32,64,128]{2,1,0:T(8,128)(2,1)S(1)} %get-tuple-element.23.fr_ref, bf16[32,64,128]{2,1,0:T(8,128)(2,1)S(1)} %get-tuple-element.24.gr_ref, ...), custom_call_target="tpu_custom_call" | custom-call | flops 75497472 | bytes 1818624 | tf_op jit(solution)/shard_map/pallas_call | solution.py:39
  23.7 12.9 %all_to_all.15.parts_ref = f32[32,1,1152]{2,1,0:T(1,128)S(1)} all-to-all(f32[32,1,1152]{2,1,0:T(1,128)S(1)} %get-tuple-element.35), channel_id=1, replica_groups={{65,80,81,96,97,112,113,128,129,144,145,160,161,176,177,192,193,208,209..., dimensions={0} | all-to-all | bytes 294912 | tf_op jit(solution)/shard_map/all_to_all | solution.py:445
  36.6 0.1 shard_map.64
  36.7 8.5 %all_to_all.16.after_ref.parts_ref = f32[8,1,1152]{2,1,0:T(1,128)S(1)} all-to-all(f32[8,1,1152]{2,1,0:T(1,128)S(1)} %shard_map.64), channel_id=1, replica_groups={{8,10,12,14,0,2,4,6},{9,11,13,15,1,3,5,7},{24,26,28,30,16,18,20,22},{25..., dimensions={0} | all-to-all | bytes 73728 | tf_op jit(solution)/shard_map/all_to_all | solution.py:445
  45.2 0.7 %shard_map.66 = bf16[32,2,640]{2,1,0:T(2,128)(2,1)} custom-call(f32[8,1,1152]{2,1,0:T(1,128)S(1)} %all_to_all.16.after_ref.parts_ref), custom_call_target="tpu_custom_call" | custom-call | bytes 118784 | tf_op jit(solution)/shard_map/pallas_call | solution.py:39
  45.9 9.8 %all-to-all-start.2 = ((bf16[32,2,640]{2,1,0:T(2,128)(2,1)}), bf16[32,2,640]{2,1,0:T(2,128)(2,1)S(1)}, u32[]{:S(2)}, u32[]{:S(2)}) async-start(bf16[32,2,640]{2,1,0:T(2,128)(2,1)} %shard_map.66), calls=%async_computation.2 | async-start | bytes 163840 | tf_op jit(solution)/shard_map/all_to_all | solution.py:445
  55.6 0.1 copy.15.wb3_ref
  55.8 0.1 copy.14.wb_ref
  55.9 1.8 %shard_map.63 = bf16[2048,128]{1,0:T(8,128)(2,1)} custom-call(bf16[30,64,128]{2,1,0:T(8,128)(2,1)S(1)} %get-tuple-element.25.mid_ref, bf16[2,64,128]{2,1,0:T(8,128)(2,1)S(1)} %get-tuple-element.33.rim_ref, bf16[64,128]{1,0:T(8,128)(2,1)S(1)} %get-tuple-element.34.strip_ref), custom_call_target="tpu_custom_call" | custom-call | bytes 1064960 | tf_op jit(solution)/shard_map/pallas_call | solution.py:39
  57.8 3.2 %shard_map.65 = bf16[2048,128]{1,0:T(8,128)(2,1)} custom-call(f32[8,1,1152]{2,1,0:T(1,128)S(1)} %all_to_all.16.after_ref.parts_ref, bf16[30,64,128]{2,1,0:T(8,128)(2,1)S(1)} %get-tuple-element.36.mid_ref, bf16[4,64,128]{2,1,0:T(8,128)(2,1)S(1)} %get-tuple-element.37.rim_ref, bf16[64,384]{1,0:T(8,128)(2,1)S(1)} %get-tuple-element.38.dstrip_ref, ...), custom_call_target="tpu_custom_call" | custom-call | flops 301989888 | bytes 1839104 | tf_op jit(solution)/shard_map/pallas_call | solution.py:39
  61.0 0.0 all-to-all-done.2.parts_ref
  61.0 0.9 %shard_map.67 = f32[9,64,64]{2,1,0:T(8,128)} custom-call(bf16[32,2,640]{2,1,0:T(2,128)(2,1)S(1)} %all-to-all-done.2.parts_ref), custom_call_target="tpu_custom_call" | custom-call | bytes 229376 | tf_op jit(solution)/shard_map/pallas_call | solution.py:39
  (1 shorter events, 0.0 us)
Async XLA Ops:
  0.6 10.2 %copy-start = (bf16[3,3,64,64]{3,2,1,0:T(8,128)(2,1)S(1)}, bf16[3,3,64,64]{3,2,1,0:T(8,128)(2,1)}, u32[]{:S(2)}) copy-start(bf16[3,3,64,64]{3,2,1,0:T(8,128)(2,1)} %param.4) | copy-start | bytes 221188
  2.1 13.4 %collective-permute-start = (bf16[192,128]{1,0:T(8,128)(2,1)S(1)}, bf16[192,128]{1,0:T(8,128)(2,1)S(1)}, u32[]{:S(2)}, u32[]{:S(2)}) collective-permute-start(bf16[192,128]{1,0:T(8,128)(2,1)S(1)} %get-tuple-element.27), channel_id=1, source_target_pairs={{0,8},{1,9},{2,10},{3,11},{4,12},{5,13},{6,14},{7,15},{8,0},{9,1},... | collective-permute-start | bytes 147464 | tf_op jit(solution)/shard_map/ppermute | solution.py:394
  4.8 10.7 %collective-permute-start.1 = (bf16[192,128]{1,0:T(8,128)(2,1)S(1)}, bf16[192,128]{1,0:T(8,128)(2,1)S(1)}, u32[]{:S(2)}, u32[]{:S(2)}) collective-permute-start(bf16[192,128]{1,0:T(8,128)(2,1)S(1)} %get-tuple-element.28), channel_id=1, source_target_pairs={{0,16},{16,0},{32,48},{48,32},{64,80},{80,64},{96,112},{112,96},{1... | collective-permute-start | bytes 147464 | tf_op jit(solution)/shard_map/ppermute | solution.py:395
  15.7 6.3 %collective-permute-start.2 = (bf16[64,128]{1,0:T(8,128)(2,1)S(1)}, bf16[64,128]{1,0:T(8,128)(2,1)S(1)}, u32[]{:S(2)}, u32[]{:S(2)}) collective-permute-start(bf16[64,128]{1,0:T(8,128)(2,1)S(1)} %get-tuple-element.30), channel_id=1, source_target_pairs={{0,15},{1,2},{2,1},{3,4},{4,3},{5,6},{6,5},{7,8},{8,7},{9,10},{10,... | collective-permute-start | bytes 49160 | tf_op jit(solution)/shard_map/ppermute | solution.py:425
  18.2 4.4 %collective-permute-start.3 = (bf16[64,128]{1,0:T(8,128)(2,1)S(1)}, bf16[64,128]{1,0:T(8,128)(2,1)S(1)}, u32[]{:S(2)}, u32[]{:S(2)}) collective-permute-start(bf16[64,128]{1,0:T(8,128)(2,1)S(1)} %get-tuple-element.31), channel_id=1, source_target_pairs={{0,1},{1,0},{2,3},{3,2},{4,5},{5,4},{6,7},{7,6},{8,9},{9,8},{10,11... | collective-permute-start | bytes 49160 | tf_op jit(solution)/shard_map/ppermute | solution.py:426
  45.9 15.1 %all-to-all-start.2 = ((bf16[32,2,640]{2,1,0:T(2,128)(2,1)}), bf16[32,2,640]{2,1,0:T(2,128)(2,1)S(1)}, u32[]{:S(2)}, u32[]{:S(2)}) async-start(bf16[32,2,640]{2,1,0:T(2,128)(2,1)} %shard_map.66), calls=%async_computation.2 | async-start | bytes 163840 | tf_op jit(solution)/shard_map/all_to_all | solution.py:445

commit v11 on v10

--- a/solution.py
+++ b/solution.py
@@ -181,7 +181,7 @@
 
 
 def border_body(
-    fr_ref, gr_ref, edge_ref, far_ref, near_ref, outer_ref, inner_ref, w_ref, wa_ref, part_ref,
+    fr_ref, gr_ref, edge_ref, far_ref, near_ref, outer_ref, inner_ref, w_ref, wa_ref, part_ref, wb_ref, wb3_ref,
     out_ref, outstrip_ref, delta_ref, dstrip_ref, grad_ref, xs,
 ):
     lat = lax.axis_index("lat")
@@ -434,11 +434,12 @@
             ((CH, 3 * COLS), bf16),
             ((plane, 1, piece), f32),
         ],
-        (fr, gr, edge, far, near, outer, inner, w, w3, grad_mid),
+        (fr, gr, edge, far, near, outer, inner, w, w3, grad_mid, wb, wb3),
         [pltpu.VMEM((8, TAPS, COLS), bf16)],
         conv_flops // 4,
     )
 
+    root = (5 * plane // 8) % plane
     def exchange(parts, axes, first):
         count = lax.axis_size(axes)
         order = [(first + i) % count for i in range(count)]
@@ -448,7 +449,7 @@
         return call(fold_body, [(shape, dtype)], (parts,))[0]
 
     writing = [pltpu.VMEM(flat, f32), pltpu.VMEM(flat, bf16), pltpu.SemaphoreType.DMA((PIECES,))]
-    parts = exchange(grad, PLANE, plane // 4 + 1)
+    parts = exchange(grad, PLANE, root)
     (output,) = call(restore_body, [(flat, bf16)], (out_mid, out_rim, out_strip), writing, out_space=pl.ANY)
     parts = exchange(spread(parts, (lax.axis_size("z"), 1, piece), f32), "z", lax.axis_size("z") // 2)
     (grad_input,) = call(
@@ -460,7 +461,7 @@
         out_space=pl.ANY,
     )
     packed = (plane, 2, -(-piece // (2 * COLS)) * COLS)
-    parts = exchange(spread(parts, packed, bf16), PLANE, plane // 4 + 1)
+    parts = exchange(spread(parts, packed, bf16), PLANE, root)
     (grad_kernel,) = call(
         unpack_body,
         [((9, CH, CH), f32)],

time: 62.2 us -> 60.4 us (0.971)
  starting transfers between devices: 22 us -> 18.7 us
  waiting for transfers between devices: 3.14 us -> 4.01 us
  blocking collectives: 21.4 us -> 22.1 us
    all_to_all x1, starting transfers between devices: 9.75 us -> 6.44 us  [exchange(): return lax.all_to_all(parts, axes, 0, 0, axis_index_groups=[order])]
    all_to_all x1, waiting for transfers between devices: 0.01 us -> 1.16 us  [exchange(): return lax.all_to_all(parts, axes, 0, 0, axis_index_groups=[order])]
    all_to_all x2, blocking collectives: 21.4 us -> 22.1 us  [exchange(): return lax.all_to_all(parts, axes, 0, 0, axis_index_groups=[order])]
  transfers between devices with their start and end apart: 5 -> 5, of which waited for: 2 -> 3; matrix products, arithmetic and copies ran while one was open for 1% -> 1% of each run, Pallas kernels for 15% -> 16%
where the time goes in v11:
time: 60.4 us; the launch traced here: 60.2 us
  blocking collectives  22.1 us (37%)
  starting transfers between devices  18.7 us (31%)
  Pallas kernels  13.7 us (23%)
  waiting for transfers between devices  4.01 us (7%)
  local copies, waits for them, and re-layouts  0.87 us (1%)
  between operations  0.74 us (1%)
    all_to_all x2, blocking collectives, exchange(): return lax.all_to_all(parts, axes, 0, 0, axis_index_groups=[order])  22.1 us
    pallas_call x10, Pallas kernels, call(): pl.pallas_call(body, out_shape=outs, in_specs=[pl.BlockSpec(memory_space=...  13.7 us
    all_to_all x1, starting transfers between devices, exchange(): return lax.all_to_all(parts, axes, 0, 0, axis_index_groups=[order])  6.44 us
    ppermute x1, starting transfers between devices, on_device(): inner = lax.ppermute(inner, 'lat', [(i, i ^ 1) for i in range(lat_count)])  6.09 us
    ppermute x1, starting transfers between devices, on_device(): outer = lax.ppermute(outer, EVERY, outer_pairs(lat_count, lon_count))  2.69 us
    ppermute x1, starting transfers between devices, on_device(): far = lax.ppermute(far, LON, swaps)  2.55 us
    ppermute x1, waiting for transfers between devices, on_device(): far = lax.ppermute(far, LON, swaps)  2.19 us
  transfers between devices with their start and end apart: 5, of which 3 were waited for; matrix products, arithmetic and copies ran while one was open for 1% of the time, Pallas kernels for 16%

profile of v11, /device:TPU:1, one launch (start us, length us, event | category | flops | bytes accessed | tf_op | source)
XLA Modules:
  0.0 60.2 jit_solution(18384754663536809626)
XLA Ops:
  0.6 0.0 copy-start
  0.6 1.4 %shard_map.58 = (bf16[192,128]{1,0:T(8,128)(2,1)S(1)}, bf16[192,128]{1,0:T(8,128)(2,1)S(1)}, bf16[2048,128]{1,0:T(8,128)(2,1)S(1)}, bf16[2048,128]{1,0:T(8,128)(2,1)S(1)}) custom-call(bf16[2048,128]{1,0:T(8,128)(2,1)} %bitcast.20, bf16[2048,128]{1,0:T(8,128)(2,1)} %bitcast.21), custom_call_target="tpu_custom_call" | custom-call | bytes 2195456 | tf_op jit(solution)/shard_map/pallas_call | solution.py:39
  2.1 2.7 %collective-permute-start = (bf16[192,128]{1,0:T(8,128)(2,1)S(1)}, bf16[192,128]{1,0:T(8,128)(2,1)S(1)}, u32[]{:S(2)}, u32[]{:S(2)}) collective-permute-start(bf16[192,128]{1,0:T(8,128)(2,1)S(1)} %get-tuple-element.27), channel_id=1, source_target_pairs={{0,8},{1,9},{2,10},{3,11},{4,12},{5,13},{6,14},{7,15},{8,0},{9,1},... | collective-permute-start | bytes 147464 | tf_op jit(solution)/shard_map/ppermute | solution.py:394
  4.8 6.1 %collective-permute-start.1 = (bf16[192,128]{1,0:T(8,128)(2,1)S(1)}, bf16[192,128]{1,0:T(8,128)(2,1)S(1)}, u32[]{:S(2)}, u32[]{:S(2)}) collective-permute-start(bf16[192,128]{1,0:T(8,128)(2,1)S(1)} %get-tuple-element.28), channel_id=1, source_target_pairs={{0,16},{16,0},{32,48},{48,32},{64,80},{80,64},{96,112},{112,96},{1... | collective-permute-start | bytes 147464 | tf_op jit(solution)/shard_map/ppermute | solution.py:395
  10.9 0.0 copy-done
  10.9 0.1 copy.10
  11.0 0.1 copy.11.w_ref
  11.2 1.7 %shard_map.59 = (bf16[32,64,128]{2,1,0:T(8,128)(2,1)S(1)}, bf16[32,64,128]{2,1,0:T(8,128)(2,1)S(1)}, bf16[128,128]{1,0:T(8,128)(2,1)S(1)}) custom-call(bf16[2048,128]{1,0:T(8,128)(2,1)S(1)} %get-tuple-element.21.f_ref, bf16[2048,128]{1,0:T(8,128)(2,1)S(1)} %get-tuple-element.22.g_ref), custom_call_target="tpu_custom_call" | custom-call | bytes 2129920 | tf_op jit(solution)/shard_map/pallas_call | solution.py:39
  12.8 2.7 %shard_map.60 = (bf16[30,64,128]{2,1,0:T(8,128)(2,1)S(1)}, bf16[30,64,128]{2,1,0:T(8,128)(2,1)S(1)}, f32[64,576]{1,0:T(8,128)S(1)}, f32[8,128]{1,0:T(8,128)S(1)}) custom-call(bf16[32,64,128]{2,1,0:T(8,128)(2,1)S(1)} %get-tuple-element.23.fr_ref, bf16[32,64,128]{2,1,0:T(8,128)(2,1)S(1)} %get-tuple-element.24.gr_ref, bf16[64,576]{1,0:T(8,128)(2,1)S(1)} %copy.11.w_ref), custom_call_target="tpu_custom_call" | custom-call | flops 603979776 | bytes 2256896 | tf_op jit(solution)/shard_map/pallas_call | solution.py:39
  15.5 0.0 collective-permute-done.outer_ref
  15.5 0.0 collective-permute-done.1.inner_ref
  15.5 0.2 shard_map.61
  15.7 2.5 %collective-permute-start.2 = (bf16[64,128]{1,0:T(8,128)(2,1)S(1)}, bf16[64,128]{1,0:T(8,128)(2,1)S(1)}, u32[]{:S(2)}, u32[]{:S(2)}) collective-permute-start(bf16[64,128]{1,0:T(8,128)(2,1)S(1)} %get-tuple-element.30), channel_id=1, source_target_pairs={{0,15},{1,2},{2,1},{3,4},{4,3},{5,6},{6,5},{7,8},{8,7},{9,10},{10,... | collective-permute-start | bytes 49160 | tf_op jit(solution)/shard_map/ppermute | solution.py:425
  18.2 1.0 %collective-permute-start.3 = (bf16[64,128]{1,0:T(8,128)(2,1)S(1)}, bf16[64,128]{1,0:T(8,128)(2,1)S(1)}, u32[]{:S(2)}, u32[]{:S(2)}) collective-permute-start(bf16[64,128]{1,0:T(8,128)(2,1)S(1)} %get-tuple-element.31), channel_id=1, source_target_pairs={{0,1},{1,0},{2,3},{3,2},{4,5},{5,4},{6,7},{7,6},{8,9},{9,8},{10,11... | collective-permute-start | bytes 49160 | tf_op jit(solution)/shard_map/ppermute | solution.py:426
  19.2 0.1 copy.14.wb_ref
  19.4 0.1 copy.15.wb3_ref
  19.5 0.1 copy.12
  19.6 0.2 reshape.36.wa_ref
  19.8 2.2 %collective-permute-done.2.far_ref = bf16[64,128]{1,0:T(8,128)(2,1)S(1)} collective-permute-done((bf16[64,128]{1,0:T(8,128)(2,1)S(1)}, bf16[64,128]{1,0:T(8,128)(2,1)S(1)}, u32[]{:S(2)}, u32[]{:S(2)}) %collective-permute-start.2) | collective-permute-done | bytes 16416 | tf_op jit(solution)/shard_map/ppermute | solution.py:425
  22.0 0.7 %collective-permute-done.3.near_ref = bf16[64,128]{1,0:T(8,128)(2,1)S(1)} collective-permute-done((bf16[64,128]{1,0:T(8,128)(2,1)S(1)}, bf16[64,128]{1,0:T(8,128)(2,1)S(1)}, u32[]{:S(2)}, u32[]{:S(2)}) %collective-permute-start.3) | collective-permute-done | bytes 16416 | tf_op jit(solution)/shard_map/ppermute | solution.py:426
  22.6 1.0 %shard_map.62 = (bf16[2,64,128]{2,1,0:T(8,128)(2,1)S(1)}, bf16[64,128]{1,0:T(8,128)(2,1)S(1)}, bf16[4,64,128]{2,1,0:T(8,128)(2,1)S(1)}, bf16[64,384]{1,0:T(8,128)(2,1)S(1)}, f32[32,1,1152]{2,1,0:T(1,128)S(1)}) custom-call(bf16[32,64,128]{2,1,0:T(8,128)(2,1)S(1)} %get-tuple-element.23.fr_ref, bf16[32,64,128]{2,1,0:T(8,128)(2,1)S(1)} %get-tuple-element.24.gr_ref, ...), custom_call_target="tpu_custom_call" | custom-call | flops 75497472 | bytes 1966080 | tf_op jit(solution)/shard_map/pallas_call | solution.py:39
  23.7 13.6 %all_to_all.15.parts_ref = f32[32,1,1152]{2,1,0:T(1,128)S(1)} all-to-all(f32[32,1,1152]{2,1,0:T(1,128)S(1)} %get-tuple-element.35), channel_id=1, replica_groups={{160,161,176,177,192,193,208,209,224,225,240,241,0,1,16,17,32,33,48,49,..., dimensions={0} | all-to-all | bytes 294912 | tf_op jit(solution)/shard_map/all_to_all | solution.py:446
  37.3 0.1 shard_map.64
  37.4 8.5 %all_to_all.16.after_ref.parts_ref = f32[8,1,1152]{2,1,0:T(1,128)S(1)} all-to-all(f32[8,1,1152]{2,1,0:T(1,128)S(1)} %shard_map.64), channel_id=1, replica_groups={{8,10,12,14,0,2,4,6},{9,11,13,15,1,3,5,7},{24,26,28,30,16,18,20,22},{25..., dimensions={0} | all-to-all | bytes 73728 | tf_op jit(solution)/shard_map/all_to_all | solution.py:446
  45.9 0.7 %shard_map.66 = bf16[32,2,640]{2,1,0:T(2,128)(2,1)} custom-call(f32[8,1,1152]{2,1,0:T(1,128)S(1)} %all_to_all.16.after_ref.parts_ref), custom_call_target="tpu_custom_call" | custom-call | bytes 118784 | tf_op jit(solution)/shard_map/pallas_call | solution.py:39
  46.6 6.4 %all-to-all-start.2 = ((bf16[32,2,640]{2,1,0:T(2,128)(2,1)}), bf16[32,2,640]{2,1,0:T(2,128)(2,1)S(1)}, u32[]{:S(2)}, u32[]{:S(2)}) async-start(bf16[32,2,640]{2,1,0:T(2,128)(2,1)} %shard_map.66), calls=%async_computation.2 | async-start | bytes 163840 | tf_op jit(solution)/shard_map/all_to_all | solution.py:446
  53.0 1.8 %shard_map.63 = bf16[2048,128]{1,0:T(8,128)(2,1)} custom-call(bf16[30,64,128]{2,1,0:T(8,128)(2,1)S(1)} %get-tuple-element.25.mid_ref, bf16[2,64,128]{2,1,0:T(8,128)(2,1)S(1)} %get-tuple-element.33.rim_ref, bf16[64,128]{1,0:T(8,128)(2,1)S(1)} %get-tuple-element.34.strip_ref), custom_call_target="tpu_custom_call" | custom-call | bytes 1064960 | tf_op jit(solution)/shard_map/pallas_call | solution.py:39
  54.9 3.2 %shard_map.65 = bf16[2048,128]{1,0:T(8,128)(2,1)} custom-call(f32[8,1,1152]{2,1,0:T(1,128)S(1)} %all_to_all.16.after_ref.parts_ref, bf16[30,64,128]{2,1,0:T(8,128)(2,1)S(1)} %get-tuple-element.36.mid_ref, bf16[4,64,128]{2,1,0:T(8,128)(2,1)S(1)} %get-tuple-element.37.rim_ref, bf16[64,384]{1,0:T(8,128)(2,1)S(1)} %get-tuple-element.38.dstrip_ref, ...), custom_call_target="tpu_custom_call" | custom-call | flops 301989888 | bytes 1839104 | tf_op jit(solution)/shard_map/pallas_call | solution.py:39
  58.1 1.2 %all-to-all-done.2.parts_ref = bf16[32,2,640]{2,1,0:T(2,128)(2,1)S(1)} async-done(((bf16[32,2,640]{2,1,0:T(2,128)(2,1)}), bf16[32,2,640]{2,1,0:T(2,128)(2,1)S(1)}, u32[]{:S(2)}, u32[]{:S(2)}) %all-to-all-start.2) | async-done | bytes 81952 | tf_op jit(solution)/shard_map/all_to_all | solution.py:446
  59.2 0.9 %shard_map.67 = f32[9,64,64]{2,1,0:T(8,128)} custom-call(bf16[32,2,640]{2,1,0:T(2,128)(2,1)S(1)} %all-to-all-done.2.parts_ref), custom_call_target="tpu_custom_call" | custom-call | bytes 229376 | tf_op jit(solution)/shard_map/pallas_call | solution.py:39
  (1 shorter events, 0.0 us)
Async XLA Ops:
  0.6 10.2 %copy-start = (bf16[3,3,64,64]{3,2,1,0:T(8,128)(2,1)S(1)}, bf16[3,3,64,64]{3,2,1,0:T(8,128)(2,1)}, u32[]{:S(2)}) copy-start(bf16[3,3,64,64]{3,2,1,0:T(8,128)(2,1)} %param.4) | copy-start | bytes 221188
  2.1 13.4 %collective-permute-start = (bf16[192,128]{1,0:T(8,128)(2,1)S(1)}, bf16[192,128]{1,0:T(8,128)(2,1)S(1)}, u32[]{:S(2)}, u32[]{:S(2)}) collective-permute-start(bf16[192,128]{1,0:T(8,128)(2,1)S(1)} %get-tuple-element.27), channel_id=1, source_target_pairs={{0,8},{1,9},{2,10},{3,11},{4,12},{5,13},{6,14},{7,15},{8,0},{9,1},... | collective-permute-start | bytes 147464 | tf_op jit(solution)/shard_map/ppermute | solution.py:394
  4.8 10.7 %collective-permute-start.1 = (bf16[192,128]{1,0:T(8,128)(2,1)S(1)}, bf16[192,128]{1,0:T(8,128)(2,1)S(1)}, u32[]{:S(2)}, u32[]{:S(2)}) collective-permute-start(bf16[192,128]{1,0:T(8,128)(2,1)S(1)} %get-tuple-element.28), channel_id=1, source_target_pairs={{0,16},{16,0},{32,48},{48,32},{64,80},{80,64},{96,112},{112,96},{1... | collective-permute-start | bytes 147464 | tf_op jit(solution)/shard_map/ppermute | solution.py:395
  15.7 6.3 %collective-permute-start.2 = (bf16[64,128]{1,0:T(8,128)(2,1)S(1)}, bf16[64,128]{1,0:T(8,128)(2,1)S(1)}, u32[]{:S(2)}, u32[]{:S(2)}) collective-permute-start(bf16[64,128]{1,0:T(8,128)(2,1)S(1)} %get-tuple-element.30), channel_id=1, source_target_pairs={{0,15},{1,2},{2,1},{3,4},{4,3},{5,6},{6,5},{7,8},{8,7},{9,10},{10,... | collective-permute-start | bytes 49160 | tf_op jit(solution)/shard_map/ppermute | solution.py:425
  18.2 4.4 %collective-permute-start.3 = (bf16[64,128]{1,0:T(8,128)(2,1)S(1)}, bf16[64,128]{1,0:T(8,128)(2,1)S(1)}, u32[]{:S(2)}, u32[]{:S(2)}) collective-permute-start(bf16[64,128]{1,0:T(8,128)(2,1)S(1)} %get-tuple-element.31), channel_id=1, source_target_pairs={{0,1},{1,0},{2,3},{3,2},{4,5},{5,4},{6,7},{7,6},{8,9},{9,8},{10,11... | collective-permute-start | bytes 49160 | tf_op jit(solution)/shard_map/ppermute | solution.py:426
  46.6 12.7 %all-to-all-start.2 = ((bf16[32,2,640]{2,1,0:T(2,128)(2,1)}), bf16[32,2,640]{2,1,0:T(2,128)(2,1)S(1)}, u32[]{:S(2)}, u32[]{:S(2)}) async-start(bf16[32,2,640]{2,1,0:T(2,128)(2,1)} %shard_map.66), calls=%async_computation.2 | async-start | bytes 163840 | tf_op jit(solution)/shard_map/all_to_all | solution.py:446

commit v12 on v11

--- a/solution.py
+++ b/solution.py
@@ -345,9 +345,8 @@
 def unpack_body(parts_ref, out_hbm, out_ref, sems):
     count = parts_ref.shape[0]
     half = parts_ref.shape[2] // COLS
-    tiles = []
-    for q in range(2 * half):
-        tiles.append(parts_ref[:, q // half, pl.ds(q % half * COLS, COLS)].astype(f32))
+    parts = parts_ref[...].astype(f32)
+    tiles = [parts[:, q // half, q % half * COLS : (q % half + 1) * COLS] for q in range(2 * half)]
     copies = []
     for tap in range(9):
         for j in range(CH // count):

time: 60.4 us -> 60.4 us (level)
  no operation moved by 1% of the time
where the time goes in v12:
time: 60.4 us; the launch traced here: 60.2 us
  blocking collectives  22.1 us (37%)
  starting transfers between devices  18.7 us (31%)
  Pallas kernels  13.7 us (23%)
  waiting for transfers between devices  4.01 us (7%)
  local copies, waits for them, and re-layouts  0.87 us (1%)
  between operations  0.74 us (1%)
    all_to_all x2, blocking collectives, exchange(): return lax.all_to_all(parts, axes, 0, 0, axis_index_groups=[order])  22.1 us
    pallas_call x10, Pallas kernels, call(): pl.pallas_call(body, out_shape=outs, in_specs=[pl.BlockSpec(memory_space=...  13.7 us
    all_to_all x1, starting transfers between devices, exchange(): return lax.all_to_all(parts, axes, 0, 0, axis_index_groups=[order])  6.44 us
    ppermute x1, starting transfers between devices, on_device(): inner = lax.ppermute(inner, 'lat', [(i, i ^ 1) for i in range(lat_count)])  6.09 us
    ppermute x1, starting transfers between devices, on_device(): outer = lax.ppermute(outer, EVERY, outer_pairs(lat_count, lon_count))  2.69 us
    ppermute x1, starting transfers between devices, on_device(): far = lax.ppermute(far, LON, swaps)  2.55 us
    ppermute x1, waiting for transfers between devices, on_device(): far = lax.ppermute(far, LON, swaps)  2.19 us
  transfers between devices with their start and end apart: 5, of which 3 were waited for; matrix products, arithmetic and copies ran while one was open for 1% of the time, Pallas kernels for 16%

profile of v12, /device:TPU:1, one launch (start us, length us, event | category | flops | bytes accessed | tf_op | source)
XLA Modules:
  0.0 60.2 jit_solution(3777653166636321723)
XLA Ops:
  0.6 0.0 copy-start
  0.6 1.4 %shard_map.58 = (bf16[192,128]{1,0:T(8,128)(2,1)S(1)}, bf16[192,128]{1,0:T(8,128)(2,1)S(1)}, bf16[2048,128]{1,0:T(8,128)(2,1)S(1)}, bf16[2048,128]{1,0:T(8,128)(2,1)S(1)}) custom-call(bf16[2048,128]{1,0:T(8,128)(2,1)} %bitcast.20, bf16[2048,128]{1,0:T(8,128)(2,1)} %bitcast.21), custom_call_target="tpu_custom_call" | custom-call | bytes 2195456 | tf_op jit(solution)/shard_map/pallas_call | solution.py:39
  2.1 2.7 %collective-permute-start = (bf16[192,128]{1,0:T(8,128)(2,1)S(1)}, bf16[192,128]{1,0:T(8,128)(2,1)S(1)}, u32[]{:S(2)}, u32[]{:S(2)}) collective-permute-start(bf16[192,128]{1,0:T(8,128)(2,1)S(1)} %get-tuple-element.27), channel_id=1, source_target_pairs={{0,8},{1,9},{2,10},{3,11},{4,12},{5,13},{6,14},{7,15},{8,0},{9,1},... | collective-permute-start | bytes 147464 | tf_op jit(solution)/shard_map/ppermute | solution.py:393
  4.8 6.1 %collective-permute-start.1 = (bf16[192,128]{1,0:T(8,128)(2,1)S(1)}, bf16[192,128]{1,0:T(8,128)(2,1)S(1)}, u32[]{:S(2)}, u32[]{:S(2)}) collective-permute-start(bf16[192,128]{1,0:T(8,128)(2,1)S(1)} %get-tuple-element.28), channel_id=1, source_target_pairs={{0,16},{16,0},{32,48},{48,32},{64,80},{80,64},{96,112},{112,96},{1... | collective-permute-start | bytes 147464 | tf_op jit(solution)/shard_map/ppermute | solution.py:394
  10.9 0.0 copy-done
  10.9 0.1 copy.10
  11.0 0.1 copy.11.w_ref
  11.2 1.7 %shard_map.59 = (bf16[32,64,128]{2,1,0:T(8,128)(2,1)S(1)}, bf16[32,64,128]{2,1,0:T(8,128)(2,1)S(1)}, bf16[128,128]{1,0:T(8,128)(2,1)S(1)}) custom-call(bf16[2048,128]{1,0:T(8,128)(2,1)S(1)} %get-tuple-element.21.f_ref, bf16[2048,128]{1,0:T(8,128)(2,1)S(1)} %get-tuple-element.22.g_ref), custom_call_target="tpu_custom_call" | custom-call | bytes 2129920 | tf_op jit(solution)/shard_map/pallas_call | solution.py:39
  12.8 2.7 %shard_map.60 = (bf16[30,64,128]{2,1,0:T(8,128)(2,1)S(1)}, bf16[30,64,128]{2,1,0:T(8,128)(2,1)S(1)}, f32[64,576]{1,0:T(8,128)S(1)}, f32[8,128]{1,0:T(8,128)S(1)}) custom-call(bf16[32,64,128]{2,1,0:T(8,128)(2,1)S(1)} %get-tuple-element.23.fr_ref, bf16[32,64,128]{2,1,0:T(8,128)(2,1)S(1)} %get-tuple-element.24.gr_ref, bf16[64,576]{1,0:T(8,128)(2,1)S(1)} %copy.11.w_ref), custom_call_target="tpu_custom_call" | custom-call | flops 603979776 | bytes 2256896 | tf_op jit(solution)/shard_map/pallas_call | solution.py:39
  15.5 0.0 collective-permute-done.outer_ref
  15.5 0.0 collective-permute-done.1.inner_ref
  15.5 0.2 shard_map.61
  15.7 2.5 %collective-permute-start.2 = (bf16[64,128]{1,0:T(8,128)(2,1)S(1)}, bf16[64,128]{1,0:T(8,128)(2,1)S(1)}, u32[]{:S(2)}, u32[]{:S(2)}) collective-permute-start(bf16[64,128]{1,0:T(8,128)(2,1)S(1)} %get-tuple-element.30), channel_id=1, source_target_pairs={{0,15},{1,2},{2,1},{3,4},{4,3},{5,6},{6,5},{7,8},{8,7},{9,10},{10,... | collective-permute-start | bytes 49160 | tf_op jit(solution)/shard_map/ppermute | solution.py:424
  18.2 1.0 %collective-permute-start.3 = (bf16[64,128]{1,0:T(8,128)(2,1)S(1)}, bf16[64,128]{1,0:T(8,128)(2,1)S(1)}, u32[]{:S(2)}, u32[]{:S(2)}) collective-permute-start(bf16[64,128]{1,0:T(8,128)(2,1)S(1)} %get-tuple-element.31), channel_id=1, source_target_pairs={{0,1},{1,0},{2,3},{3,2},{4,5},{5,4},{6,7},{7,6},{8,9},{9,8},{10,11... | collective-permute-start | bytes 49160 | tf_op jit(solution)/shard_map/ppermute | solution.py:425
  19.2 0.1 copy.14.wb_ref
  19.4 0.1 copy.15.wb3_ref
  19.5 0.1 copy.12
  19.6 0.2 reshape.36.wa_ref
  19.8 2.2 %collective-permute-done.2.far_ref = bf16[64,128]{1,0:T(8,128)(2,1)S(1)} collective-permute-done((bf16[64,128]{1,0:T(8,128)(2,1)S(1)}, bf16[64,128]{1,0:T(8,128)(2,1)S(1)}, u32[]{:S(2)}, u32[]{:S(2)}) %collective-permute-start.2) | collective-permute-done | bytes 16416 | tf_op jit(solution)/shard_map/ppermute | solution.py:424
  22.0 0.7 %collective-permute-done.3.near_ref = bf16[64,128]{1,0:T(8,128)(2,1)S(1)} collective-permute-done((bf16[64,128]{1,0:T(8,128)(2,1)S(1)}, bf16[64,128]{1,0:T(8,128)(2,1)S(1)}, u32[]{:S(2)}, u32[]{:S(2)}) %collective-permute-start.3) | collective-permute-done | bytes 16416 | tf_op jit(solution)/shard_map/ppermute | solution.py:425
  22.6 1.0 %shard_map.62 = (bf16[2,64,128]{2,1,0:T(8,128)(2,1)S(1)}, bf16[64,128]{1,0:T(8,128)(2,1)S(1)}, bf16[4,64,128]{2,1,0:T(8,128)(2,1)S(1)}, bf16[64,384]{1,0:T(8,128)(2,1)S(1)}, f32[32,1,1152]{2,1,0:T(1,128)S(1)}) custom-call(bf16[32,64,128]{2,1,0:T(8,128)(2,1)S(1)} %get-tuple-element.23.fr_ref, bf16[32,64,128]{2,1,0:T(8,128)(2,1)S(1)} %get-tuple-element.24.gr_ref, ...), custom_call_target="tpu_custom_call" | custom-call | flops 75497472 | bytes 1966080 | tf_op jit(solution)/shard_map/pallas_call | solution.py:39
  23.7 13.6 %all_to_all.15.parts_ref = f32[32,1,1152]{2,1,0:T(1,128)S(1)} all-to-all(f32[32,1,1152]{2,1,0:T(1,128)S(1)} %get-tuple-element.35), channel_id=1, replica_groups={{160,161,176,177,192,193,208,209,224,225,240,241,0,1,16,17,32,33,48,49,..., dimensions={0} | all-to-all | bytes 294912 | tf_op jit(solution)/shard_map/all_to_all | solution.py:445
  37.3 0.1 shard_map.64
  37.4 8.5 %all_to_all.16.after_ref.parts_ref = f32[8,1,1152]{2,1,0:T(1,128)S(1)} all-to-all(f32[8,1,1152]{2,1,0:T(1,128)S(1)} %shard_map.64), channel_id=1, replica_groups={{8,10,12,14,0,2,4,6},{9,11,13,15,1,3,5,7},{24,26,28,30,16,18,20,22},{25..., dimensions={0} | all-to-all | bytes 73728 | tf_op jit(solution)/shard_map/all_to_all | solution.py:445
  45.9 0.7 %shard_map.66 = bf16[32,2,640]{2,1,0:T(2,128)(2,1)} custom-call(f32[8,1,1152]{2,1,0:T(1,128)S(1)} %all_to_all.16.after_ref.parts_ref), custom_call_target="tpu_custom_call" | custom-call | bytes 118784 | tf_op jit(solution)/shard_map/pallas_call | solution.py:39
  46.6 6.4 %all-to-all-start.2 = ((bf16[32,2,640]{2,1,0:T(2,128)(2,1)}), bf16[32,2,640]{2,1,0:T(2,128)(2,1)S(1)}, u32[]{:S(2)}, u32[]{:S(2)}) async-start(bf16[32,2,640]{2,1,0:T(2,128)(2,1)} %shard_map.66), calls=%async_computation.2 | async-start | bytes 163840 | tf_op jit(solution)/shard_map/all_to_all | solution.py:445
  53.0 1.8 %shard_map.63 = bf16[2048,128]{1,0:T(8,128)(2,1)} custom-call(bf16[30,64,128]{2,1,0:T(8,128)(2,1)S(1)} %get-tuple-element.25.mid_ref, bf16[2,64,128]{2,1,0:T(8,128)(2,1)S(1)} %get-tuple-element.33.rim_ref, bf16[64,128]{1,0:T(8,128)(2,1)S(1)} %get-tuple-element.34.strip_ref), custom_call_target="tpu_custom_call" | custom-call | bytes 1064960 | tf_op jit(solution)/shard_map/pallas_call | solution.py:39
  54.9 3.2 %shard_map.65 = bf16[2048,128]{1,0:T(8,128)(2,1)} custom-call(f32[8,1,1152]{2,1,0:T(1,128)S(1)} %all_to_all.16.after_ref.parts_ref, bf16[30,64,128]{2,1,0:T(8,128)(2,1)S(1)} %get-tuple-element.36.mid_ref, bf16[4,64,128]{2,1,0:T(8,128)(2,1)S(1)} %get-tuple-element.37.rim_ref, bf16[64,384]{1,0:T(8,128)(2,1)S(1)} %get-tuple-element.38.dstrip_ref, ...), custom_call_target="tpu_custom_call" | custom-call | flops 301989888 | bytes 1839104 | tf_op jit(solution)/shard_map/pallas_call | solution.py:39
  58.1 1.2 %all-to-all-done.2.parts_ref = bf16[32,2,640]{2,1,0:T(2,128)(2,1)S(1)} async-done(((bf16[32,2,640]{2,1,0:T(2,128)(2,1)}), bf16[32,2,640]{2,1,0:T(2,128)(2,1)S(1)}, u32[]{:S(2)}, u32[]{:S(2)}) %all-to-all-start.2) | async-done | bytes 81952 | tf_op jit(solution)/shard_map/all_to_all | solution.py:445
  59.2 0.9 %shard_map.67 = f32[9,64,64]{2,1,0:T(8,128)} custom-call(bf16[32,2,640]{2,1,0:T(2,128)(2,1)S(1)} %all-to-all-done.2.parts_ref), custom_call_target="tpu_custom_call" | custom-call | bytes 229376 | tf_op jit(solution)/shard_map/pallas_call | solution.py:39
  (1 shorter events, 0.0 us)
Async XLA Ops:
  0.6 10.2 %copy-start = (bf16[3,3,64,64]{3,2,1,0:T(8,128)(2,1)S(1)}, bf16[3,3,64,64]{3,2,1,0:T(8,128)(2,1)}, u32[]{:S(2)}) copy-start(bf16[3,3,64,64]{3,2,1,0:T(8,128)(2,1)} %param.4) | copy-start | bytes 221188
  2.1 13.4 %collective-permute-start = (bf16[192,128]{1,0:T(8,128)(2,1)S(1)}, bf16[192,128]{1,0:T(8,128)(2,1)S(1)}, u32[]{:S(2)}, u32[]{:S(2)}) collective-permute-start(bf16[192,128]{1,0:T(8,128)(2,1)S(1)} %get-tuple-element.27), channel_id=1, source_target_pairs={{0,8},{1,9},{2,10},{3,11},{4,12},{5,13},{6,14},{7,15},{8,0},{9,1},... | collective-permute-start | bytes 147464 | tf_op jit(solution)/shard_map/ppermute | solution.py:393
  4.8 10.7 %collective-permute-start.1 = (bf16[192,128]{1,0:T(8,128)(2,1)S(1)}, bf16[192,128]{1,0:T(8,128)(2,1)S(1)}, u32[]{:S(2)}, u32[]{:S(2)}) collective-permute-start(bf16[192,128]{1,0:T(8,128)(2,1)S(1)} %get-tuple-element.28), channel_id=1, source_target_pairs={{0,16},{16,0},{32,48},{48,32},{64,80},{80,64},{96,112},{112,96},{1... | collective-permute-start | bytes 147464 | tf_op jit(solution)/shard_map/ppermute | solution.py:394
  15.7 6.3 %collective-permute-start.2 = (bf16[64,128]{1,0:T(8,128)(2,1)S(1)}, bf16[64,128]{1,0:T(8,128)(2,1)S(1)}, u32[]{:S(2)}, u32[]{:S(2)}) collective-permute-start(bf16[64,128]{1,0:T(8,128)(2,1)S(1)} %get-tuple-element.30), channel_id=1, source_target_pairs={{0,15},{1,2},{2,1},{3,4},{4,3},{5,6},{6,5},{7,8},{8,7},{9,10},{10,... | collective-permute-start | bytes 49160 | tf_op jit(solution)/shard_map/ppermute | solution.py:424
  18.2 4.4 %collective-permute-start.3 = (bf16[64,128]{1,0:T(8,128)(2,1)S(1)}, bf16[64,128]{1,0:T(8,128)(2,1)S(1)}, u32[]{:S(2)}, u32[]{:S(2)}) collective-permute-start(bf16[64,128]{1,0:T(8,128)(2,1)S(1)} %get-tuple-element.31), channel_id=1, source_target_pairs={{0,1},{1,0},{2,3},{3,2},{4,5},{5,4},{6,7},{7,6},{8,9},{9,8},{10,11... | collective-permute-start | bytes 49160 | tf_op jit(solution)/shard_map/ppermute | solution.py:425
  46.6 12.7 %all-to-all-start.2 = ((bf16[32,2,640]{2,1,0:T(2,128)(2,1)}), bf16[32,2,640]{2,1,0:T(2,128)(2,1)S(1)}, u32[]{:S(2)}, u32[]{:S(2)}) async-start(bf16[32,2,640]{2,1,0:T(2,128)(2,1)} %shard_map.66), calls=%async_computation.2 | async-start | bytes 163840 | tf_op jit(solution)/shard_map/all_to_all | solution.py:445

commit v13 on v12

--- a/solution.py
+++ b/solution.py
@@ -438,7 +438,7 @@
         conv_flops // 4,
     )
 
-    root = (5 * plane // 8) % plane
+    root = 6 * plane // 8
     def exchange(parts, axes, first):
         count = lax.axis_size(axes)
         order = [(first + i) % count for i in range(count)]

time: 60.4 us -> 60.5 us (level)
  starting transfers between devices: 18.7 us -> 20.3 us
  waiting for transfers between devices: 4.01 us -> 2.85 us
    all_to_all x1, starting transfers between devices: 6.44 us -> 8.04 us  [exchange(): return lax.all_to_all(parts, axes, 0, 0, axis_index_groups=[order])]
    all_to_all x1, waiting for transfers between devices: 1.16 us -> 0.01 us  [exchange(): return lax.all_to_all(parts, axes, 0, 0, axis_index_groups=[order])]
  transfers between devices with their start and end apart: 5 -> 5, of which waited for: 3 -> 2; matrix products, arithmetic and copies ran while one was open for 1% -> 1% of each run, Pallas kernels for 16% -> 16%
where the time goes in v13:
time: 60.5 us; the launch traced here: 60.2 us
  blocking collectives  21.8 us (36%)
  starting transfers between devices  20.3 us (34%)
  Pallas kernels  13.7 us (23%)
  waiting for transfers between devices  2.85 us (5%)
  local copies, waits for them, and re-layouts  0.87 us (1%)
  between operations  0.75 us (1%)
    all_to_all x2, blocking collectives, exchange(): return lax.all_to_all(parts, axes, 0, 0, axis_index_groups=[order])  21.8 us
    pallas_call x10, Pallas kernels, call(): pl.pallas_call(body, out_shape=outs, in_specs=[pl.BlockSpec(memory_space=...  13.7 us
    all_to_all x1, starting transfers between devices, exchange(): return lax.all_to_all(parts, axes, 0, 0, axis_index_groups=[order])  8.04 us
    ppermute x1, starting transfers between devices, on_device(): inner = lax.ppermute(inner, 'lat', [(i, i ^ 1) for i in range(lat_count)])  6.09 us
    ppermute x1, starting transfers between devices, on_device(): outer = lax.ppermute(outer, EVERY, outer_pairs(lat_count, lon_count))  2.69 us
    ppermute x1, starting transfers between devices, on_device(): far = lax.ppermute(far, LON, swaps)  2.55 us
    ppermute x1, waiting for transfers between devices, on_device(): far = lax.ppermute(far, LON, swaps)  2.19 us
  transfers between devices with their start and end apart: 5, of which 2 were waited for; matrix products, arithmetic and copies ran while one was open for 1% of the time, Pallas kernels for 16%

profile of v13, /device:TPU:1, one launch (start us, length us, event | category | flops | bytes accessed | tf_op | source)
XLA Modules:
  0.0 60.2 jit_solution(11421618870244366742)
XLA Ops:
  0.6 0.0 copy-start
  0.6 1.4 %shard_map.58 = (bf16[192,128]{1,0:T(8,128)(2,1)S(1)}, bf16[192,128]{1,0:T(8,128)(2,1)S(1)}, bf16[2048,128]{1,0:T(8,128)(2,1)S(1)}, bf16[2048,128]{1,0:T(8,128)(2,1)S(1)}) custom-call(bf16[2048,128]{1,0:T(8,128)(2,1)} %bitcast.20, bf16[2048,128]{1,0:T(8,128)(2,1)} %bitcast.21), custom_call_target="tpu_custom_call" | custom-call | bytes 2195456 | tf_op jit(solution)/shard_map/pallas_call | solution.py:39
  2.1 2.7 %collective-permute-start = (bf16[192,128]{1,0:T(8,128)(2,1)S(1)}, bf16[192,128]{1,0:T(8,128)(2,1)S(1)}, u32[]{:S(2)}, u32[]{:S(2)}) collective-permute-start(bf16[192,128]{1,0:T(8,128)(2,1)S(1)} %get-tuple-element.27), channel_id=1, source_target_pairs={{0,8},{1,9},{2,10},{3,11},{4,12},{5,13},{6,14},{7,15},{8,0},{9,1},... | collective-permute-start | bytes 147464 | tf_op jit(solution)/shard_map/ppermute | solution.py:393
  4.8 6.1 %collective-permute-start.1 = (bf16[192,128]{1,0:T(8,128)(2,1)S(1)}, bf16[192,128]{1,0:T(8,128)(2,1)S(1)}, u32[]{:S(2)}, u32[]{:S(2)}) collective-permute-start(bf16[192,128]{1,0:T(8,128)(2,1)S(1)} %get-tuple-element.28), channel_id=1, source_target_pairs={{0,16},{16,0},{32,48},{48,32},{64,80},{80,64},{96,112},{112,96},{1... | collective-permute-start | bytes 147464 | tf_op jit(solution)/shard_map/ppermute | solution.py:394
  10.9 0.0 copy-done
  10.9 0.1 copy.10
  11.0 0.1 copy.11.w_ref
  11.2 1.7 %shard_map.59 = (bf16[32,64,128]{2,1,0:T(8,128)(2,1)S(1)}, bf16[32,64,128]{2,1,0:T(8,128)(2,1)S(1)}, bf16[128,128]{1,0:T(8,128)(2,1)S(1)}) custom-call(bf16[2048,128]{1,0:T(8,128)(2,1)S(1)} %get-tuple-element.21.f_ref, bf16[2048,128]{1,0:T(8,128)(2,1)S(1)} %get-tuple-element.22.g_ref), custom_call_target="tpu_custom_call" | custom-call | bytes 2129920 | tf_op jit(solution)/shard_map/pallas_call | solution.py:39
  12.8 2.7 %shard_map.60 = (bf16[30,64,128]{2,1,0:T(8,128)(2,1)S(1)}, bf16[30,64,128]{2,1,0:T(8,128)(2,1)S(1)}, f32[64,576]{1,0:T(8,128)S(1)}, f32[8,128]{1,0:T(8,128)S(1)}) custom-call(bf16[32,64,128]{2,1,0:T(8,128)(2,1)S(1)} %get-tuple-element.23.fr_ref, bf16[32,64,128]{2,1,0:T(8,128)(2,1)S(1)} %get-tuple-element.24.gr_ref, bf16[64,576]{1,0:T(8,128)(2,1)S(1)} %copy.11.w_ref), custom_call_target="tpu_custom_call" | custom-call | flops 603979776 | bytes 2256896 | tf_op jit(solution)/shard_map/pallas_call | solution.py:39
  15.5 0.0 collective-permute-done.outer_ref
  15.5 0.0 collective-permute-done.1.inner_ref
  15.5 0.2 shard_map.61
  15.7 2.5 %collective-permute-start.2 = (bf16[64,128]{1,0:T(8,128)(2,1)S(1)}, bf16[64,128]{1,0:T(8,128)(2,1)S(1)}, u32[]{:S(2)}, u32[]{:S(2)}) collective-permute-start(bf16[64,128]{1,0:T(8,128)(2,1)S(1)} %get-tuple-element.30), channel_id=1, source_target_pairs={{0,15},{1,2},{2,1},{3,4},{4,3},{5,6},{6,5},{7,8},{8,7},{9,10},{10,... | collective-permute-start | bytes 49160 | tf_op jit(solution)/shard_map/ppermute | solution.py:424
  18.2 1.0 %collective-permute-start.3 = (bf16[64,128]{1,0:T(8,128)(2,1)S(1)}, bf16[64,128]{1,0:T(8,128)(2,1)S(1)}, u32[]{:S(2)}, u32[]{:S(2)}) collective-permute-start(bf16[64,128]{1,0:T(8,128)(2,1)S(1)} %get-tuple-element.31), channel_id=1, source_target_pairs={{0,1},{1,0},{2,3},{3,2},{4,5},{5,4},{6,7},{7,6},{8,9},{9,8},{10,11... | collective-permute-start | bytes 49160 | tf_op jit(solution)/shard_map/ppermute | solution.py:425
  19.2 0.1 copy.14.wb_ref
  19.4 0.1 copy.15.wb3_ref
  19.5 0.1 copy.12
  19.6 0.2 reshape.36.wa_ref
  19.8 2.2 %collective-permute-done.2.far_ref = bf16[64,128]{1,0:T(8,128)(2,1)S(1)} collective-permute-done((bf16[64,128]{1,0:T(8,128)(2,1)S(1)}, bf16[64,128]{1,0:T(8,128)(2,1)S(1)}, u32[]{:S(2)}, u32[]{:S(2)}) %collective-permute-start.2) | collective-permute-done | bytes 16416 | tf_op jit(solution)/shard_map/ppermute | solution.py:424
  22.0 0.7 %collective-permute-done.3.near_ref = bf16[64,128]{1,0:T(8,128)(2,1)S(1)} collective-permute-done((bf16[64,128]{1,0:T(8,128)(2,1)S(1)}, bf16[64,128]{1,0:T(8,128)(2,1)S(1)}, u32[]{:S(2)}, u32[]{:S(2)}) %collective-permute-start.3) | collective-permute-done | bytes 16416 | tf_op jit(solution)/shard_map/ppermute | solution.py:425
  22.6 1.0 %shard_map.62 = (bf16[2,64,128]{2,1,0:T(8,128)(2,1)S(1)}, bf16[64,128]{1,0:T(8,128)(2,1)S(1)}, bf16[4,64,128]{2,1,0:T(8,128)(2,1)S(1)}, bf16[64,384]{1,0:T(8,128)(2,1)S(1)}, f32[32,1,1152]{2,1,0:T(1,128)S(1)}) custom-call(bf16[32,64,128]{2,1,0:T(8,128)(2,1)S(1)} %get-tuple-element.23.fr_ref, bf16[32,64,128]{2,1,0:T(8,128)(2,1)S(1)} %get-tuple-element.24.gr_ref, ...), custom_call_target="tpu_custom_call" | custom-call | flops 75497472 | bytes 1966080 | tf_op jit(solution)/shard_map/pallas_call | solution.py:39
  23.7 13.2 %all_to_all.15.parts_ref = f32[32,1,1152]{2,1,0:T(1,128)S(1)} all-to-all(f32[32,1,1152]{2,1,0:T(1,128)S(1)} %get-tuple-element.35), channel_id=1, replica_groups={{192,193,208,209,224,225,240,241,0,1,16,17,32,33,48,49,64,65,80,81,96,9..., dimensions={0} | all-to-all | bytes 294912 | tf_op jit(solution)/shard_map/all_to_all | solution.py:445
  36.9 0.1 shard_map.64
  37.0 8.5 %all_to_all.16.after_ref.parts_ref = f32[8,1,1152]{2,1,0:T(1,128)S(1)} all-to-all(f32[8,1,1152]{2,1,0:T(1,128)S(1)} %shard_map.64), channel_id=1, replica_groups={{8,10,12,14,0,2,4,6},{9,11,13,15,1,3,5,7},{24,26,28,30,16,18,20,22},{25..., dimensions={0} | all-to-all | bytes 73728 | tf_op jit(solution)/shard_map/all_to_all | solution.py:445
  45.5 0.7 %shard_map.66 = bf16[32,2,640]{2,1,0:T(2,128)(2,1)} custom-call(f32[8,1,1152]{2,1,0:T(1,128)S(1)} %all_to_all.16.after_ref.parts_ref), custom_call_target="tpu_custom_call" | custom-call | bytes 118784 | tf_op jit(solution)/shard_map/pallas_call | solution.py:39
  46.2 8.0 %all-to-all-start.2 = ((bf16[32,2,640]{2,1,0:T(2,128)(2,1)}), bf16[32,2,640]{2,1,0:T(2,128)(2,1)S(1)}, u32[]{:S(2)}, u32[]{:S(2)}) async-start(bf16[32,2,640]{2,1,0:T(2,128)(2,1)} %shard_map.66), calls=%async_computation.2 | async-start | bytes 163840 | tf_op jit(solution)/shard_map/all_to_all | solution.py:445
  54.3 1.8 %shard_map.63 = bf16[2048,128]{1,0:T(8,128)(2,1)} custom-call(bf16[30,64,128]{2,1,0:T(8,128)(2,1)S(1)} %get-tuple-element.25.mid_ref, bf16[2,64,128]{2,1,0:T(8,128)(2,1)S(1)} %get-tuple-element.33.rim_ref, bf16[64,128]{1,0:T(8,128)(2,1)S(1)} %get-tuple-element.34.strip_ref), custom_call_target="tpu_custom_call" | custom-call | bytes 1064960 | tf_op jit(solution)/shard_map/pallas_call | solution.py:39
  56.1 3.2 %shard_map.65 = bf16[2048,128]{1,0:T(8,128)(2,1)} custom-call(f32[8,1,1152]{2,1,0:T(1,128)S(1)} %all_to_all.16.after_ref.parts_ref, bf16[30,64,128]{2,1,0:T(8,128)(2,1)S(1)} %get-tuple-element.36.mid_ref, bf16[4,64,128]{2,1,0:T(8,128)(2,1)S(1)} %get-tuple-element.37.rim_ref, bf16[64,384]{1,0:T(8,128)(2,1)S(1)} %get-tuple-element.38.dstrip_ref, ...), custom_call_target="tpu_custom_call" | custom-call | flops 301989888 | bytes 1839104 | tf_op jit(solution)/shard_map/pallas_call | solution.py:39
  59.3 0.0 all-to-all-done.2.parts_ref
  59.3 0.9 %shard_map.67 = f32[9,64,64]{2,1,0:T(8,128)} custom-call(bf16[32,2,640]{2,1,0:T(2,128)(2,1)S(1)} %all-to-all-done.2.parts_ref), custom_call_target="tpu_custom_call" | custom-call | bytes 229376 | tf_op jit(solution)/shard_map/pallas_call | solution.py:39
  (1 shorter events, 0.0 us)
Async XLA Ops:
  0.6 10.2 %copy-start = (bf16[3,3,64,64]{3,2,1,0:T(8,128)(2,1)S(1)}, bf16[3,3,64,64]{3,2,1,0:T(8,128)(2,1)}, u32[]{:S(2)}) copy-start(bf16[3,3,64,64]{3,2,1,0:T(8,128)(2,1)} %param.4) | copy-start | bytes 221188
  2.1 13.4 %collective-permute-start = (bf16[192,128]{1,0:T(8,128)(2,1)S(1)}, bf16[192,128]{1,0:T(8,128)(2,1)S(1)}, u32[]{:S(2)}, u32[]{:S(2)}) collective-permute-start(bf16[192,128]{1,0:T(8,128)(2,1)S(1)} %get-tuple-element.27), channel_id=1, source_target_pairs={{0,8},{1,9},{2,10},{3,11},{4,12},{5,13},{6,14},{7,15},{8,0},{9,1},... | collective-permute-start | bytes 147464 | tf_op jit(solution)/shard_map/ppermute | solution.py:393
  4.8 10.7 %collective-permute-start.1 = (bf16[192,128]{1,0:T(8,128)(2,1)S(1)}, bf16[192,128]{1,0:T(8,128)(2,1)S(1)}, u32[]{:S(2)}, u32[]{:S(2)}) collective-permute-start(bf16[192,128]{1,0:T(8,128)(2,1)S(1)} %get-tuple-element.28), channel_id=1, source_target_pairs={{0,16},{16,0},{32,48},{48,32},{64,80},{80,64},{96,112},{112,96},{1... | collective-permute-start | bytes 147464 | tf_op jit(solution)/shard_map/ppermute | solution.py:394
  15.7 6.3 %collective-permute-start.2 = (bf16[64,128]{1,0:T(8,128)(2,1)S(1)}, bf16[64,128]{1,0:T(8,128)(2,1)S(1)}, u32[]{:S(2)}, u32[]{:S(2)}) collective-permute-start(bf16[64,128]{1,0:T(8,128)(2,1)S(1)} %get-tuple-element.30), channel_id=1, source_target_pairs={{0,15},{1,2},{2,1},{3,4},{4,3},{5,6},{6,5},{7,8},{8,7},{9,10},{10,... | collective-permute-start | bytes 49160 | tf_op jit(solution)/shard_map/ppermute | solution.py:424
  18.2 4.4 %collective-permute-start.3 = (bf16[64,128]{1,0:T(8,128)(2,1)S(1)}, bf16[64,128]{1,0:T(8,128)(2,1)S(1)}, u32[]{:S(2)}, u32[]{:S(2)}) collective-permute-start(bf16[64,128]{1,0:T(8,128)(2,1)S(1)} %get-tuple-element.31), channel_id=1, source_target_pairs={{0,1},{1,0},{2,3},{3,2},{4,5},{5,4},{6,7},{7,6},{8,9},{9,8},{10,11... | collective-permute-start | bytes 49160 | tf_op jit(solution)/shard_map/ppermute | solution.py:425
  46.2 13.1 %all-to-all-start.2 = ((bf16[32,2,640]{2,1,0:T(2,128)(2,1)}), bf16[32,2,640]{2,1,0:T(2,128)(2,1)S(1)}, u32[]{:S(2)}, u32[]{:S(2)}) async-start(bf16[32,2,640]{2,1,0:T(2,128)(2,1)} %shard_map.66), calls=%async_computation.2 | async-start | bytes 163840 | tf_op jit(solution)/shard_map/all_to_all | solution.py:445

commit v14 on v12

--- a/solution.py
+++ b/solution.py
@@ -332,14 +332,28 @@
 
 def fold_body(parts_ref, out_ref):
     total = jnp.sum(parts_ref[...], 0)
-    if out_ref.shape[1] == 2:
-        width = out_ref.shape[2]
-        rest = jnp.zeros((1, 2 * width - total.shape[1]), f32)
-        total = jnp.concatenate([total, rest], 1)
-        total = jnp.concatenate([total[:, :width], total[:, width:]], 0)
     total = total.astype(out_ref.dtype)
     for i in range(out_ref.shape[0]):
         out_ref[i] = total
+
+
+def pack_chunk_body(parts_ref, out_hbm, few_ref, sems):
+    width = few_ref.shape[2]
+    total = jnp.sum(parts_ref[...], 0)
+    rest = jnp.zeros((1, 2 * width - total.shape[1]), f32)
+    total = jnp.concatenate([total, rest], 1)
+    total = jnp.concatenate([total[:, :width], total[:, width:]], 0).astype(bf16)
+    few = few_ref.shape[0]
+    for i in range(few):
+        few_ref[i] = total
+    copies = [
+        pltpu.make_async_copy(few_ref, out_hbm.at[pl.ds(i * few, few)], sems.at[i])
+        for i in range(out_hbm.shape[0] // few)
+    ]
+    for copy in copies:
+        copy.start()
+    for copy in copies:
+        copy.wait()
 
 
 def unpack_body(parts_ref, out_hbm, out_ref, sems):
@@ -460,7 +474,15 @@
         out_space=pl.ANY,
     )
     packed = (plane, 2, -(-piece // (2 * COLS)) * COLS)
-    parts = exchange(spread(parts, packed, bf16), PLANE, root)
+    few = plane // PIECES
+    (parts,) = call(
+        pack_chunk_body,
+        [(packed, bf16)],
+        (parts,),
+        [pltpu.VMEM((few,) + packed[1:], bf16), pltpu.SemaphoreType.DMA((PIECES,))],
+        out_space=pl.ANY,
+    )
+    parts = exchange(parts, PLANE, root)
     (grad_kernel,) = call(
         unpack_body,
         [((9, CH, CH), f32)],

time: 60.4 us -> 60.4 us (level)
  no operation moved by 1% of the time
where the time goes in v14:
time: 60.4 us; the launch traced here: 60.2 us
  blocking collectives  22.1 us (37%)
  starting transfers between devices  18.7 us (31%)
  Pallas kernels  13.7 us (23%)
  waiting for transfers between devices  4.01 us (7%)
  local copies, waits for them, and re-layouts  0.87 us (1%)
  between operations  0.75 us (1%)
    all_to_all x2, blocking collectives, exchange(): return lax.all_to_all(parts, axes, 0, 0, axis_index_groups=[order])  22.1 us
    pallas_call x10, Pallas kernels, call(): pl.pallas_call(body, out_shape=outs, in_specs=[pl.BlockSpec(memory_space=...  13.7 us
    all_to_all x1, starting transfers between devices, exchange(): return lax.all_to_all(parts, axes, 0, 0, axis_index_groups=[order])  6.45 us
    ppermute x1, starting transfers between devices, on_device(): inner = lax.ppermute(inner, 'lat', [(i, i ^ 1) for i in range(lat_count)])  6.09 us
    ppermute x1, starting transfers between devices, on_device(): outer = lax.ppermute(outer, EVERY, outer_pairs(lat_count, lon_count))  2.69 us
    ppermute x1, starting transfers between devices, on_device(): far = lax.ppermute(far, LON, swaps)  2.55 us
    ppermute x1, waiting for transfers between devices, on_device(): far = lax.ppermute(far, LON, swaps)  2.19 us
  transfers between devices with their start and end apart: 5, of which 3 were waited for; matrix products, arithmetic and copies ran while one was open for 1% of the time, Pallas kernels for 16%

profile of v14, /device:TPU:1, one launch (start us, length us, event | category | flops | bytes accessed | tf_op | source)
XLA Modules:
  0.0 60.2 jit_solution(6621548658133352259)
XLA Ops:
  0.6 0.0 copy-start
  0.6 1.4 %shard_map.58 = (bf16[192,128]{1,0:T(8,128)(2,1)S(1)}, bf16[192,128]{1,0:T(8,128)(2,1)S(1)}, bf16[2048,128]{1,0:T(8,128)(2,1)S(1)}, bf16[2048,128]{1,0:T(8,128)(2,1)S(1)}) custom-call(bf16[2048,128]{1,0:T(8,128)(2,1)} %bitcast.20, bf16[2048,128]{1,0:T(8,128)(2,1)} %bitcast.21), custom_call_target="tpu_custom_call" | custom-call | bytes 2195456 | tf_op jit(solution)/shard_map/pallas_call | solution.py:39
  2.1 2.7 %collective-permute-start = (bf16[192,128]{1,0:T(8,128)(2,1)S(1)}, bf16[192,128]{1,0:T(8,128)(2,1)S(1)}, u32[]{:S(2)}, u32[]{:S(2)}) collective-permute-start(bf16[192,128]{1,0:T(8,128)(2,1)S(1)} %get-tuple-element.27), channel_id=1, source_target_pairs={{0,8},{1,9},{2,10},{3,11},{4,12},{5,13},{6,14},{7,15},{8,0},{9,1},... | collective-permute-start | bytes 147464 | tf_op jit(solution)/shard_map/ppermute | solution.py:407
  4.8 6.1 %collective-permute-start.1 = (bf16[192,128]{1,0:T(8,128)(2,1)S(1)}, bf16[192,128]{1,0:T(8,128)(2,1)S(1)}, u32[]{:S(2)}, u32[]{:S(2)}) collective-permute-start(bf16[192,128]{1,0:T(8,128)(2,1)S(1)} %get-tuple-element.28), channel_id=1, source_target_pairs={{0,16},{16,0},{32,48},{48,32},{64,80},{80,64},{96,112},{112,96},{1... | collective-permute-start | bytes 147464 | tf_op jit(solution)/shard_map/ppermute | solution.py:408
  10.9 0.0 copy-done
  10.9 0.1 copy.10
  11.0 0.1 copy.11.w_ref
  11.2 1.7 %shard_map.59 = (bf16[32,64,128]{2,1,0:T(8,128)(2,1)S(1)}, bf16[32,64,128]{2,1,0:T(8,128)(2,1)S(1)}, bf16[128,128]{1,0:T(8,128)(2,1)S(1)}) custom-call(bf16[2048,128]{1,0:T(8,128)(2,1)S(1)} %get-tuple-element.21.f_ref, bf16[2048,128]{1,0:T(8,128)(2,1)S(1)} %get-tuple-element.22.g_ref), custom_call_target="tpu_custom_call" | custom-call | bytes 2129920 | tf_op jit(solution)/shard_map/pallas_call | solution.py:39
  12.8 2.7 %shard_map.60 = (bf16[30,64,128]{2,1,0:T(8,128)(2,1)S(1)}, bf16[30,64,128]{2,1,0:T(8,128)(2,1)S(1)}, f32[64,576]{1,0:T(8,128)S(1)}, f32[8,128]{1,0:T(8,128)S(1)}) custom-call(bf16[32,64,128]{2,1,0:T(8,128)(2,1)S(1)} %get-tuple-element.23.fr_ref, bf16[32,64,128]{2,1,0:T(8,128)(2,1)S(1)} %get-tuple-element.24.gr_ref, bf16[64,576]{1,0:T(8,128)(2,1)S(1)} %copy.11.w_ref), custom_call_target="tpu_custom_call" | custom-call | flops 603979776 | bytes 2256896 | tf_op jit(solution)/shard_map/pallas_call | solution.py:39
  15.5 0.0 collective-permute-done.outer_ref
  15.5 0.0 collective-permute-done.1.inner_ref
  15.5 0.2 shard_map.61
  15.7 2.5 %collective-permute-start.2 = (bf16[64,128]{1,0:T(8,128)(2,1)S(1)}, bf16[64,128]{1,0:T(8,128)(2,1)S(1)}, u32[]{:S(2)}, u32[]{:S(2)}) collective-permute-start(bf16[64,128]{1,0:T(8,128)(2,1)S(1)} %get-tuple-element.30), channel_id=1, source_target_pairs={{0,15},{1,2},{2,1},{3,4},{4,3},{5,6},{6,5},{7,8},{8,7},{9,10},{10,... | collective-permute-start | bytes 49160 | tf_op jit(solution)/shard_map/ppermute | solution.py:438
  18.2 1.0 %collective-permute-start.3 = (bf16[64,128]{1,0:T(8,128)(2,1)S(1)}, bf16[64,128]{1,0:T(8,128)(2,1)S(1)}, u32[]{:S(2)}, u32[]{:S(2)}) collective-permute-start(bf16[64,128]{1,0:T(8,128)(2,1)S(1)} %get-tuple-element.31), channel_id=1, source_target_pairs={{0,1},{1,0},{2,3},{3,2},{4,5},{5,4},{6,7},{7,6},{8,9},{9,8},{10,11... | collective-permute-start | bytes 49160 | tf_op jit(solution)/shard_map/ppermute | solution.py:439
  19.2 0.1 copy.14.wb_ref
  19.4 0.1 copy.15.wb3_ref
  19.5 0.1 copy.12
  19.6 0.2 reshape.36.wa_ref
  19.8 2.2 %collective-permute-done.2.far_ref = bf16[64,128]{1,0:T(8,128)(2,1)S(1)} collective-permute-done((bf16[64,128]{1,0:T(8,128)(2,1)S(1)}, bf16[64,128]{1,0:T(8,128)(2,1)S(1)}, u32[]{:S(2)}, u32[]{:S(2)}) %collective-permute-start.2) | collective-permute-done | bytes 16416 | tf_op jit(solution)/shard_map/ppermute | solution.py:438
  22.0 0.7 %collective-permute-done.3.near_ref = bf16[64,128]{1,0:T(8,128)(2,1)S(1)} collective-permute-done((bf16[64,128]{1,0:T(8,128)(2,1)S(1)}, bf16[64,128]{1,0:T(8,128)(2,1)S(1)}, u32[]{:S(2)}, u32[]{:S(2)}) %collective-permute-start.3) | collective-permute-done | bytes 16416 | tf_op jit(solution)/shard_map/ppermute | solution.py:439
  22.6 1.0 %shard_map.62 = (bf16[2,64,128]{2,1,0:T(8,128)(2,1)S(1)}, bf16[64,128]{1,0:T(8,128)(2,1)S(1)}, bf16[4,64,128]{2,1,0:T(8,128)(2,1)S(1)}, bf16[64,384]{1,0:T(8,128)(2,1)S(1)}, f32[32,1,1152]{2,1,0:T(1,128)S(1)}) custom-call(bf16[32,64,128]{2,1,0:T(8,128)(2,1)S(1)} %get-tuple-element.23.fr_ref, bf16[32,64,128]{2,1,0:T(8,128)(2,1)S(1)} %get-tuple-element.24.gr_ref, ...), custom_call_target="tpu_custom_call" | custom-call | flops 75497472 | bytes 1966080 | tf_op jit(solution)/shard_map/pallas_call | solution.py:39
  23.7 13.6 %all_to_all.15.parts_ref = f32[32,1,1152]{2,1,0:T(1,128)S(1)} all-to-all(f32[32,1,1152]{2,1,0:T(1,128)S(1)} %get-tuple-element.35), channel_id=1, replica_groups={{160,161,176,177,192,193,208,209,224,225,240,241,0,1,16,17,32,33,48,49,..., dimensions={0} | all-to-all | bytes 294912 | tf_op jit(solution)/shard_map/all_to_all | solution.py:459
  37.3 0.1 shard_map.64
  37.4 8.5 %all_to_all.16.after_ref.parts_ref = f32[8,1,1152]{2,1,0:T(1,128)S(1)} all-to-all(f32[8,1,1152]{2,1,0:T(1,128)S(1)} %shard_map.64), channel_id=1, replica_groups={{8,10,12,14,0,2,4,6},{9,11,13,15,1,3,5,7},{24,26,28,30,16,18,20,22},{25..., dimensions={0} | all-to-all | bytes 73728 | tf_op jit(solution)/shard_map/all_to_all | solution.py:459
  45.9 0.7 %shard_map.66 = bf16[32,2,640]{2,1,0:T(2,128)(2,1)} custom-call(f32[8,1,1152]{2,1,0:T(1,128)S(1)} %all_to_all.16.after_ref.parts_ref), custom_call_target="tpu_custom_call" | custom-call | bytes 118784 | tf_op jit(solution)/shard_map/pallas_call | solution.py:39
  46.6 6.5 %all-to-all-start.2 = ((bf16[32,2,640]{2,1,0:T(2,128)(2,1)}), bf16[32,2,640]{2,1,0:T(2,128)(2,1)S(1)}, u32[]{:S(2)}, u32[]{:S(2)}) async-start(bf16[32,2,640]{2,1,0:T(2,128)(2,1)} %shard_map.66), calls=%async_computation.2 | async-start | bytes 163840 | tf_op jit(solution)/shard_map/all_to_all | solution.py:459
  53.0 1.8 %shard_map.63 = bf16[2048,128]{1,0:T(8,128)(2,1)} custom-call(bf16[30,64,128]{2,1,0:T(8,128)(2,1)S(1)} %get-tuple-element.25.mid_ref, bf16[2,64,128]{2,1,0:T(8,128)(2,1)S(1)} %get-tuple-element.33.rim_ref, bf16[64,128]{1,0:T(8,128)(2,1)S(1)} %get-tuple-element.34.strip_ref), custom_call_target="tpu_custom_call" | custom-call | bytes 1064960 | tf_op jit(solution)/shard_map/pallas_call | solution.py:39
  54.9 3.2 %shard_map.65 = bf16[2048,128]{1,0:T(8,128)(2,1)} custom-call(f32[8,1,1152]{2,1,0:T(1,128)S(1)} %all_to_all.16.after_ref.parts_ref, bf16[30,64,128]{2,1,0:T(8,128)(2,1)S(1)} %get-tuple-element.36.mid_ref, bf16[4,64,128]{2,1,0:T(8,128)(2,1)S(1)} %get-tuple-element.37.rim_ref, bf16[64,384]{1,0:T(8,128)(2,1)S(1)} %get-tuple-element.38.dstrip_ref, ...), custom_call_target="tpu_custom_call" | custom-call | flops 301989888 | bytes 1839104 | tf_op jit(solution)/shard_map/pallas_call | solution.py:39
  58.1 1.2 %all-to-all-done.2.parts_ref = bf16[32,2,640]{2,1,0:T(2,128)(2,1)S(1)} async-done(((bf16[32,2,640]{2,1,0:T(2,128)(2,1)}), bf16[32,2,640]{2,1,0:T(2,128)(2,1)S(1)}, u32[]{:S(2)}, u32[]{:S(2)}) %all-to-all-start.2) | async-done | bytes 81952 | tf_op jit(solution)/shard_map/all_to_all | solution.py:459
  59.3 0.9 %shard_map.67 = f32[9,64,64]{2,1,0:T(8,128)} custom-call(bf16[32,2,640]{2,1,0:T(2,128)(2,1)S(1)} %all-to-all-done.2.parts_ref), custom_call_target="tpu_custom_call" | custom-call | bytes 229376 | tf_op jit(solution)/shard_map/pallas_call | solution.py:39
  (1 shorter events, 0.0 us)
Async XLA Ops:
  0.6 10.2 %copy-start = (bf16[3,3,64,64]{3,2,1,0:T(8,128)(2,1)S(1)}, bf16[3,3,64,64]{3,2,1,0:T(8,128)(2,1)}, u32[]{:S(2)}) copy-start(bf16[3,3,64,64]{3,2,1,0:T(8,128)(2,1)} %param.4) | copy-start | bytes 221188
  2.1 13.4 %collective-permute-start = (bf16[192,128]{1,0:T(8,128)(2,1)S(1)}, bf16[192,128]{1,0:T(8,128)(2,1)S(1)}, u32[]{:S(2)}, u32[]{:S(2)}) collective-permute-start(bf16[192,128]{1,0:T(8,128)(2,1)S(1)} %get-tuple-element.27), channel_id=1, source_target_pairs={{0,8},{1,9},{2,10},{3,11},{4,12},{5,13},{6,14},{7,15},{8,0},{9,1},... | collective-permute-start | bytes 147464 | tf_op jit(solution)/shard_map/ppermute | solution.py:407
  4.8 10.7 %collective-permute-start.1 = (bf16[192,128]{1,0:T(8,128)(2,1)S(1)}, bf16[192,128]{1,0:T(8,128)(2,1)S(1)}, u32[]{:S(2)}, u32[]{:S(2)}) collective-permute-start(bf16[192,128]{1,0:T(8,128)(2,1)S(1)} %get-tuple-element.28), channel_id=1, source_target_pairs={{0,16},{16,0},{32,48},{48,32},{64,80},{80,64},{96,112},{112,96},{1... | collective-permute-start | bytes 147464 | tf_op jit(solution)/shard_map/ppermute | solution.py:408
  15.7 6.3 %collective-permute-start.2 = (bf16[64,128]{1,0:T(8,128)(2,1)S(1)}, bf16[64,128]{1,0:T(8,128)(2,1)S(1)}, u32[]{:S(2)}, u32[]{:S(2)}) collective-permute-start(bf16[64,128]{1,0:T(8,128)(2,1)S(1)} %get-tuple-element.30), channel_id=1, source_target_pairs={{0,15},{1,2},{2,1},{3,4},{4,3},{5,6},{6,5},{7,8},{8,7},{9,10},{10,... | collective-permute-start | bytes 49160 | tf_op jit(solution)/shard_map/ppermute | solution.py:438
  18.2 4.4 %collective-permute-start.3 = (bf16[64,128]{1,0:T(8,128)(2,1)S(1)}, bf16[64,128]{1,0:T(8,128)(2,1)S(1)}, u32[]{:S(2)}, u32[]{:S(2)}) collective-permute-start(bf16[64,128]{1,0:T(8,128)(2,1)S(1)} %get-tuple-element.31), channel_id=1, source_target_pairs={{0,1},{1,0},{2,3},{3,2},{4,5},{5,4},{6,7},{7,6},{8,9},{9,8},{10,11... | collective-permute-start | bytes 49160 | tf_op jit(solution)/shard_map/ppermute | solution.py:439
  46.6 12.7 %all-to-all-start.2 = ((bf16[32,2,640]{2,1,0:T(2,128)(2,1)}), bf16[32,2,640]{2,1,0:T(2,128)(2,1)S(1)}, u32[]{:S(2)}, u32[]{:S(2)}) async-start(bf16[32,2,640]{2,1,0:T(2,128)(2,1)} %shard_map.66), calls=%async_computation.2 | async-start | bytes 163840 | tf_op jit(solution)/shard_map/all_to_all | solution.py:459

commit v15 on v12

--- a/solution.py
+++ b/solution.py
@@ -11,7 +11,7 @@
 gelu_scale = math.sqrt(2.0 / math.pi)
 ROWS, COLS, CH = 32, 128, 64
 TAPS = 3 * CH
-PIECES = 4
+PIECES = 8
 f32, bf16 = jnp.float32, jnp.bfloat16
 LON = ("z", "side")
 PLANE = ("lat", "side")

time: 60.4 us -> 60.4 us (level)
  no operation moved by 1% of the time
where the time goes in v15:
time: 60.4 us; the launch traced here: 60.2 us
  blocking collectives  22.1 us (37%)
  starting transfers between devices  18.7 us (31%)
  Pallas kernels  13.7 us (23%)
  waiting for transfers between devices  3.98 us (7%)
  local copies, waits for them, and re-layouts  0.87 us (1%)
  between operations  0.74 us (1%)
    all_to_all x2, blocking collectives, exchange(): return lax.all_to_all(parts, axes, 0, 0, axis_index_groups=[order])  22.1 us
    pallas_call x10, Pallas kernels, call(): pl.pallas_call(body, out_shape=outs, in_specs=[pl.BlockSpec(memory_space=...  13.7 us
    all_to_all x1, starting transfers between devices, exchange(): return lax.all_to_all(parts, axes, 0, 0, axis_index_groups=[order])  6.44 us
    ppermute x1, starting transfers between devices, on_device(): inner = lax.ppermute(inner, 'lat', [(i, i ^ 1) for i in range(lat_count)])  6.09 us
    ppermute x1, starting transfers between devices, on_device(): outer = lax.ppermute(outer, EVERY, outer_pairs(lat_count, lon_count))  2.69 us
    ppermute x1, starting transfers between devices, on_device(): far = lax.ppermute(far, LON, swaps)  2.54 us
    ppermute x1, waiting for transfers between devices, on_device(): far = lax.ppermute(far, LON, swaps)  2.19 us
  transfers between devices with their start and end apart: 5, of which 3 were waited for; matrix products, arithmetic and copies ran while one was open for 1% of the time, Pallas kernels for 16%

profile of v15, /device:TPU:1, one launch (start us, length us, event | category | flops | bytes accessed | tf_op | source)
XLA Modules:
  0.0 60.2 jit_solution(18144209755504213535)
XLA Ops:
  0.6 0.0 copy-start
  0.6 1.4 %shard_map.58 = (bf16[192,128]{1,0:T(8,128)(2,1)S(1)}, bf16[192,128]{1,0:T(8,128)(2,1)S(1)}, bf16[2048,128]{1,0:T(8,128)(2,1)S(1)}, bf16[2048,128]{1,0:T(8,128)(2,1)S(1)}) custom-call(bf16[2048,128]{1,0:T(8,128)(2,1)} %bitcast.20, bf16[2048,128]{1,0:T(8,128)(2,1)} %bitcast.21), custom_call_target="tpu_custom_call" | custom-call | bytes 2195456 | tf_op jit(solution)/shard_map/pallas_call | solution.py:39
  2.1 2.7 %collective-permute-start = (bf16[192,128]{1,0:T(8,128)(2,1)S(1)}, bf16[192,128]{1,0:T(8,128)(2,1)S(1)}, u32[]{:S(2)}, u32[]{:S(2)}) collective-permute-start(bf16[192,128]{1,0:T(8,128)(2,1)S(1)} %get-tuple-element.27), channel_id=1, source_target_pairs={{0,8},{1,9},{2,10},{3,11},{4,12},{5,13},{6,14},{7,15},{8,0},{9,1},... | collective-permute-start | bytes 147464 | tf_op jit(solution)/shard_map/ppermute | solution.py:393
  4.8 6.1 %collective-permute-start.1 = (bf16[192,128]{1,0:T(8,128)(2,1)S(1)}, bf16[192,128]{1,0:T(8,128)(2,1)S(1)}, u32[]{:S(2)}, u32[]{:S(2)}) collective-permute-start(bf16[192,128]{1,0:T(8,128)(2,1)S(1)} %get-tuple-element.28), channel_id=1, source_target_pairs={{0,16},{16,0},{32,48},{48,32},{64,80},{80,64},{96,112},{112,96},{1... | collective-permute-start | bytes 147464 | tf_op jit(solution)/shard_map/ppermute | solution.py:394
  10.9 0.0 copy-done
  10.9 0.1 copy.10
  11.0 0.1 copy.11.w_ref
  11.2 1.7 %shard_map.59 = (bf16[32,64,128]{2,1,0:T(8,128)(2,1)S(1)}, bf16[32,64,128]{2,1,0:T(8,128)(2,1)S(1)}, bf16[128,128]{1,0:T(8,128)(2,1)S(1)}) custom-call(bf16[2048,128]{1,0:T(8,128)(2,1)S(1)} %get-tuple-element.21.f_ref, bf16[2048,128]{1,0:T(8,128)(2,1)S(1)} %get-tuple-element.22.g_ref), custom_call_target="tpu_custom_call" | custom-call | bytes 2129920 | tf_op jit(solution)/shard_map/pallas_call | solution.py:39
  12.8 2.7 %shard_map.60 = (bf16[30,64,128]{2,1,0:T(8,128)(2,1)S(1)}, bf16[30,64,128]{2,1,0:T(8,128)(2,1)S(1)}, f32[64,576]{1,0:T(8,128)S(1)}, f32[8,128]{1,0:T(8,128)S(1)}) custom-call(bf16[32,64,128]{2,1,0:T(8,128)(2,1)S(1)} %get-tuple-element.23.fr_ref, bf16[32,64,128]{2,1,0:T(8,128)(2,1)S(1)} %get-tuple-element.24.gr_ref, bf16[64,576]{1,0:T(8,128)(2,1)S(1)} %copy.11.w_ref), custom_call_target="tpu_custom_call" | custom-call | flops 603979776 | bytes 2256896 | tf_op jit(solution)/shard_map/pallas_call | solution.py:39
  15.5 0.0 collective-permute-done.outer_ref
  15.5 0.0 collective-permute-done.1.inner_ref
  15.5 0.2 shard_map.61
  15.7 2.5 %collective-permute-start.2 = (bf16[64,128]{1,0:T(8,128)(2,1)S(1)}, bf16[64,128]{1,0:T(8,128)(2,1)S(1)}, u32[]{:S(2)}, u32[]{:S(2)}) collective-permute-start(bf16[64,128]{1,0:T(8,128)(2,1)S(1)} %get-tuple-element.30), channel_id=1, source_target_pairs={{0,15},{1,2},{2,1},{3,4},{4,3},{5,6},{6,5},{7,8},{8,7},{9,10},{10,... | collective-permute-start | bytes 49160 | tf_op jit(solution)/shard_map/ppermute | solution.py:424
  18.2 1.0 %collective-permute-start.3 = (bf16[64,128]{1,0:T(8,128)(2,1)S(1)}, bf16[64,128]{1,0:T(8,128)(2,1)S(1)}, u32[]{:S(2)}, u32[]{:S(2)}) collective-permute-start(bf16[64,128]{1,0:T(8,128)(2,1)S(1)} %get-tuple-element.31), channel_id=1, source_target_pairs={{0,1},{1,0},{2,3},{3,2},{4,5},{5,4},{6,7},{7,6},{8,9},{9,8},{10,11... | collective-permute-start | bytes 49160 | tf_op jit(solution)/shard_map/ppermute | solution.py:425
  19.2 0.1 copy.14.wb_ref
  19.4 0.1 copy.15.wb3_ref
  19.5 0.1 copy.12
  19.6 0.2 reshape.36.wa_ref
  19.8 2.2 %collective-permute-done.2.far_ref = bf16[64,128]{1,0:T(8,128)(2,1)S(1)} collective-permute-done((bf16[64,128]{1,0:T(8,128)(2,1)S(1)}, bf16[64,128]{1,0:T(8,128)(2,1)S(1)}, u32[]{:S(2)}, u32[]{:S(2)}) %collective-permute-start.2) | collective-permute-done | bytes 16416 | tf_op jit(solution)/shard_map/ppermute | solution.py:424
  22.0 0.7 %collective-permute-done.3.near_ref = bf16[64,128]{1,0:T(8,128)(2,1)S(1)} collective-permute-done((bf16[64,128]{1,0:T(8,128)(2,1)S(1)}, bf16[64,128]{1,0:T(8,128)(2,1)S(1)}, u32[]{:S(2)}, u32[]{:S(2)}) %collective-permute-start.3) | collective-permute-done | bytes 16416 | tf_op jit(solution)/shard_map/ppermute | solution.py:425
  22.6 1.0 %shard_map.62 = (bf16[2,64,128]{2,1,0:T(8,128)(2,1)S(1)}, bf16[64,128]{1,0:T(8,128)(2,1)S(1)}, bf16[4,64,128]{2,1,0:T(8,128)(2,1)S(1)}, bf16[64,384]{1,0:T(8,128)(2,1)S(1)}, f32[32,1,1152]{2,1,0:T(1,128)S(1)}) custom-call(bf16[32,64,128]{2,1,0:T(8,128)(2,1)S(1)} %get-tuple-element.23.fr_ref, bf16[32,64,128]{2,1,0:T(8,128)(2,1)S(1)} %get-tuple-element.24.gr_ref, ...), custom_call_target="tpu_custom_call" | custom-call | flops 75497472 | bytes 1966080 | tf_op jit(solution)/shard_map/pallas_call | solution.py:39
  23.7 13.6 %all_to_all.15.parts_ref = f32[32,1,1152]{2,1,0:T(1,128)S(1)} all-to-all(f32[32,1,1152]{2,1,0:T(1,128)S(1)} %get-tuple-element.35), channel_id=1, replica_groups={{160,161,176,177,192,193,208,209,224,225,240,241,0,1,16,17,32,33,48,49,..., dimensions={0} | all-to-all | bytes 294912 | tf_op jit(solution)/shard_map/all_to_all | solution.py:445
  37.3 0.1 shard_map.64
  37.4 8.5 %all_to_all.16.after_ref.parts_ref = f32[8,1,1152]{2,1,0:T(1,128)S(1)} all-to-all(f32[8,1,1152]{2,1,0:T(1,128)S(1)} %shard_map.64), channel_id=1, replica_groups={{8,10,12,14,0,2,4,6},{9,11,13,15,1,3,5,7},{24,26,28,30,16,18,20,22},{25..., dimensions={0} | all-to-all | bytes 73728 | tf_op jit(solution)/shard_map/all_to_all | solution.py:445
  45.9 0.7 %shard_map.66 = bf16[32,2,640]{2,1,0:T(2,128)(2,1)} custom-call(f32[8,1,1152]{2,1,0:T(1,128)S(1)} %all_to_all.16.after_ref.parts_ref), custom_call_target="tpu_custom_call" | custom-call | bytes 118784 | tf_op jit(solution)/shard_map/pallas_call | solution.py:39
  46.6 6.4 %all-to-all-start.2 = ((bf16[32,2,640]{2,1,0:T(2,128)(2,1)}), bf16[32,2,640]{2,1,0:T(2,128)(2,1)S(1)}, u32[]{:S(2)}, u32[]{:S(2)}) async-start(bf16[32,2,640]{2,1,0:T(2,128)(2,1)} %shard_map.66), calls=%async_computation.2 | async-start | bytes 163840 | tf_op jit(solution)/shard_map/all_to_all | solution.py:445
  53.0 1.9 %shard_map.63 = bf16[2048,128]{1,0:T(8,128)(2,1)} custom-call(bf16[30,64,128]{2,1,0:T(8,128)(2,1)S(1)} %get-tuple-element.25.mid_ref, bf16[2,64,128]{2,1,0:T(8,128)(2,1)S(1)} %get-tuple-element.33.rim_ref, bf16[64,128]{1,0:T(8,128)(2,1)S(1)} %get-tuple-element.34.strip_ref), custom_call_target="tpu_custom_call" | custom-call | bytes 1064960 | tf_op jit(solution)/shard_map/pallas_call | solution.py:39
  54.9 3.2 %shard_map.65 = bf16[2048,128]{1,0:T(8,128)(2,1)} custom-call(f32[8,1,1152]{2,1,0:T(1,128)S(1)} %all_to_all.16.after_ref.parts_ref, bf16[30,64,128]{2,1,0:T(8,128)(2,1)S(1)} %get-tuple-element.36.mid_ref, bf16[4,64,128]{2,1,0:T(8,128)(2,1)S(1)} %get-tuple-element.37.rim_ref, bf16[64,384]{1,0:T(8,128)(2,1)S(1)} %get-tuple-element.38.dstrip_ref, ...), custom_call_target="tpu_custom_call" | custom-call | flops 301989888 | bytes 1839104 | tf_op jit(solution)/shard_map/pallas_call | solution.py:39
  58.1 1.1 %all-to-all-done.2.parts_ref = bf16[32,2,640]{2,1,0:T(2,128)(2,1)S(1)} async-done(((bf16[32,2,640]{2,1,0:T(2,128)(2,1)}), bf16[32,2,640]{2,1,0:T(2,128)(2,1)S(1)}, u32[]{:S(2)}, u32[]{:S(2)}) %all-to-all-start.2) | async-done | bytes 81952 | tf_op jit(solution)/shard_map/all_to_all | solution.py:445
  59.3 0.9 %shard_map.67 = f32[9,64,64]{2,1,0:T(8,128)} custom-call(bf16[32,2,640]{2,1,0:T(2,128)(2,1)S(1)} %all-to-all-done.2.parts_ref), custom_call_target="tpu_custom_call" | custom-call | bytes 229376 | tf_op jit(solution)/shard_map/pallas_call | solution.py:39
  (1 shorter events, 0.0 us)
Async XLA Ops:
  0.6 10.3 %copy-start = (bf16[3,3,64,64]{3,2,1,0:T(8,128)(2,1)S(1)}, bf16[3,3,64,64]{3,2,1,0:T(8,128)(2,1)}, u32[]{:S(2)}) copy-start(bf16[3,3,64,64]{3,2,1,0:T(8,128)(2,1)} %param.4) | copy-start | bytes 221188
  2.1 13.4 %collective-permute-start = (bf16[192,128]{1,0:T(8,128)(2,1)S(1)}, bf16[192,128]{1,0:T(8,128)(2,1)S(1)}, u32[]{:S(2)}, u32[]{:S(2)}) collective-permute-start(bf16[192,128]{1,0:T(8,128)(2,1)S(1)} %get-tuple-element.27), channel_id=1, source_target_pairs={{0,8},{1,9},{2,10},{3,11},{4,12},{5,13},{6,14},{7,15},{8,0},{9,1},... | collective-permute-start | bytes 147464 | tf_op jit(solution)/shard_map/ppermute | solution.py:393
  4.8 10.7 %collective-permute-start.1 = (bf16[192,128]{1,0:T(8,128)(2,1)S(1)}, bf16[192,128]{1,0:T(8,128)(2,1)S(1)}, u32[]{:S(2)}, u32[]{:S(2)}) collective-permute-start(bf16[192,128]{1,0:T(8,128)(2,1)S(1)} %get-tuple-element.28), channel_id=1, source_target_pairs={{0,16},{16,0},{32,48},{48,32},{64,80},{80,64},{96,112},{112,96},{1... | collective-permute-start | bytes 147464 | tf_op jit(solution)/shard_map/ppermute | solution.py:394
  15.7 6.3 %collective-permute-start.2 = (bf16[64,128]{1,0:T(8,128)(2,1)S(1)}, bf16[64,128]{1,0:T(8,128)(2,1)S(1)}, u32[]{:S(2)}, u32[]{:S(2)}) collective-permute-start(bf16[64,128]{1,0:T(8,128)(2,1)S(1)} %get-tuple-element.30), channel_id=1, source_target_pairs={{0,15},{1,2},{2,1},{3,4},{4,3},{5,6},{6,5},{7,8},{8,7},{9,10},{10,... | collective-permute-start | bytes 49160 | tf_op jit(solution)/shard_map/ppermute | solution.py:424
  18.2 4.4 %collective-permute-start.3 = (bf16[64,128]{1,0:T(8,128)(2,1)S(1)}, bf16[64,128]{1,0:T(8,128)(2,1)S(1)}, u32[]{:S(2)}, u32[]{:S(2)}) collective-permute-start(bf16[64,128]{1,0:T(8,128)(2,1)S(1)} %get-tuple-element.31), channel_id=1, source_target_pairs={{0,1},{1,0},{2,3},{3,2},{4,5},{5,4},{6,7},{7,6},{8,9},{9,8},{10,11... | collective-permute-start | bytes 49160 | tf_op jit(solution)/shard_map/ppermute | solution.py:425
  46.6 12.7 %all-to-all-start.2 = ((bf16[32,2,640]{2,1,0:T(2,128)(2,1)}), bf16[32,2,640]{2,1,0:T(2,128)(2,1)S(1)}, u32[]{:S(2)}, u32[]{:S(2)}) async-start(bf16[32,2,640]{2,1,0:T(2,128)(2,1)} %shard_map.66), calls=%async_computation.2 | async-start | bytes 163840 | tf_op jit(solution)/shard_map/all_to_all | solution.py:445
